TPU v7x, 1024 devices: a whole 4x8x16 slice. The times are simulated.
1024 devices in a mesh: dp: 8 (over x, z_hi), ctx: 16 (over y, core), tp: 8 (over z_lo).
Axes of the slice: x: 4, y: 8, z: 16 (z_hi: 2, z_lo: 8; z = z_hi * 8 + z_lo), core: 2. Of those that a mesh axis runs over, the one named last changes fastest.
Arguments:
- tokens: bfloat16 [16384, 2048], P(('dp', 'ctx'), 'tp'), may hold values from -6 to 6
- grad_out: bfloat16 [16384, 2048], P(('dp', 'ctx'), 'tp'), may hold values from -1.5 to 1.5
- expert_ids: int32 [16384, 8], P(('dp', 'ctx')), may hold values from 0 to 127, all different within a row; in each aligned block of 128 rows (0 to 127, 128 to 255, ...) at most 10 rows name the same one
- gate_weights: float32 [16384, 8], P(('dp', 'ctx')), may hold values from 0.03 to 0.5
- gate_proj: bfloat16 [128, 2048, 768], P(('ctx', 'tp')), may hold values from -0.125 to 0.125
- up_proj: bfloat16 [128, 2048, 768], P(('ctx', 'tp')), may hold values from -0.125 to 0.125
- down_proj: bfloat16 [128, 768, 2048], P(('ctx', 'tp')), may hold values from -0.21875 to 0.21875
Outputs:
- combined: bfloat16 [16384, 2048], P(('dp', 'ctx'), 'tp')
- grad_tokens: bfloat16 [16384, 2048], P(('dp', 'ctx'), 'tp')
- grad_gate: float32 [16384, 8], P(('dp', 'ctx'))
- grad_down: bfloat16 [128, 768, 2048], P(('ctx', 'tp'), 'dp')
Inputs may be any that keep to these rules, and one draw needn't show every extreme that they name: `expert_ids`: each row names 8 different experts. Among the 128 rows of one token group no expert is named more than 10 times, and in every draw some group names some expert exactly 10 times.
All inputs are finite; a program needn't handle non-finite values.
Results may differ from a plain program's by a relative error of at most 0.017.
Values may be sent and summed in bfloat16 or wider, within the bound.
No kernel may reach another device: no remote copies, remote signals or barrier semaphores. Data moves between devices by JAX's collectives and lax.ppermute only.
A program may use at most 64 MiB of HBM per device.

v0:
```python
import jax
import jax.numpy as jnp
from jax import lax
from jax.sharding import PartitionSpec as P


def expert_work(expert_rows, scaled_dy, gate_weight, up_weight, down_weight):
    against = (((1,), (1,)), ((), ()))
    gate_act = jnp.dot(expert_rows, gate_weight, preferred_element_type=jnp.float32)
    up_act = jnp.dot(expert_rows, up_weight, preferred_element_type=jnp.float32)
    sigmoid_gate = jax.nn.sigmoid(gate_act)
    hidden = (gate_act * sigmoid_gate * up_act).astype(jnp.bfloat16)
    expert_out = jnp.dot(hidden, down_weight, preferred_element_type=jnp.float32).astype(
        jnp.bfloat16
    )
    d_hidden = lax.dot_general(scaled_dy, down_weight, against, preferred_element_type=jnp.float32)
    d_gate = (d_hidden * up_act * sigmoid_gate * (1.0 + gate_act * (1.0 - sigmoid_gate))).astype(
        jnp.bfloat16
    )
    d_up = (d_hidden * gate_act * sigmoid_gate).astype(jnp.bfloat16)
    dx_rows = (
        lax.dot_general(d_gate, gate_weight, against, preferred_element_type=jnp.float32)
        + lax.dot_general(d_up, up_weight, against, preferred_element_type=jnp.float32)
    ).astype(jnp.bfloat16)
    return (hidden, expert_out, dx_rows)


def slot_numbers(expert_ids, experts):
    tok_rows = expert_ids.shape[0]
    onehot = (expert_ids[:, :, None] == jnp.arange(experts, dtype=jnp.int32)[None, None, :]).astype(
        jnp.float32
    )
    row_counts = jnp.sum(onehot, axis=1)
    row_range = jnp.arange(tok_rows, dtype=jnp.int32)
    before = (row_range[:, None] > row_range[None, :]).astype(jnp.bfloat16)
    earlier = jnp.dot(before, row_counts.astype(jnp.bfloat16), preferred_element_type=jnp.float32)
    counted = jnp.sum(onehot * earlier[:, None, :], axis=2)
    return counted.astype(jnp.int32)


def slot_rows(target, slot_total, tok_rows, top_count, gate_weights, tokens, grad_out):
    token_index = jnp.arange(tok_rows * top_count, dtype=jnp.int32) // top_count
    holder = (
        jnp.full((slot_total,), tok_rows, dtype=jnp.int32).at[target].set(token_index, mode="drop")
    )
    slot_gain = (
        jnp.zeros((slot_total,), dtype=jnp.float32)
        .at[target]
        .set(gate_weights.reshape(-1), mode="drop")
    )
    padded_x = jnp.concatenate(
        [tokens, jnp.zeros((1, tokens.shape[1]), dtype=tokens.dtype)], axis=0
    )
    padded_dy = jnp.concatenate(
        [grad_out, jnp.zeros((1, grad_out.shape[1]), dtype=grad_out.dtype)], axis=0
    )
    sent_x = jnp.take(padded_x, holder, axis=0)
    dy_rows = jnp.take(padded_dy, holder, axis=0).astype(jnp.float32)
    sent_dy = (slot_gain[:, None] * dy_rows).astype(jnp.bfloat16)
    return (sent_x, sent_dy)


def pick_sums(out_flat, dx_flat, where_rows, keep_rows, gate_weights, dy_rows):
    tok_rows, top_count = where_rows.shape
    width = out_flat.shape[1]
    dy_float = dy_rows.astype(jnp.float32)
    out_total = jnp.zeros((tok_rows, width), jnp.float32)
    dx_total = jnp.zeros((tok_rows, width), jnp.float32)
    gate_terms = []
    for pick in range(top_count):
        picked_out = (
            jnp.take(out_flat, where_rows[:, pick], axis=0).astype(jnp.float32)
            * keep_rows[:, pick : pick + 1]
        )
        picked_dx = (
            jnp.take(dx_flat, where_rows[:, pick], axis=0).astype(jnp.float32)
            * keep_rows[:, pick : pick + 1]
        )
        out_total = out_total + gate_weights[:, pick : pick + 1] * picked_out
        dx_total = dx_total + picked_dx
        gate_terms.append(jnp.sum(dy_float * picked_out, axis=1))
    return (out_total, dx_total, jnp.stack(gate_terms, axis=1))


def shards(tokens, grad_out, expert_ids, gate_weights, gate_proj, up_proj, down_proj):
    ctx_count = lax.axis_size("ctx")
    lane_count = lax.axis_size("tp")
    dp_count = lax.axis_size("dp")
    tok_rows, top_count = expert_ids.shape
    experts = ctx_count * lane_count
    capacity = tok_rows * top_count * 5 // (4 * experts)
    local_width = tokens.shape[1]
    model_width = local_width * lane_count
    hidden_width = gate_proj.shape[2]
    slots = slot_numbers(expert_ids, experts)
    gate_weight = gate_proj[0]
    up_weight = up_proj[0]
    down_weight = down_proj[0]
    target = (expert_ids * capacity + slots).reshape(-1)
    sent_x, sent_dy = slot_rows(
        target, experts * capacity, tok_rows, top_count, gate_weights, tokens, grad_out
    )
    outgoing = jnp.stack([sent_x, sent_dy], axis=0).reshape(
        2, ctx_count, lane_count, capacity, local_width
    )
    arrived = lax.all_to_all(
        lax.all_to_all(outgoing, "ctx", split_axis=1, concat_axis=3, tiled=True),
        "tp",
        split_axis=2,
        concat_axis=4,
        tiled=True,
    )
    arrived = arrived.reshape(2, ctx_count * capacity, model_width)
    expert_rows = arrived[0]
    scaled_dy = arrived[1]
    hidden, expert_out, dx_rows = expert_work(
        expert_rows, scaled_dy, gate_weight, up_weight, down_weight
    )
    results = jnp.stack([expert_out, dx_rows], axis=0).reshape(
        2, ctx_count, 1, capacity, model_width
    )
    returned = lax.all_to_all(
        lax.all_to_all(results, "ctx", split_axis=1, concat_axis=1, tiled=True),
        "tp",
        split_axis=4,
        concat_axis=2,
        tiled=True,
    )
    returned = returned.reshape(2, experts * capacity, local_width)
    keep_rows = jnp.ones((tok_rows, top_count), jnp.float32)
    where_rows = expert_ids * capacity + slots
    out_total, dx_total, gate_terms = pick_sums(
        returned[0], returned[1], where_rows, keep_rows, gate_weights, grad_out
    )
    combined = out_total.astype(jnp.bfloat16)
    grad_tokens = dx_total.astype(jnp.bfloat16)
    grad_gate = lax.psum(gate_terms, "tp")
    grad_rows = lax.psum_scatter(
        lax.dot_general(
            hidden, scaled_dy, (((0,), (0,)), ((), ())), preferred_element_type=jnp.float32
        ).astype(jnp.bfloat16),
        "dp",
        scatter_dimension=0,
        tiled=True,
    )
    grad_down = grad_rows.reshape(1, hidden_width // dp_count, model_width)
    return (combined, grad_tokens, grad_gate, grad_down)


def solution(mesh):
    in_specs = (
        P(("dp", "ctx"), "tp"),
        P(("dp", "ctx"), "tp"),
        P(("dp", "ctx"), None),
        P(("dp", "ctx"), None),
        P(("ctx", "tp"), None, None),
        P(("ctx", "tp"), None, None),
        P(("ctx", "tp"), None, None),
    )
    out_specs = (
        P(("dp", "ctx"), "tp"),
        P(("dp", "ctx"), "tp"),
        P(("dp", "ctx"), None),
        P(("ctx", "tp"), "dp", None),
    )
    return jax.shard_map(shards, mesh=mesh, in_specs=in_specs, out_specs=out_specs, check_vma=False)
```

profile of v0, /device:TPU:1, one launch (start us, length us, event | category | flops | bytes accessed | tf_op | source)
XLA Modules:
  0.0 446.8 jit_solution(2566169460613374370)
XLA Ops:
  7.2 0.9 copy.74
  9.9 4.3 scatter_custom_fusion
  15.1 0.8 concatenate.8
  16.8 4.3 scatter_custom_fusion.1
  21.1 4.7 %gather_fusion.1 = bf16[1280,256]{1,0:T(8,128)(2,1)} fusion(bf16[129,256]{1,0:T(8,128)(2,1)S(1)} %concatenate.9, s32[2048]{0:T(1024)S(1)} %pad_clamp_fusion), kind=kCustom, calls=%fused_computation.2.clone | custom fusion | bytes 1315840 | tf_op jit(solution)/shard_map/jit(_take)/gather | solution.py:58
  25.8 2.3 multiply_convert_fusion
  28.1 2.1 stack.46
  30.3 4.6 %gather_fusion = bf16[1280,256]{1,0:T(8,128)(2,1)} fusion(bf16[129,256]{1,0:T(8,128)(2,1)S(1)} %concatenate.8, s32[2048]{0:T(1024)S(1)} %pad_clamp_fusion), kind=kCustom, calls=%fused_computation.clone | custom fusion | bytes 1315840 | tf_op jit(solution)/shard_map/jit(_take)/gather | solution.py:57
  34.9 2.2 broadcast_select_fusion
  37.1 2.2 stack.45
  39.2 1.8 pad_maximum_fusion
  41.6 51.0 %all_to_all.53 = bf16[2,16,8,10,256]{4,2,3,0,1:T(8,128)(2,1)S(1)} all-to-all(bf16[2,16,8,10,256]{4,2,3,0,1:T(8,128)(2,1)S(1)} %copy.78), channel_id=1, replica_groups=mesh['dp'=8,'ctx'=16,'tp'=8] {'ctx'}, dimensions={1} | all-to-all | bytes 2621440 | tf_op jit(solution)/shard_map/all_to_all | solution.py:107
  93.0 69.5 %all_to_all.54 = bf16[2,1,8,160,256]{4,3,0,1,2:T(8,128)(2,1)S(1)} all-to-all(bf16[2,1,8,160,256]{4,3,0,1,2:T(8,128)(2,1)S(1)} %copy.80), channel_id=1, replica_groups=mesh['dp'=8,'ctx'=16,'tp'=8] {'tp'}, dimensions={2} | all-to-all | bytes 2621440 | tf_op jit(solution)/shard_map/all_to_all | solution.py:106
  162.8 1.9 copy-done.4
  165.4 1.5 multiply_convert_fusion.3
  167.6 2.0 fusion
  169.6 1.6 fusion.15
  171.2 2.2 stack.48
  173.4 2.5 fusion.4
  175.9 1.2 fusion.18
  177.1 1.2 stack.49
  178.5 1.5 pad_maximum_fusion.1
  180.0 2.4 copy.83
  182.4 4.3 all-to-all-start.2
  186.8 2.8 convolution_convert_fusion
  189.6 30.4 %all-to-all-done.2 = bf16[2,16,1,10,2048]{4,0,3,2,1:T(2,128)(2,1)S(1)} async-done(((bf16[2,16,1,10,2048]{4,0,3,2,1:T(2,128)(2,1)}), bf16[2,16,1,10,2048]{4,0,3,2,1:T(2,128)(2,1)S(1)}, u32[]{:S(2)}, u32[]{:S(2)}) %all-to-all-start.2) | async-done | bytes 1310752 | tf_op jit(solution)/shard_map/all_to_all | solution.py:123
  220.0 16.2 %copy.84 = bf16[2,16,1,10,2048]{1,0,3,2,4:T(2,128)(2,1)} copy(bf16[2,16,1,10,2048]{4,0,3,2,1:T(2,128)(2,1)S(1)} %all-to-all-done.2) | data formatting | bytes 2621440 | tf_op jit(solution)/shard_map/all_to_all | solution.py:123
  236.2 12.8 %reshape.301 = bf16[8,2,40960]{2,1,0:T(2,128)(2,1)} reshape(bf16[2048,1,10,2,16]{4,3,2,1,0:T(2,128)(2,1)} %bitcast.106) | data formatting | bytes 2621440
  249.0 4.3 all-to-all-start.3
  255.2 94.8 %all-to-all-done.3 = bf16[8,2,40960]{2,1,0:T(2,128)(2,1)S(1)} async-done(((bf16[8,2,40960]{2,1,0:T(2,128)(2,1)}), bf16[8,2,40960]{2,1,0:T(2,128)(2,1)S(1)}, u32[]{:S(2)}, u32[]{:S(2)}) %all-to-all-start.3) | async-done | bytes 1310752 | tf_op jit(solution)/shard_map/all_to_all | solution.py:122
  350.0 8.9 %reshape.302 = bf16[2048,1,10,2,16]{4,3,2,1,0:T(2,128)(2,1)} reshape(bf16[8,2,40960]{2,1,0:T(2,128)(2,1)S(1)} %all-to-all-done.3) | data formatting | bytes 2621440
  358.9 14.7 %copy.88 = bf16[2,16,1,10,8,256]{5,4,1,3,0,2:T(8,128)(2,1)S(1)} copy(bf16[2,16,1,10,8,256]{1,0,3,5,4,2:T(2,128)(2,1)} %bitcast.107) | data formatting | bytes 2621440 | tf_op jit(solution)/shard_map/all_to_all | solution.py:122
  374.4 1.5 gather_fusion.17
  375.9 1.5 gather_fusion.16
  378.0 0.8 gather_fusion.9
  378.9 0.8 gather_fusion.8
  379.7 1.5 gather_fusion.15
  382.0 1.5 gather_fusion.14
  384.3 1.5 gather_fusion.13
  386.7 1.5 gather_fusion.12
  389.0 2.8 gather_fusion.11
  391.8 2.7 gather_fusion.3
  394.5 2.7 gather_fusion.10
  397.1 2.7 gather_fusion.2
  399.8 1.9 fusion.38
  402.5 33.7 %psum.7 = f32[128,8]{0,1:T(8,128)} all-reduce(f32[128,8]{0,1:T(8,128)S(1)} %stack.59), channel_id=1, replica_groups=mesh['dp'=8,'ctx'=16,'tp'=8] {'tp'}, use_global_device_ids=true, to_apply=%region_12.15 | all-reduce | flops 1024 | bytes 8192 | tf_op jit(solution)/shard_map/psum | solution.py:137
  436.1 1.9 add_convert_fusion
  438.0 1.9 fusion.30
  (72 shorter events, 13.7 us)
Async XLA Ops:
  7.2 158.2 %copy-start = (bf16[1,2048,768]{2,1,0:T(8,128)(2,1)S(1)}, bf16[1,2048,768]{2,1,0:T(8,128)(2,1)}, u32[]{:S(2)}) copy-start(bf16[1,2048,768]{2,1,0:T(8,128)(2,1)} %param.16) | copy-start | bytes 9437188
  162.5 2.1 copy-start.4
  162.8 4.1 copy-start.7
  165.4 1.5 copy-start.9
  165.4 2.2 copy-start.6
  173.4 2.5 copy-start.5
  173.4 2.5 copy-start.10
  173.4 2.5 copy-start.11
  173.4 2.6 copy-start.13
  177.1 1.4 copy-start.12
  182.4 4.4 copy-start.8
  182.4 37.6 %all-to-all-start.2 = ((bf16[2,16,1,10,2048]{4,0,3,2,1:T(2,128)(2,1)}), bf16[2,16,1,10,2048]{4,0,3,2,1:T(2,128)(2,1)S(1)}, u32[]{:S(2)}, u32[]{:S(2)}) async-start(bf16[2,16,1,10,2048]{4,0,3,2,1:T(2,128)(2,1)} %copy.83), calls=%async_computation.2 | async-start | bytes 2621440 | tf_op jit(solution)/shard_map/all_to_all | solution.py:123
  186.8 253.2 %reduce-scatter.2.cloned.1.call-start = ((), (), s32[]{:S(2)}) async-start(), calls=%async_computation.5 | async-start | bytes 3538944 | tf_op jit(solution)/shard_map/reduce_scatter | solution.py:138
  249.0 5.5 %copy-start.14 = (f32[128,8]{0,1:T(8,128)S(1)}, f32[128,8]{0,1:T(8,128)}, u32[]{:S(2)}) copy-start(f32[128,8]{0,1:T(8,128)} %param.14) | copy-start | bytes 12292
  249.0 101.0 %all-to-all-start.3 = ((bf16[8,2,40960]{2,1,0:T(2,128)(2,1)}), bf16[8,2,40960]{2,1,0:T(2,128)(2,1)S(1)}, u32[]{:S(2)}, u32[]{:S(2)}) async-start(bf16[8,2,40960]{2,1,0:T(2,128)(2,1)} %reshape.301), calls=%async_computation.3 | async-start | bytes 2621440 | tf_op jit(solution)/shard_map/all_to_all | solution.py:122
  253.9 145.9 %copy-start.15 = (pred[128]{0:T(512)(128)(4,1)}, pred[128]{0:T(512)(128)(4,1)S(1)}, u32[]{:S(2)}) copy-start(pred[128]{0:T(512)(128)(4,1)S(1)} %get-tuple-element.38) | copy-start | bytes 388
  374.4 12.2 %copy-start.2 = (bf16[1280,256]{1,0:T(8,128)(2,1)}, bf16[1280,256]{1,0:T(8,128)(2,1)S(1)}, u32[]{:S(2)}) copy-start(bf16[1280,256]{1,0:T(8,128)(2,1)S(1)} %squeeze.67) | copy-start | bytes 1966084
  378.0 10.1 %copy-start.3 = (bf16[1280,256]{1,0:T(8,128)(2,1)}, bf16[1280,256]{1,0:T(8,128)(2,1)S(1)}, u32[]{:S(2)}) copy-start(bf16[1280,256]{1,0:T(8,128)(2,1)S(1)} %squeeze.58) | copy-start | bytes 1966084
  389.0 50.9 %copy-start.1 = (bf16[1,2048,768]{2,1,0:T(8,128)(2,1)S(1)}, bf16[1,2048,768]{2,1,0:T(8,128)(2,1)}, u32[]{:S(2)}) copy-start(bf16[1,2048,768]{2,1,0:T(8,128)(2,1)} %param.16) | copy-start | bytes 9437188
Sparse Core Ops, SparseCore 0:
  194.1 214.3 reduce-scatter.1
where the time goes:
time: 451 us; the launch traced here: 447 us
  blocking collectives  154 us (34%)
  waiting for transfers between devices  125 us (28%)
  local copies, waits for them, and re-layouts  116 us (26%)
  other arithmetic  16.1 us (4%)
  between operations  14.4 us (3%)
  matrix products  12.3 us (3%)
  starting transfers between devices  8.65 us (2%)
    all_to_all x1, waiting for transfers between devices, shards(): lax.all_to_all(lax.all_to_all(results, 'ctx', split_axis=1, concat_axis=1...  94.8 us
    all_to_all x1, blocking collectives, shards(): lax.all_to_all(lax.all_to_all(outgoing, 'ctx', split_axis=1, concat_axis=...  69.5 us
    all_to_all x1, blocking collectives, shards(): lax.all_to_all(outgoing, 'ctx', split_axis=1, concat_axis=3, tiled=True)  51 us
    psum x1, blocking collectives, shards(): grad_gate = lax.psum(gate_terms, 'tp')  33.7 us
    all_to_all x1, waiting for transfers between devices, shards(): lax.all_to_all(results, 'ctx', split_axis=1, concat_axis=1, tiled=True)  30.4 us
    unnamed x38, local copies, waits for them, and re-layouts  26.5 us
    all_to_all x1, local copies, waits for them, and re-layouts, shards(): lax.all_to_all(results, 'ctx', split_axis=1, concat_axis=1, tiled=True)  16.2 us
    all_to_all x1, local copies, waits for them, and re-layouts, shards(): lax.all_to_all(lax.all_to_all(results, 'ctx', split_axis=1, concat_axis=1...  14.7 us
  transfers between devices with their start and end apart: 3, of which 2 were waited for; matrix products, arithmetic and copies ran while one was open for 20% of the time, Pallas kernels for 0%

commit v1 on v0

v1 whole, which is shorter than its diff:
```python
import functools

import jax
import jax.numpy as jnp
from jax import lax
from jax.experimental import pallas as pl
from jax.experimental.pallas import tpu as pltpu
from jax.sharding import PartitionSpec as P

BF = jnp.bfloat16
F32 = jnp.float32
MAIN = 8
REST = 2
QUAD = 4
VMEM = 60 * 1024 * 1024


def iota(shape, dim):
    return lax.broadcasted_iota(jnp.int32, shape, dim)


def dot(a, b):
    return jnp.dot(a, b, preferred_element_type=F32)


def dot_nt(a, b):
    return lax.dot_general(a, b, (((1,), (1,)), ((), ())), preferred_element_type=F32)


def routing(ids_t, gates_t, lane):
    top, tokens = ids_t.shape
    rows = (MAIN + REST) * 16
    row = iota((rows, tokens), 0)
    left = row - MAIN * 16
    expert = jnp.where(left < 0, row >> 3, left >> 1) * 8 + lane
    slot = jnp.where(left < 0, row & 7, MAIN + (left & 1)).astype(F32)
    named = jnp.zeros((rows, tokens), F32)
    weight = jnp.zeros((rows, tokens), F32)
    for k in range(top):
        hit = ids_t[k : k + 1, :] == expert
        named = named + jnp.where(hit, 1.0, 0.0)
        weight = weight + jnp.where(hit, gates_t[k : k + 1, :], 0.0)
    before = jnp.where(iota((tokens, tokens), 0) < iota((tokens, tokens), 1), 1.0, 0.0)
    earlier = dot(named.astype(BF), before.astype(BF))
    holds = (named > 0.5) & (earlier == slot)
    return holds, weight, expert


def rest_mix():
    p, q = iota((256, 256), 0), iota((256, 256), 1)
    return jnp.where(q == ((p >> 1) & 7) * 32 + (p >> 4) * 2 + (p & 1), 1.0, 0.0).astype(BF)


def rest_unmix():
    q, p = iota((256, 256), 0), iota((256, 256), 1)
    return jnp.where(p == ((q >> 1) & 15) * 16 + (q >> 5) * 2 + (q & 1), 1.0, 0.0).astype(BF)


def fold(send_ref, shard, first, second):
    split = MAIN * 16
    tiles = [v[:split].reshape(16, MAIN, 256) for v in (first, second)]
    send_ref[:, shard * 16 : (shard + 1) * 16, :] = jnp.concatenate(tiles, axis=1).astype(BF)
    return [first[split:].astype(BF), second[split:].astype(BF)]


def fold_rest(send_ref, rest):
    mixed = dot(rest_mix(), jnp.concatenate(rest, axis=0))
    send_ref[:, QUAD * 16 : QUAD * 20, :] = mixed.reshape(16, 16, 256).astype(BF)


def unfold(recv_ref):
    tail = recv_ref[:, QUAD * 16 : QUAD * 20, :].astype(F32).reshape(256, 256).astype(BF)
    rest = dot(rest_unmix(), tail)
    out = []
    for shard in range(QUAD):
        both = recv_ref[:, shard * 16 : (shard + 1) * 16, :].astype(F32)
        pair = []
        for a in range(2):
            tiles = both[:, a * MAIN : (a + 1) * MAIN, :].reshape(MAIN * 16, 256)
            at = (shard * 2 + a) * 32
            pair.append(jnp.concatenate([tiles, rest[at : at + 32]], axis=0).astype(BF))
        out.append(pair)
    return out


def dispatch_kernel(where_ref, ids_ref, gates_ref, p0, p1, p2, p3, send_ref):
    holds, weight, _ = routing(ids_ref[...], gates_ref[...], where_ref[0])
    pick = jnp.where(holds, 1.0, 0.0).astype(BF)
    gain = jnp.sum(jnp.where(holds, weight, 0.0), axis=1, keepdims=True)
    rest = []
    for shard, ref in enumerate((p0, p1, p2, p3)):
        x_rows = dot(pick, ref[:128, :])
        dy_rows = dot(pick, ref[128:, :]) * gain
        rest += fold(send_ref, shard, x_rows, dy_rows)
    fold_rest(send_ref, rest)


def shard_at(where_ref, far, shard):
    return pl.multiple_of(((where_ref[0] ^ (far * QUAD)) ^ shard) * 256, 256)


def fetch(where_ref, far, weights, held, sems, first=0):
    copies = []
    for shard in range(QUAD):
        at = pl.ds(shard_at(where_ref, far, shard), 256)
        parts = [w.at[at, :] for w in weights[:2]] + [w.at[:, at] for w in weights[2:]]
        trio = [
            pltpu.make_async_copy(src, dst.at[shard], sems.at[shard, first + n])
            for n, (src, dst) in enumerate(zip(parts, held))
        ]
        for copy in trio:
            copy.start()
        copies.append(trio)
    return copies


def inward(recv_ref, copies, held, dy_list, sums):
    gate, up, d_hidden = sums
    wg, wu, wd = held[:3]
    for shard, (x_rows, dy_rows) in enumerate(unfold(recv_ref)):
        dy_list.append(dy_rows)
        for copy in copies[shard]:
            copy.wait()
        gate = gate + dot(x_rows, wg[shard])
        up = up + dot(x_rows, wu[shard])
        d_hidden = d_hidden + dot_nt(dy_rows, wd[shard])
    return gate, up, d_hidden


def outward(outs, d_gate, d_up, copies, held, send_ref):
    wg, wu = held[:2]
    rest = []
    for shard in range(QUAD):
        if copies is not None:
            for copy in copies[shard]:
                copy.wait()
        dx = dot_nt(d_gate, wg[shard]) + dot_nt(d_up, wu[shard])
        rest += fold(send_ref, shard, outs[shard], dx)
    fold_rest(send_ref, rest)


def tail_pick(turn):
    p, q = (0, 1) if turn else (1, 0)
    shape = (128, 32) if turn else (32, 128)
    row, rest = iota(shape, p), iota(shape, q)
    return jnp.where(((row >> 3) == (rest >> 1)) & ((row & 7) == (rest & 1)), 1.0, 0.0).astype(BF)


def near_kernel(where_ref, recv_ref, *refs):
    weights, held, sems = refs[:3], refs[7:10], refs[10]
    gate_ref, up_ref, dh_ref, dy_ref = refs[3:7]
    copies = fetch(where_ref, 0, weights, held, sems)
    zero = jnp.zeros(gate_ref.shape, F32)
    dy_rows = []
    gate_ref[...], up_ref[...], dh_ref[...] = inward(
        recv_ref, copies, held, dy_rows, (zero, zero, zero)
    )
    for shard, rows in enumerate(dy_rows):
        dy_ref[shard] = rows


def far_kernel(where_ref, recv_ref, gate_ref, up_ref, dh_ref, near_ref, *refs):
    weights, outs, held, sems, block = refs[:3], refs[3:12], refs[12:16], refs[16], refs[17]
    home_ref, dgate_ref, dup_ref, send_ref, partial_ref = outs[:5]
    copies = fetch(where_ref, 1, weights, held[:3], sems)
    wd_near = []
    for shard in range(QUAD):
        at = pl.ds(shard_at(where_ref, 0, shard), 256)
        copy = pltpu.make_async_copy(weights[2].at[:, at], held[3].at[shard], sems.at[shard, 3])
        copy.start()
        wd_near.append(copy)
    dy_rows = []
    gate, up, d_hidden = inward(
        recv_ref, copies, held, dy_rows, (gate_ref[...], up_ref[...], dh_ref[...])
    )
    s = jax.nn.sigmoid(gate)
    hidden32 = gate * s * up
    hidden = hidden32.astype(BF)
    d_gate = (d_hidden * up * s * (1.0 + gate * (1.0 - s))).astype(BF)
    d_up = (d_hidden * gate * s).astype(BF)
    dgate_ref[...] = d_gate
    dup_ref[...] = d_up
    far_outs = [dot(hidden, held[2][shard]) for shard in range(QUAD)]
    outward(far_outs, d_gate, d_up, None, held, send_ref)
    dots = jnp.zeros((gate.shape[0], 1), F32)
    for shard in range(QUAD):
        wd_near[shard].wait()
        out = dot(hidden, held[3][shard]).astype(BF)
        home_ref[shard] = out
        for rows, dy in ((out, near_ref[shard]), (far_outs[shard].astype(BF), dy_rows[shard])):
            dots = dots + jnp.sum(rows.astype(F32) * dy.astype(F32), axis=1, keepdims=True)
    high = dots.astype(BF).astype(F32)
    terms = jnp.where(iota((dots.shape[0], 256), 1) < 128, high, dots - high)
    tail = dot(tail_pick(True), terms[MAIN * 16 :].astype(BF))
    terms = [v.reshape(16, 8, 256) for v in (terms[: MAIN * 16], tail)]
    send_ref[:, QUAD * 20 :, :] = jnp.concatenate(terms, axis=1).astype(BF)
    turned = hidden32.T.astype(BF)
    for shard in range(QUAD):
        at = slice(shard * 256, (shard + 1) * 256)
        partial_ref[:, at] = dot(turned, dy_rows[shard]).astype(BF)
        block[:, at] = dot(turned, near_ref[shard]).astype(BF)
    for n, ref in enumerate(outs[5:]):
        ref[...] = block[pl.ds(pl.multiple_of((where_ref[2] ^ n) * 192, 192), 192), :]


def back_kernel(where_ref, home_ref, dgate_ref, dup_ref, *refs):
    weights, send_ref, held, sems = refs[:2], refs[2], refs[3:5], refs[5]
    copies = fetch(where_ref, 0, weights, held, sems)
    outs = [home_ref[shard].astype(F32) for shard in range(QUAD)]
    outward(outs, dgate_ref[...], dup_ref[...], copies, held, send_ref)


def split_lines(lines):
    high = lines.astype(BF).astype(F32)
    middle = (lines - high).astype(BF).astype(F32)
    low = lines - high - middle
    pairs = [jnp.concatenate(v, axis=1) for v in ((high, middle), (low, jnp.zeros_like(low)))]
    return jnp.concatenate(pairs, axis=0).astype(BF)


def join_lines(ref):
    terms = ref[256:, :].astype(F32)
    return terms[:8, :128] + terms[:8, 128:] + terms[8:, :128]


def first_kernel(where_ref, ids_ref, gates_ref, recv_ref, next_ref, *outs):
    outs[-1][...] = next_ref[...]
    combine_kernel(True, where_ref, ids_ref, gates_ref, recv_ref, *outs[:-1])


def combine_kernel(first, where_ref, ids_ref, gates_ref, recv_ref, *outs):
    holds, weight, expert = routing(ids_ref[...], gates_ref[...], where_ref[0])
    gains = jnp.where(holds, weight, 0.0)
    picks = jnp.where(holds, 1.0, 0.0).T.astype(BF)
    turned = gains.T
    high = turned.astype(BF)
    low = (turned - high.astype(F32)).astype(BF)
    for (out, dx), to in zip(unfold(recv_ref), outs):
        to[:128, :] = (dot(high, out) + dot(low, out)).astype(BF)
        to[128:256, :] = dot(picks, dx).astype(BF)
    if not first:
        return
    terms = recv_ref[:, QUAD * 20 :, :].astype(F32)
    main, tail = [terms[:, n * 8 : (n + 1) * 8, :].reshape(128, 256) for n in range(2)]
    terms = jnp.concatenate([main, dot(tail_pick(False), tail.astype(BF))], axis=0)
    dots = terms[:, :1] + terms[:, 128:129]
    gain = jnp.sum(gains, axis=1, keepdims=True)
    slopes = jnp.where(gain > 0.0, dots / jnp.where(gain > 0.0, gain, 1.0), 0.0)
    sums = jnp.where(holds, slopes, 0.0)
    ids = ids_ref[...]
    lines = [
        jnp.sum(jnp.where(ids[k : k + 1, :] == expert, sums, 0.0), axis=0, keepdims=True)
        for k in range(ids.shape[0])
    ]
    lines = split_lines(jnp.concatenate(lines, axis=0))
    for to in outs:
        to[256:, :] = lines


def end_kernel(where_ref, sum_ref, *refs):
    for flip, to in enumerate(refs[-2:]):
        rows = pl.ds(pl.multiple_of((where_ref[1] ^ flip) * 96, 96), 96)
        total = refs[0][rows, :].astype(F32)
        for ref in refs[1:-2]:
            total = total + ref[rows, :].astype(F32)
        to[:, : QUAD * 256] = total.astype(BF)
        to[:, QUAD * 256 :] = sum_ref[rows, :]


def total_of(refs):
    total = refs[0][:256, :].astype(F32)
    for ref in refs[1:]:
        total = total + ref[:256, :].astype(F32)
    return total.astype(BF)


def total_kernel(where_ref, *refs):
    refs[-1][:256, :] = total_of(refs[:-1])
    lines = join_lines(refs[0])
    for ref in refs[1:-1]:
        lines = lines + join_lines(ref)
    refs[-1][256:, :] = split_lines(lines)


def last_kernel(where_ref, mine_ref, other_ref, *refs):
    total = total_of((other_ref, *refs[:-3]))
    refs[-3][...] = total[:128]
    refs[-2][...] = total[128:]
    refs[-1][...] = join_lines(mine_ref) + join_lines(other_ref)


def add_kernel(where_ref, held_ref, got_ref, out_ref):
    for n in range(2 * QUAD):
        at = slice(n * 256, (n + 1) * 256)
        total = held_ref[:, at].astype(F32) + got_ref[:, at].astype(F32)
        out_ref[:, pl.ds(shard_at(where_ref, n // QUAD, n % QUAD), 256)] = total.astype(BF)


def whole(shape):
    return pl.BlockSpec(shape, lambda i: (0,) * len(shape))


def call(kernel, outs, micros, scalars, *operands, weights=(), downs=0, more=(), after=()):
    specs = [pl.BlockSpec(memory_space=pltpu.SMEM)] + [whole(v.shape) for v in operands]
    specs += [pl.BlockSpec(memory_space=pl.ANY) for _ in (*weights, *after)]
    first = 1 + len(operands) + len(weights)
    last = first + len(after)

    def body(*refs):
        kernel(*refs[:first], *refs[last:])

    scratch = []
    if weights:
        wide = weights[0].shape[1]
        scratch = [pltpu.VMEM((QUAD, 256, wide), BF) for _ in weights[:2]]
        scratch += [pltpu.VMEM((QUAD, wide, 256), BF) for _ in range(downs)]
        scratch += [pltpu.SemaphoreType.DMA((QUAD, len(scratch)))]
    shapes = [jax.ShapeDtypeStruct(s, d) for s, d in outs]
    results = pl.pallas_call(
        body,
        grid=(1,),
        out_shape=shapes,
        in_specs=specs,
        out_specs=[whole(v.shape) for v in shapes],
        scratch_shapes=[*scratch, *more],
        compiler_params=pltpu.CompilerParams(vmem_limit_bytes=VMEM),
        cost_estimate=pl.CostEstimate(
            flops=micros * 10**9, bytes_accessed=micros * 3 * 10**6, transcendentals=0
        ),
    )(scalars, *operands, *weights, *after)
    return results[0] if len(results) == 1 else results


def swap(value, axis, bit):
    size = lax.axis_size(axis)
    return lax.ppermute(value, axis, [(i, i ^ bit) for i in range(size)])


def over_ctx(value):
    return lax.all_to_all(value, "ctx", split_axis=0, concat_axis=0, tiled=True)


def shards(tokens, grad_out, expert_ids, gate_weights, gate_proj, up_proj, down_proj):
    dp, lane = lax.axis_index("dp"), lax.axis_index("tp")
    scalars = jnp.stack([lane, dp & 1, dp >> 1]).astype(jnp.int32)
    wg, wu, wd = gate_proj[0], up_proj[0], down_proj[0]
    width, hidden_width = wg.shape
    ids_t, gates_t = expert_ids.T, gate_weights.T
    table = (scalars, ids_t, gates_t)
    slots = (MAIN + REST) * 16
    travel = (16, QUAD * 20, 256)

    own = jnp.concatenate([tokens, grad_out], axis=0)
    across = swap(own, "tp", 4)
    near = [own] + [swap(own, "tp", d) for d in (1, 2, 3)]
    far = [across] + [swap(across, "tp", d) for d in (1, 2, 3)]

    send_near = call(dispatch_kernel, [(travel, BF)], 4, *table, *near, after=(across,))
    got_near = over_ctx(send_near)
    send_far = call(dispatch_kernel, [(travel, BF)], 4, *table, *far, after=(send_near,))
    got_far = over_ctx(send_far)

    sums = ((slots, hidden_width), F32)
    dy_shape = ((QUAD, slots, 256), BF)
    act = ((slots, hidden_width), BF)
    gate, up, d_hidden, dy_near = call(
        near_kernel, [sums, sums, sums, dy_shape], 5, scalars, got_near,
        weights=(wg, wu, wd), downs=1, after=(send_far,),
    )
    longer = (16, QUAD * 20 + 16, 256)
    home, d_gate, d_up, back_far, partial, *blocks = call(
        far_kernel,
        [dy_shape, act, act, (longer, BF), ((hidden_width, width // 2), BF)]
        + [((hidden_width // 4, width // 2), BF)] * 4,
        8, scalars, got_far, gate, up, d_hidden, dy_near, weights=(wg, wu, wd), downs=2,
        more=(pltpu.VMEM((hidden_width, width // 2), BF),),
    )
    home_far = over_ctx(back_far)

    quarter = lax.psum_scatter(
        partial, "dp", scatter_dimension=0, axis_index_groups=[[0, 2, 4, 6], [1, 3, 5, 7]], tiled=True
    )
    came = [swap(blocks[d], "dp", d << 1) for d in (1, 2, 3)]
    back_near = call(
        back_kernel, [(travel, BF)], 4, scalars, home, d_gate, d_up, weights=(wg, wu),
    )
    part, longer = ((256, 256), BF), ((272, 256), BF)
    *sums_far, leaving = call(
        first_kernel, [longer] * 4 + [(travel, BF)], 4, *table, home_far, back_near, after=came
    )
    home_near = over_ctx(leaving)
    came_far = [swap(sums_far[d], "tp", d) for d in (1, 2, 3)]
    end = ((96, width), BF)
    held, over = call(end_kernel, [end, end], 1, scalars, quarter, blocks[0], *came, after=(sums_far[0],))
    ends = swap(over, "dp", 1)
    total_far = call(total_kernel, [longer], 1, scalars, sums_far[0], *came_far, after=(over,))
    from_far = swap(total_far, "tp", 4)
    sums_near = call(
        functools.partial(combine_kernel, False), [part] * 4, 4, *table, home_near,
        after=(total_far,),
    )
    came_near = [swap(sums_near[d], "tp", d) for d in (1, 2, 3)]
    flat = ((128, 256), BF)
    combined, grad_tokens, lines = call(
        last_kernel, [flat, flat, (ids_t.shape, F32)], 1,
        scalars, total_far, from_far, sums_near[0], *came_near,
    )
    grad_down = call(add_kernel, [end], 2, scalars, held, ends)
    return combined, grad_tokens, lines.T, grad_down[None]


def solution(mesh):
    in_specs = (
        P(("dp", "ctx"), "tp"),
        P(("dp", "ctx"), "tp"),
        P(("dp", "ctx"), None),
        P(("dp", "ctx"), None),
        P(("ctx", "tp"), None, None),
        P(("ctx", "tp"), None, None),
        P(("ctx", "tp"), None, None),
    )
    out_specs = (
        P(("dp", "ctx"), "tp"),
        P(("dp", "ctx"), "tp"),
        P(("dp", "ctx"), None),
        P(("ctx", "tp"), "dp", None),
    )
    return jax.shard_map(shards, mesh=mesh, in_specs=in_specs, out_specs=out_specs, check_vma=False)
```

time: 451 us -> 259 us (0.57)
  blocking collectives: 154 us -> 0 us
  starting transfers between devices: 8.65 us -> 118 us
  local copies, waits for them, and re-layouts: 116 us -> 9.75 us
  waiting for transfers between devices: 125 us -> 75 us
  Pallas kernels: 0 us -> 40.1 us
  other arithmetic: 16.1 us -> 0.65 us
  matrix products: 12.3 us -> 0 us
    all_to_all x2 -> x0, blocking collectives: 121 us -> none  [the longest x1 69.5 us: shards(): lax.all_to_all(lax.all_to_all(outgoing, 'ctx', split_axis=1, concat_axis=...]
    all_to_all x2 -> x4, waiting for transfers between devices: 125 us -> 14.8 us  [over_ctx(): return lax.all_to_all(value, 'ctx', split_axis=0, concat_axis=0, tiled=True)]
    ppermute x0 -> x18, starting transfers between devices: none -> 80.2 us  [swap(): return lax.ppermute(value, axis, [(i, i ^ bit) for i in range(size)])]
    ppermute x0 -> x18, waiting for transfers between devices: none -> 60.2 us  [swap(): return lax.ppermute(value, axis, [(i, i ^ bit) for i in range(size)])]
    pallas_call x0 -> x11, Pallas kernels: none -> 40.1 us  [call(): pl.pallas_call(body, grid=(1,), out_shape=shapes, in_specs=specs, out_spe...]
    gather x18 -> x0, local copies, waits for them, and re-layouts: 34 us -> none  [the longest x8 14.3 us: pick_sums(): jnp.take(dx_flat, where_rows[:, pick], axis=0).astype(jnp.float32)]
    psum x1 -> x0, blocking collectives: 33.7 us -> none  [shards(): grad_gate = lax.psum(gate_terms, 'tp')]
    all_to_all x4 -> x0, local copies, waits for them, and re-layouts: 31.3 us -> none  [the longest x1 16.2 us: shards(): lax.all_to_all(results, 'ctx', split_axis=1, concat_axis=1, tiled=True)]
  transfers between devices with their start and end apart: 3 -> 23, of which waited for: 2 -> 8; matrix products, arithmetic and copies ran while one was open for 20% -> 0% of each run, Pallas kernels for 0% -> 10%
where the time goes in v1:
time: 259 us; the launch traced here: 258 us
  starting transfers between devices  118 us (46%)
  waiting for transfers between devices  75 us (29%)
  Pallas kernels  40.1 us (15%)
  between operations  14.5 us (6%)
  local copies, waits for them, and re-layouts  9.75 us (4%)
    ppermute x18, starting transfers between devices, swap(): return lax.ppermute(value, axis, [(i, i ^ bit) for i in range(size)])  80.2 us
    ppermute x18, waiting for transfers between devices, swap(): return lax.ppermute(value, axis, [(i, i ^ bit) for i in range(size)])  60.2 us
    pallas_call x11, Pallas kernels, call(): pl.pallas_call(body, grid=(1,), out_shape=shapes, in_specs=specs, out_spe...  40.1 us
    all_to_all x4, starting transfers between devices, over_ctx(): return lax.all_to_all(value, 'ctx', split_axis=0, concat_axis=0, tiled=True)  37.3 us
    all_to_all x4, waiting for transfers between devices, over_ctx(): return lax.all_to_all(value, 'ctx', split_axis=0, concat_axis=0, tiled=True)  14.8 us
    unnamed x53, local copies, waits for them, and re-layouts  8.9 us
  transfers between devices with their start and end apart: 23, of which 8 were waited for; matrix products, arithmetic and copies ran while one was open for 0% of the time, Pallas kernels for 10%

profile of v1, /device:TPU:1, one launch (start us, length us, event | category | flops | bytes accessed | tf_op | source)
XLA Modules:
  0.0 257.5 jit_solution(6257688283819947811)
XLA Ops:
  7.2 0.8 constant_dynamic-update-slice_fusion.1
  8.0 0.8 constant_dynamic-update-slice_fusion.refs_3_
  8.9 8.4 %collective-permute-start.6 = (bf16[256,256]{1,0:T(8,128)(2,1)S(1)}, bf16[256,256]{1,0:T(8,128)(2,1)S(1)}, u32[]{:S(2)}, u32[]{:S(2)}) collective-permute-start(bf16[256,256]{1,0:T(8,128)(2,1)S(1)} %constant_dynamic-update-slice_fusion.refs_3_), channel_id=1, source_target_pairs={{0,3},{1,2},{2,1},{3,0},{4,7},{5,6},{6,5},{7,4},{8,11},{9,10},{10,... | collective-permute-start | bytes 393224 | tf_op jit(solution)/shard_map/ppermute | solution.py:336
  17.3 1.9 collective-permute-start.5
  19.2 2.2 collective-permute-start.4
  21.4 10.6 %collective-permute-start = (bf16[256,256]{1,0:T(8,128)(2,1)S(1)}, bf16[256,256]{1,0:T(8,128)(2,1)S(1)}, u32[]{:S(2)}, u32[]{:S(2)}) collective-permute-start(bf16[256,256]{1,0:T(8,128)(2,1)S(1)} %constant_dynamic-update-slice_fusion.refs_3_), channel_id=1, source_target_pairs={{0,4},{1,5},{2,6},{3,7},{4,0},{5,1},{6,2},{7,3},{8,12},{9,13},{10,... | collective-permute-start | bytes 393224 | tf_op jit(solution)/shard_map/ppermute | solution.py:336
  32.8 1.7 collective-permute-done.refs_7_.refs_3_
  35.2 2.6 %shard_map.102.refs_7_ = bf16[16,80,256]{2,1,0:T(8,128)(2,1)} custom-call(s32[3]{0:T(128)} %pad_add_fusion.refs_0_, s32[8,128]{1,0:T(8,128)} %bitcast.18, f32[8,128]{1,0:T(8,128)} %bitcast.22, bf16[256,256]{1,0:T(8,128)(2,1)} %copy-done.4, bf16[256,256]{1,0:T(8,128)(2,1)} %copy-done.19, bf16[256,256]{1,0:T(8,128)(2,1)} %copy-done.18, ...), custom_call_target="tpu_custom_call" | custom-call | flops 4000000000 | bytes 12000000 | tf_op jit(solution)/shard_map/pallas_call | solution.py:319
  37.8 17.0 %all-to-all-start.1 = ((bf16[16,80,256]{2,1,0:T(8,128)(2,1)}), bf16[16,80,256]{2,1,0:T(8,128)(2,1)S(1)}, u32[]{:S(2)}, u32[]{:S(2)}) async-start(bf16[16,80,256]{2,1,0:T(8,128)(2,1)} %shard_map.102.refs_7_), calls=%async_computation.1 | async-start | bytes 1310720 | tf_op jit(solution)/shard_map/all_to_all | solution.py:340
  54.8 4.7 %collective-permute-start.3 = (bf16[256,256]{1,0:T(8,128)(2,1)}, bf16[256,256]{1,0:T(8,128)(2,1)S(1)}, u32[]{:S(2)}, u32[]{:S(2)}) collective-permute-start(bf16[256,256]{1,0:T(8,128)(2,1)} %copy-done.16), channel_id=1, source_target_pairs={{0,3},{1,2},{2,1},{3,0},{4,7},{5,6},{6,5},{7,4},{8,11},{9,10},{10,... | collective-permute-start | bytes 393224 | tf_op jit(solution)/shard_map/ppermute | solution.py:336
  59.5 2.9 %collective-permute-start.2 = (bf16[256,256]{1,0:T(8,128)(2,1)}, bf16[256,256]{1,0:T(8,128)(2,1)S(1)}, u32[]{:S(2)}, u32[]{:S(2)}) collective-permute-start(bf16[256,256]{1,0:T(8,128)(2,1)} %copy-done.16), channel_id=1, source_target_pairs={{0,2},{1,3},{2,0},{3,1},{4,6},{5,7},{6,4},{7,5},{8,10},{9,11},{10,... | collective-permute-start | bytes 393224 | tf_op jit(solution)/shard_map/ppermute | solution.py:336
  62.4 1.9 collective-permute-start.1
  64.4 8.2 %collective-permute-done.2.refs_5_ = bf16[256,256]{1,0:T(8,128)(2,1)S(1)} collective-permute-done((bf16[256,256]{1,0:T(8,128)(2,1)}, bf16[256,256]{1,0:T(8,128)(2,1)S(1)}, u32[]{:S(2)}, u32[]{:S(2)}) %collective-permute-start.2) | collective-permute-done | bytes 131104 | tf_op jit(solution)/shard_map/ppermute | solution.py:336
  73.9 2.6 %shard_map.103.refs_5_ = bf16[16,80,256]{2,1,0:T(8,128)(2,1)} custom-call(s32[3]{0:T(128)} %pad_add_fusion.refs_0_, s32[8,128]{1,0:T(8,128)} %bitcast.19, f32[8,128]{1,0:T(8,128)} %bitcast.23, bf16[256,256]{1,0:T(8,128)(2,1)} %copy-done.16, bf16[256,256]{1,0:T(8,128)(2,1)} %copy-done.25, bf16[256,256]{1,0:T(8,128)(2,1)} %copy-done.24, ...), custom_call_target="tpu_custom_call" | custom-call | flops 4000000000 | bytes 12000000 | tf_op jit(solution)/shard_map/pallas_call | solution.py:319
  76.6 7.4 %all-to-all-start = ((bf16[16,80,256]{2,1,0:T(8,128)(2,1)}), bf16[16,80,256]{2,1,0:T(8,128)(2,1)S(1)}, u32[]{:S(2)}, u32[]{:S(2)}) async-start(bf16[16,80,256]{2,1,0:T(8,128)(2,1)} %shard_map.103.refs_5_), calls=%async_computation | async-start | bytes 1310720 | tf_op jit(solution)/shard_map/all_to_all | solution.py:340
  84.0 5.2 %shard_map.104 = (f32[160,768]{1,0:T(8,128)}, f32[160,768]{1,0:T(8,128)}, f32[160,768]{1,0:T(8,128)}, bf16[4,160,256]{2,1,0:T(8,128)(2,1)}) custom-call(s32[3]{0:T(128)} %pad_add_fusion.refs_0_, bf16[16,80,256]{2,1,0:T(8,128)(2,1)} %copy-done.2, bf16[2048,768]{1,0:T(8,128)(2,1)} %bitcast.12, bf16[2048,768]{1,0:T(8,128)(2,1)} %bitcast.15, ...), custom_call_target="tpu_custom_call" | custom-call | flops 5000000000 | bytes 15000000 | tf_op jit(solution)/shard_map/pallas_call | solution.py:319
  89.2 14.8 %all-to-all-done.refs_1_ = bf16[16,80,256]{2,1,0:T(8,128)(2,1)S(1)} async-done(((bf16[16,80,256]{2,1,0:T(8,128)(2,1)}), bf16[16,80,256]{2,1,0:T(8,128)(2,1)S(1)}, u32[]{:S(2)}, u32[]{:S(2)}) %all-to-all-start) | async-done | bytes 655392 | tf_op jit(solution)/shard_map/all_to_all | solution.py:340
  104.0 0.8 copy-done.3
  104.8 10.2 %shard_map.105 = (bf16[4,160,256]{2,1,0:T(8,128)(2,1)}, bf16[160,768]{1,0:T(8,128)(2,1)}, bf16[160,768]{1,0:T(8,128)(2,1)}, bf16[16,96,256]{2,1,0:T(8,128)(2,1)}...) custom-call(s32[3]{0:T(128)} %pad_add_fusion.refs_0_, ...), custom_call_target="tpu_custom_call" | custom-call | flops 8000000000 | bytes 24000000 | tf_op jit(solution)/shard_map/pallas_call | solution.py:319
  115.1 3.7 %all-to-all-start.2 = ((bf16[16,96,256]{2,1,0:T(8,128)(2,1)}), bf16[16,96,256]{2,1,0:T(8,128)(2,1)S(1)}, u32[]{:S(2)}, u32[]{:S(2)}) async-start(bf16[16,96,256]{2,1,0:T(8,128)(2,1)} %get-tuple-element.35), calls=%async_computation.2 | async-start | bytes 1572864 | tf_op jit(solution)/shard_map/all_to_all | solution.py:340
  118.7 2.6 %collective-permute-start.7 = (bf16[192,1024]{1,0:T(8,128)(2,1)S(1)}, bf16[192,1024]{1,0:T(8,128)(2,1)S(1)}, u32[]{:S(2)}, u32[]{:S(2)}) collective-permute-start(bf16[192,1024]{1,0:T(8,128)(2,1)S(1)} %copy-done.11), channel_id=1, source_target_pairs={{0,256},{128,384},{256,0},{384,128},{512,768},{640,896},{768,512},... | collective-permute-start | bytes 1179656 | tf_op jit(solution)/shard_map/ppermute | solution.py:336
  121.4 4.4 %collective-permute-start.8 = (bf16[192,1024]{1,0:T(8,128)(2,1)S(1)}, bf16[192,1024]{1,0:T(8,128)(2,1)S(1)}, u32[]{:S(2)}, u32[]{:S(2)}) collective-permute-start(bf16[192,1024]{1,0:T(8,128)(2,1)S(1)} %copy-done.10), channel_id=1, source_target_pairs={{0,512},{128,640},{256,768},{384,896},{512,0},{640,128},{768,256},... | collective-permute-start | bytes 1179656 | tf_op jit(solution)/shard_map/ppermute | solution.py:336
  125.8 2.6 %collective-permute-start.9 = (bf16[192,1024]{1,0:T(8,128)(2,1)S(1)}, bf16[192,1024]{1,0:T(8,128)(2,1)S(1)}, u32[]{:S(2)}, u32[]{:S(2)}) collective-permute-start(bf16[192,1024]{1,0:T(8,128)(2,1)S(1)} %copy-done.9), channel_id=1, source_target_pairs={{0,768},{128,896},{256,512},{384,640},{512,256},{640,384},{768,0},... | collective-permute-start | bytes 1179656 | tf_op jit(solution)/shard_map/ppermute | solution.py:336
  128.4 5.7 %shard_map.106.refs_4_ = bf16[16,80,256]{2,1,0:T(8,128)(2,1)} custom-call(s32[3]{0:T(128)} %pad_add_fusion.refs_0_, bf16[4,160,256]{2,1,0:T(8,128)(2,1)} %get-tuple-element.36.refs_1_, bf16[160,768]{1,0:T(8,128)(2,1)} %get-tuple-element.37.refs_2_, bf16[160,768]{1,0:T(8,128)(2,1)} %get-tuple-element.38.refs_3_, bf16[2048,768]{1,0:T(8,128)(2,1)} %bitcast.14, ...), custom_call_target="tpu_custom_call" | custom-call | flops 4000000000 | bytes 12000000 | tf_op jit(solution)/shard_map/pallas_call | solution.py:319
  134.1 13.8 %collective-permute-done.8.refs_6_.refs_4_ = bf16[192,1024]{1,0:T(8,128)(2,1)S(1)} collective-permute-done((bf16[192,1024]{1,0:T(8,128)(2,1)S(1)}, bf16[192,1024]{1,0:T(8,128)(2,1)S(1)}, u32[]{:S(2)}, u32[]{:S(2)}) %collective-permute-start.8) | collective-permute-done | bytes 393248 | tf_op jit(solution)/shard_map/ppermute | solution.py:336
  147.8 5.8 %collective-permute-done.9.refs_7_.refs_5_ = bf16[192,1024]{1,0:T(8,128)(2,1)S(1)} collective-permute-done((bf16[192,1024]{1,0:T(8,128)(2,1)S(1)}, bf16[192,1024]{1,0:T(8,128)(2,1)S(1)}, u32[]{:S(2)}, u32[]{:S(2)}) %collective-permute-start.9) | collective-permute-done | bytes 393248 | tf_op jit(solution)/shard_map/ppermute | solution.py:336
  153.7 0.7 copy-done.8
  154.4 0.9 copy-done
  155.3 3.1 %shard_map.107 = (bf16[272,256]{1,0:T(8,128)(2,1)}, bf16[272,256]{1,0:T(8,128)(2,1)}, bf16[272,256]{1,0:T(8,128)(2,1)}, bf16[272,256]{1,0:T(8,128)(2,1)}, bf16[16,80,256]{2,1,0:T(8,128)(2,1)}) custom-call(s32[3]{0:T(128)} %pad_add_fusion.refs_0_, s32[8,128]{1,0:T(8,128)} %bitcast.20, f32[8,128]{1,0:T(8,128)} %bitcast.24, bf16[16,96,256]{2,1,0:T(8,128)(2,1)} %copy-done, ...), custom_call_target="tpu_custom_call" | custom-call | flops 4000000000 | bytes 12000000 | tf_op jit(solution)/shard_map/pallas_call | solution.py:319
  158.5 9.3 %all-to-all-start.3 = ((bf16[16,80,256]{2,1,0:T(8,128)(2,1)}), bf16[16,80,256]{2,1,0:T(8,128)(2,1)S(1)}, u32[]{:S(2)}, u32[]{:S(2)}) async-start(bf16[16,80,256]{2,1,0:T(8,128)(2,1)} %get-tuple-element.49), calls=%async_computation.4 | async-start | bytes 1310720 | tf_op jit(solution)/shard_map/all_to_all | solution.py:340
  167.8 1.9 collective-permute-start.10
  169.7 3.8 %collective-permute-start.11 = (bf16[272,256]{1,0:T(8,128)(2,1)}, bf16[272,256]{1,0:T(8,128)(2,1)S(1)}, u32[]{:S(2)}, u32[]{:S(2)}) collective-permute-start(bf16[272,256]{1,0:T(8,128)(2,1)} %get-tuple-element.44), channel_id=1, source_target_pairs={{0,2},{1,3},{2,0},{3,1},{4,6},{5,7},{6,4},{7,5},{8,10},{9,11},{10,... | collective-permute-start | bytes 417800 | tf_op jit(solution)/shard_map/ppermute | solution.py:336
  173.5 3.6 %collective-permute-start.12 = (bf16[272,256]{1,0:T(8,128)(2,1)}, bf16[272,256]{1,0:T(8,128)(2,1)S(1)}, u32[]{:S(2)}, u32[]{:S(2)}) collective-permute-start(bf16[272,256]{1,0:T(8,128)(2,1)} %get-tuple-element.45), channel_id=1, source_target_pairs={{0,3},{1,2},{2,1},{3,0},{4,7},{5,6},{6,5},{7,4},{8,11},{9,10},{10,... | collective-permute-start | bytes 417800 | tf_op jit(solution)/shard_map/ppermute | solution.py:336
  177.1 2.5 shard_map.108
  179.6 12.3 %collective-permute-start.17 = (bf16[96,2048]{1,0:T(8,128)(2,1)}, bf16[96,2048]{1,0:T(8,128)(2,1)S(1)}, u32[]{:S(2)}, u32[]{:S(2)}) collective-permute-start(bf16[96,2048]{1,0:T(8,128)(2,1)} %get-tuple-element.48.refs_5_), channel_id=1, source_target_pairs={{0,128},{128,0},{256,384},{384,256},{512,640},{640,512},{768,896},... | collective-permute-start | bytes 1179656 | tf_op jit(solution)/shard_map/ppermute | solution.py:336
  193.3 1.8 shard_map.109.refs_4_.refs_1_
  195.2 7.0 %collective-permute-start.13 = (bf16[272,256]{1,0:T(8,128)(2,1)}, bf16[272,256]{1,0:T(8,128)(2,1)S(1)}, u32[]{:S(2)}, u32[]{:S(2)}) collective-permute-start(bf16[272,256]{1,0:T(8,128)(2,1)} %shard_map.109.refs_4_.refs_1_), channel_id=1, source_target_pairs={{0,4},{1,5},{2,6},{3,7},{4,0},{5,1},{6,2},{7,3},{8,12},{9,13},{10,... | collective-permute-start | bytes 417800 | tf_op jit(solution)/shard_map/ppermute | solution.py:336
  202.1 0.8 copy-done.1
  203.0 2.4 shard_map.110
  205.4 1.9 collective-permute-start.14
  207.3 4.7 %collective-permute-start.15 = (bf16[256,256]{1,0:T(8,128)(2,1)}, bf16[256,256]{1,0:T(8,128)(2,1)S(1)}, u32[]{:S(2)}, u32[]{:S(2)}) collective-permute-start(bf16[256,256]{1,0:T(8,128)(2,1)} %get-tuple-element.52), channel_id=1, source_target_pairs={{0,2},{1,3},{2,0},{3,1},{4,6},{5,7},{6,4},{7,5},{8,10},{9,11},{10,... | collective-permute-start | bytes 393224 | tf_op jit(solution)/shard_map/ppermute | solution.py:336
  212.1 2.6 %collective-permute-start.16 = (bf16[256,256]{1,0:T(8,128)(2,1)}, bf16[256,256]{1,0:T(8,128)(2,1)S(1)}, u32[]{:S(2)}, u32[]{:S(2)}) collective-permute-start(bf16[256,256]{1,0:T(8,128)(2,1)} %get-tuple-element.53), channel_id=1, source_target_pairs={{0,3},{1,2},{2,1},{3,0},{4,7},{5,6},{6,5},{7,4},{8,11},{9,10},{10,... | collective-permute-start | bytes 393224 | tf_op jit(solution)/shard_map/ppermute | solution.py:336
  214.7 15.5 %collective-permute-done.14.refs_4_ = bf16[256,256]{1,0:T(8,128)(2,1)S(1)} collective-permute-done((bf16[256,256]{1,0:T(8,128)(2,1)}, bf16[256,256]{1,0:T(8,128)(2,1)S(1)}, u32[]{:S(2)}, u32[]{:S(2)}) %collective-permute-start.14) | collective-permute-done | bytes 131104 | tf_op jit(solution)/shard_map/ppermute | solution.py:336
  230.2 2.8 %collective-permute-done.15.refs_5_ = bf16[256,256]{1,0:T(8,128)(2,1)S(1)} collective-permute-done((bf16[256,256]{1,0:T(8,128)(2,1)}, bf16[256,256]{1,0:T(8,128)(2,1)S(1)}, u32[]{:S(2)}, u32[]{:S(2)}) %collective-permute-start.15) | collective-permute-done | bytes 131104 | tf_op jit(solution)/shard_map/ppermute | solution.py:336
  233.0 12.3 %collective-permute-done.16.refs_6_ = bf16[256,256]{1,0:T(8,128)(2,1)S(1)} collective-permute-done((bf16[256,256]{1,0:T(8,128)(2,1)}, bf16[256,256]{1,0:T(8,128)(2,1)S(1)}, u32[]{:S(2)}, u32[]{:S(2)}) %collective-permute-start.16) | collective-permute-done | bytes 131104 | tf_op jit(solution)/shard_map/ppermute | solution.py:336
  246.0 1.9 shard_map.111
  248.0 0.8 copy-done.5
  248.7 2.0 shard_map.112
  (65 shorter events, 4.8 us)
Async XLA Ops:
  8.9 25.7 %copy-start.4 = (bf16[256,256]{1,0:T(8,128)(2,1)}, bf16[256,256]{1,0:T(8,128)(2,1)S(1)}, u32[]{:S(2)}) copy-start(bf16[256,256]{1,0:T(8,128)(2,1)S(1)} %constant_dynamic-update-slice_fusion.refs_3_) | copy-start | bytes 393220
  8.9 23.9 %collective-permute-start.6 = (bf16[256,256]{1,0:T(8,128)(2,1)S(1)}, bf16[256,256]{1,0:T(8,128)(2,1)S(1)}, u32[]{:S(2)}, u32[]{:S(2)}) collective-permute-start(bf16[256,256]{1,0:T(8,128)(2,1)S(1)} %constant_dynamic-update-slice_fusion.refs_3_), channel_id=1, source_target_pairs={{0,3},{1,2},{2,1},{3,0},{4,7},{5,6},{6,5},{7,4},{8,11},{9,10},{10,... | collective-permute-start | bytes 393224 | tf_op jit(solution)/shard_map/ppermute | solution.py:336
  17.3 15.4 %collective-permute-start.5 = (bf16[256,256]{1,0:T(8,128)(2,1)S(1)}, bf16[256,256]{1,0:T(8,128)(2,1)S(1)}, u32[]{:S(2)}, u32[]{:S(2)}) collective-permute-start(bf16[256,256]{1,0:T(8,128)(2,1)S(1)} %constant_dynamic-update-slice_fusion.refs_3_), channel_id=1, source_target_pairs={{0,2},{1,3},{2,0},{3,1},{4,6},{5,7},{6,4},{7,5},{8,10},{9,11},{10,... | collective-permute-start | bytes 393224 | tf_op jit(solution)/shard_map/ppermute | solution.py:336
  19.2 13.5 %collective-permute-start.4 = (bf16[256,256]{1,0:T(8,128)(2,1)S(1)}, bf16[256,256]{1,0:T(8,128)(2,1)S(1)}, u32[]{:S(2)}, u32[]{:S(2)}) collective-permute-start(bf16[256,256]{1,0:T(8,128)(2,1)S(1)} %constant_dynamic-update-slice_fusion.refs_3_), channel_id=1, source_target_pairs={{0,1},{1,0},{2,3},{3,2},{4,5},{5,4},{6,7},{7,6},{8,9},{9,8},{10,11... | collective-permute-start | bytes 393224 | tf_op jit(solution)/shard_map/ppermute | solution.py:336
  21.4 13.1 %collective-permute-start = (bf16[256,256]{1,0:T(8,128)(2,1)S(1)}, bf16[256,256]{1,0:T(8,128)(2,1)S(1)}, u32[]{:S(2)}, u32[]{:S(2)}) collective-permute-start(bf16[256,256]{1,0:T(8,128)(2,1)S(1)} %constant_dynamic-update-slice_fusion.refs_3_), channel_id=1, source_target_pairs={{0,4},{1,5},{2,6},{3,7},{4,0},{5,1},{6,2},{7,3},{8,12},{9,13},{10,... | collective-permute-start | bytes 393224 | tf_op jit(solution)/shard_map/ppermute | solution.py:336
  32.7 1.8 copy-start.17
  32.7 1.8 copy-start.18
  32.8 1.8 copy-start.19
  34.5 0.7 copy-start.16
  37.8 38.7 %all-to-all-start.1 = ((bf16[16,80,256]{2,1,0:T(8,128)(2,1)}), bf16[16,80,256]{2,1,0:T(8,128)(2,1)S(1)}, u32[]{:S(2)}, u32[]{:S(2)}) async-start(bf16[16,80,256]{2,1,0:T(8,128)(2,1)} %shard_map.102.refs_7_), calls=%async_computation.1 | async-start | bytes 1310720 | tf_op jit(solution)/shard_map/all_to_all | solution.py:340
  54.8 9.6 %collective-permute-start.3 = (bf16[256,256]{1,0:T(8,128)(2,1)}, bf16[256,256]{1,0:T(8,128)(2,1)S(1)}, u32[]{:S(2)}, u32[]{:S(2)}) collective-permute-start(bf16[256,256]{1,0:T(8,128)(2,1)} %copy-done.16), channel_id=1, source_target_pairs={{0,3},{1,2},{2,1},{3,0},{4,7},{5,6},{6,5},{7,4},{8,11},{9,10},{10,... | collective-permute-start | bytes 393224 | tf_op jit(solution)/shard_map/ppermute | solution.py:336
  59.5 13.1 %collective-permute-start.2 = (bf16[256,256]{1,0:T(8,128)(2,1)}, bf16[256,256]{1,0:T(8,128)(2,1)S(1)}, u32[]{:S(2)}, u32[]{:S(2)}) collective-permute-start(bf16[256,256]{1,0:T(8,128)(2,1)} %copy-done.16), channel_id=1, source_target_pairs={{0,2},{1,3},{2,0},{3,1},{4,6},{5,7},{6,4},{7,5},{8,10},{9,11},{10,... | collective-permute-start | bytes 393224 | tf_op jit(solution)/shard_map/ppermute | solution.py:336
  62.4 10.2 %collective-permute-start.1 = (bf16[256,256]{1,0:T(8,128)(2,1)}, bf16[256,256]{1,0:T(8,128)(2,1)S(1)}, u32[]{:S(2)}, u32[]{:S(2)}) collective-permute-start(bf16[256,256]{1,0:T(8,128)(2,1)} %copy-done.16), channel_id=1, source_target_pairs={{0,1},{1,0},{2,3},{3,2},{4,5},{5,4},{6,7},{7,6},{8,9},{9,8},{10,11... | collective-permute-start | bytes 393224 | tf_op jit(solution)/shard_map/ppermute | solution.py:336
  64.4 8.2 %copy-start.23 = (bf16[256,256]{1,0:T(8,128)(2,1)}, bf16[256,256]{1,0:T(8,128)(2,1)S(1)}, u32[]{:S(2)}) copy-start(bf16[256,256]{1,0:T(8,128)(2,1)S(1)} %collective-permute-done.3.refs_6_) | copy-start | bytes 393220
  72.6 0.7 copy-start.24
  76.6 7.5 %copy-start.2 = (bf16[16,80,256]{2,1,0:T(8,128)(2,1)}, bf16[16,80,256]{2,1,0:T(8,128)(2,1)S(1)}, u32[]{:S(2)}) copy-start(bf16[16,80,256]{2,1,0:T(8,128)(2,1)S(1)} %all-to-all-done.1.refs_1_) | copy-start | bytes 1966084
  76.6 27.4 %all-to-all-start = ((bf16[16,80,256]{2,1,0:T(8,128)(2,1)}), bf16[16,80,256]{2,1,0:T(8,128)(2,1)S(1)}, u32[]{:S(2)}, u32[]{:S(2)}) async-start(bf16[16,80,256]{2,1,0:T(8,128)(2,1)} %shard_map.103.refs_5_), calls=%async_computation | async-start | bytes 1310720 | tf_op jit(solution)/shard_map/all_to_all | solution.py:340
  84.0 93.1 %reduce-scatter.2.cloned.1.call-start = ((), (), s32[]{:S(2)}) async-start(), calls=%async_computation.5 | async-start | bytes 1966080 | tf_op jit(solution)/shard_map/reduce_scatter | solution.py:380
  104.0 0.8 copy-start.3
  115.0 3.7 %copy-start.11 = (bf16[192,1024]{1,0:T(8,128)(2,1)S(1)}, bf16[192,1024]{1,0:T(8,128)(2,1)}, u32[]{:S(2)}) copy-start(bf16[192,1024]{1,0:T(8,128)(2,1)} %get-tuple-element.39) | copy-start | bytes 1179652
  115.0 6.4 %copy-start.10 = (bf16[192,1024]{1,0:T(8,128)(2,1)S(1)}, bf16[192,1024]{1,0:T(8,128)(2,1)}, u32[]{:S(2)}) copy-start(bf16[192,1024]{1,0:T(8,128)(2,1)} %get-tuple-element.40) | copy-start | bytes 1179652
  115.0 10.7 %copy-start.9 = (bf16[192,1024]{1,0:T(8,128)(2,1)S(1)}, bf16[192,1024]{1,0:T(8,128)(2,1)}, u32[]{:S(2)}) copy-start(bf16[192,1024]{1,0:T(8,128)(2,1)} %get-tuple-element.41) | copy-start | bytes 1179652
  115.1 38.6 %all-to-all-start.2 = ((bf16[16,96,256]{2,1,0:T(8,128)(2,1)}), bf16[16,96,256]{2,1,0:T(8,128)(2,1)S(1)}, u32[]{:S(2)}, u32[]{:S(2)}) async-start(bf16[16,96,256]{2,1,0:T(8,128)(2,1)} %get-tuple-element.35), calls=%async_computation.2 | async-start | bytes 1572864 | tf_op jit(solution)/shard_map/all_to_all | solution.py:340
  118.7 15.3 %collective-permute-start.7 = (bf16[192,1024]{1,0:T(8,128)(2,1)S(1)}, bf16[192,1024]{1,0:T(8,128)(2,1)S(1)}, u32[]{:S(2)}, u32[]{:S(2)}) collective-permute-start(bf16[192,1024]{1,0:T(8,128)(2,1)S(1)} %copy-done.11), channel_id=1, source_target_pairs={{0,256},{128,384},{256,0},{384,128},{512,768},{640,896},{768,512},... | collective-permute-start | bytes 1179656 | tf_op jit(solution)/shard_map/ppermute | solution.py:336
  121.4 26.5 %collective-permute-start.8 = (bf16[192,1024]{1,0:T(8,128)(2,1)S(1)}, bf16[192,1024]{1,0:T(8,128)(2,1)S(1)}, u32[]{:S(2)}, u32[]{:S(2)}) collective-permute-start(bf16[192,1024]{1,0:T(8,128)(2,1)S(1)} %copy-done.10), channel_id=1, source_target_pairs={{0,512},{128,640},{256,768},{384,896},{512,0},{640,128},{768,256},... | collective-permute-start | bytes 1179656 | tf_op jit(solution)/shard_map/ppermute | solution.py:336
  125.8 27.9 %collective-permute-start.9 = (bf16[192,1024]{1,0:T(8,128)(2,1)S(1)}, bf16[192,1024]{1,0:T(8,128)(2,1)S(1)}, u32[]{:S(2)}, u32[]{:S(2)}) collective-permute-start(bf16[192,1024]{1,0:T(8,128)(2,1)S(1)} %copy-done.9), channel_id=1, source_target_pairs={{0,768},{128,896},{256,512},{384,640},{512,256},{640,384},{768,0},... | collective-permute-start | bytes 1179656 | tf_op jit(solution)/shard_map/ppermute | solution.py:336
  134.1 19.6 %copy-start.6 = (bf16[192,1024]{1,0:T(8,128)(2,1)}, bf16[192,1024]{1,0:T(8,128)(2,1)S(1)}, u32[]{:S(2)}) copy-start(bf16[192,1024]{1,0:T(8,128)(2,1)S(1)} %collective-permute-done.7.refs_5_.refs_3_) | copy-start | bytes 1179652
  147.8 5.9 %copy-start.7 = (bf16[192,1024]{1,0:T(8,128)(2,1)}, bf16[192,1024]{1,0:T(8,128)(2,1)S(1)}, u32[]{:S(2)}) copy-start(bf16[192,1024]{1,0:T(8,128)(2,1)S(1)} %collective-permute-done.8.refs_6_.refs_4_) | copy-start | bytes 1179652
  153.7 0.8 copy-start.8
  154.4 0.9 copy-start
  158.5 43.7 %all-to-all-start.3 = ((bf16[16,80,256]{2,1,0:T(8,128)(2,1)}), bf16[16,80,256]{2,1,0:T(8,128)(2,1)S(1)}, u32[]{:S(2)}, u32[]{:S(2)}) async-start(bf16[16,80,256]{2,1,0:T(8,128)(2,1)} %get-tuple-element.49), calls=%async_computation.4 | async-start | bytes 1310720 | tf_op jit(solution)/shard_map/all_to_all | solution.py:340
  167.8 24.2 %collective-permute-start.10 = (bf16[272,256]{1,0:T(8,128)(2,1)}, bf16[272,256]{1,0:T(8,128)(2,1)S(1)}, u32[]{:S(2)}, u32[]{:S(2)}) collective-permute-start(bf16[272,256]{1,0:T(8,128)(2,1)} %get-tuple-element.43), channel_id=1, source_target_pairs={{0,1},{1,0},{2,3},{3,2},{4,5},{5,4},{6,7},{7,6},{8,9},{9,8},{10,11... | collective-permute-start | bytes 417800 | tf_op jit(solution)/shard_map/ppermute | solution.py:336
  169.7 22.3 %collective-permute-start.11 = (bf16[272,256]{1,0:T(8,128)(2,1)}, bf16[272,256]{1,0:T(8,128)(2,1)S(1)}, u32[]{:S(2)}, u32[]{:S(2)}) collective-permute-start(bf16[272,256]{1,0:T(8,128)(2,1)} %get-tuple-element.44), channel_id=1, source_target_pairs={{0,2},{1,3},{2,0},{3,1},{4,6},{5,7},{6,4},{7,5},{8,10},{9,11},{10,... | collective-permute-start | bytes 417800 | tf_op jit(solution)/shard_map/ppermute | solution.py:336
  173.5 18.5 %collective-permute-start.12 = (bf16[272,256]{1,0:T(8,128)(2,1)}, bf16[272,256]{1,0:T(8,128)(2,1)S(1)}, u32[]{:S(2)}, u32[]{:S(2)}) collective-permute-start(bf16[272,256]{1,0:T(8,128)(2,1)} %get-tuple-element.45), channel_id=1, source_target_pairs={{0,3},{1,2},{2,1},{3,0},{4,7},{5,6},{6,5},{7,4},{8,11},{9,10},{10,... | collective-permute-start | bytes 417800 | tf_op jit(solution)/shard_map/ppermute | solution.py:336
  179.6 68.4 %collective-permute-start.17 = (bf16[96,2048]{1,0:T(8,128)(2,1)}, bf16[96,2048]{1,0:T(8,128)(2,1)S(1)}, u32[]{:S(2)}, u32[]{:S(2)}) collective-permute-start(bf16[96,2048]{1,0:T(8,128)(2,1)} %get-tuple-element.48.refs_5_), channel_id=1, source_target_pairs={{0,128},{128,0},{256,384},{384,256},{512,640},{640,512},{768,896},... | collective-permute-start | bytes 1179656 | tf_op jit(solution)/shard_map/ppermute | solution.py:336
  191.9 0.7 copy-start.13
  192.0 0.7 copy-start.14
  192.7 0.7 copy-start.15
  195.2 50.2 %collective-permute-start.13 = (bf16[272,256]{1,0:T(8,128)(2,1)}, bf16[272,256]{1,0:T(8,128)(2,1)S(1)}, u32[]{:S(2)}, u32[]{:S(2)}) collective-permute-start(bf16[272,256]{1,0:T(8,128)(2,1)} %shard_map.109.refs_4_.refs_1_), channel_id=1, source_target_pairs={{0,4},{1,5},{2,6},{3,7},{4,0},{5,1},{6,2},{7,3},{8,12},{9,13},{10,... | collective-permute-start | bytes 417800 | tf_op jit(solution)/shard_map/ppermute | solution.py:336
  202.1 0.9 copy-start.1
  205.4 24.7 %collective-permute-start.14 = (bf16[256,256]{1,0:T(8,128)(2,1)}, bf16[256,256]{1,0:T(8,128)(2,1)S(1)}, u32[]{:S(2)}, u32[]{:S(2)}) collective-permute-start(bf16[256,256]{1,0:T(8,128)(2,1)} %get-tuple-element.51), channel_id=1, source_target_pairs={{0,1},{1,0},{2,3},{3,2},{4,5},{5,4},{6,7},{7,6},{8,9},{9,8},{10,11... | collective-permute-start | bytes 393224 | tf_op jit(solution)/shard_map/ppermute | solution.py:336
  207.3 25.6 %collective-permute-start.15 = (bf16[256,256]{1,0:T(8,128)(2,1)}, bf16[256,256]{1,0:T(8,128)(2,1)S(1)}, u32[]{:S(2)}, u32[]{:S(2)}) collective-permute-start(bf16[256,256]{1,0:T(8,128)(2,1)} %get-tuple-element.52), channel_id=1, source_target_pairs={{0,2},{1,3},{2,0},{3,1},{4,6},{5,7},{6,4},{7,5},{8,10},{9,11},{10,... | collective-permute-start | bytes 393224 | tf_op jit(solution)/shard_map/ppermute | solution.py:336
  212.1 33.3 %collective-permute-start.16 = (bf16[256,256]{1,0:T(8,128)(2,1)}, bf16[256,256]{1,0:T(8,128)(2,1)S(1)}, u32[]{:S(2)}, u32[]{:S(2)}) collective-permute-start(bf16[256,256]{1,0:T(8,128)(2,1)} %get-tuple-element.53), channel_id=1, source_target_pairs={{0,3},{1,2},{2,1},{3,0},{4,7},{5,6},{6,5},{7,4},{8,11},{9,10},{10,... | collective-permute-start | bytes 393224 | tf_op jit(solution)/shard_map/ppermute | solution.py:336
  230.2 15.2 %copy-start.20 = (bf16[256,256]{1,0:T(8,128)(2,1)}, bf16[256,256]{1,0:T(8,128)(2,1)S(1)}, u32[]{:S(2)}) copy-start(bf16[256,256]{1,0:T(8,128)(2,1)S(1)} %collective-permute-done.14.refs_4_) | copy-start | bytes 393220
  233.0 12.4 %copy-start.21 = (bf16[256,256]{1,0:T(8,128)(2,1)}, bf16[256,256]{1,0:T(8,128)(2,1)S(1)}, u32[]{:S(2)}) copy-start(bf16[256,256]{1,0:T(8,128)(2,1)S(1)} %collective-permute-done.15.refs_5_) | copy-start | bytes 393220
  245.3 0.7 copy-start.22
  245.3 0.7 copy-start.12
  248.0 0.8 copy-start.5
  (1 other events, 0.7 us)
Sparse Core Ops, SparseCore 0:
  115.2 46.8 reduce-scatter.1

commit v2 on v1

--- a/solution.py
+++ b/solution.py
@@ -12,7 +12,9 @@
 MAIN = 8
 REST = 2
 QUAD = 4
-VMEM = 60 * 1024 * 1024
+VMEM = 67_000_000
+NEAR, FAR = (0, 1, 2, 4), (3, 5, 6, 7)
+LAST, FIRST = (0, 1, 2, 3), (4, 5, 6, 7)
 
 
 def iota(shape, dim):
@@ -83,58 +85,69 @@
     return out
 
 
-def dispatch_kernel(where_ref, ids_ref, gates_ref, p0, p1, p2, p3, send_ref):
+def near_dispatch(where_ref, ids_ref, gates_ref, p0, p1, p2, p4, send_ref, pair_ref):
+    dispatch(where_ref, ids_ref, gates_ref, (p0[...], p1[...], p2[...], p4[...]), send_ref)
+    pair_ref[:256, :] = p0[...]
+    pair_ref[256:, :] = p4[...]
+
+
+def far_dispatch(where_ref, ids_ref, gates_ref, p37, p5, p6, send_ref):
+    pieces = (p37[:256, :], p5[...], p6[...], p37[256:, :])
+    dispatch(where_ref, ids_ref, gates_ref, pieces, send_ref)
+
+
+def dispatch(where_ref, ids_ref, gates_ref, pieces, send_ref):
     holds, weight, _ = routing(ids_ref[...], gates_ref[...], where_ref[0])
     pick = jnp.where(holds, 1.0, 0.0).astype(BF)
     gain = jnp.sum(jnp.where(holds, weight, 0.0), axis=1, keepdims=True)
     rest = []
-    for shard, ref in enumerate((p0, p1, p2, p3)):
-        x_rows = dot(pick, ref[:128, :])
-        dy_rows = dot(pick, ref[128:, :]) * gain
+    for shard, piece in enumerate(pieces):
+        x_rows = dot(pick, piece[:128, :])
+        dy_rows = dot(pick, piece[128:, :]) * gain
         rest += fold(send_ref, shard, x_rows, dy_rows)
     fold_rest(send_ref, rest)
 
 
-def shard_at(where_ref, far, shard):
-    return pl.multiple_of(((where_ref[0] ^ (far * QUAD)) ^ shard) * 256, 256)
-
-
-def fetch(where_ref, far, weights, held, sems, first=0):
-    copies = []
-    for shard in range(QUAD):
-        at = pl.ds(shard_at(where_ref, far, shard), 256)
-        parts = [w.at[at, :] for w in weights[:2]] + [w.at[:, at] for w in weights[2:]]
-        trio = [
-            pltpu.make_async_copy(src, dst.at[shard], sems.at[shard, first + n])
-            for n, (src, dst) in enumerate(zip(parts, held))
-        ]
-        for copy in trio:
-            copy.start()
-        copies.append(trio)
-    return copies
-
-
-def inward(recv_ref, copies, held, dy_list, sums):
+def shard_at(where_ref, offset):
+    return pl.multiple_of((where_ref[0] ^ offset) * 256, 256)
+
+
+def fetch(where_ref, wants, weights, held, sems):
+    copies, waited = {}, set()
+    for slot in range(max(len(v) for v in wants)):
+        for n, offsets in enumerate(wants):
+            if slot < len(offsets):
+                at = pl.ds(shard_at(where_ref, offsets[slot]), 256)
+                part = weights[n].at[:, at] if n == 2 else weights[n].at[at, :]
+                copy = pltpu.make_async_copy(part, held[n].at[slot], sems.at[n, slot])
+                copy.start()
+                copies[n, offsets[slot]] = (copy, slot)
+
+    def get(n, offset):
+        copy, slot = copies[n, offset]
+        if (n, offset) not in waited:
+            copy.wait()
+            waited.add((n, offset))
+        return held[n][slot]
+
+    return get
+
+
+def inward(recv_ref, offsets, get, sums):
     gate, up, d_hidden = sums
-    wg, wu, wd = held[:3]
-    for shard, (x_rows, dy_rows) in enumerate(unfold(recv_ref)):
-        dy_list.append(dy_rows)
-        for copy in copies[shard]:
-            copy.wait()
-        gate = gate + dot(x_rows, wg[shard])
-        up = up + dot(x_rows, wu[shard])
-        d_hidden = d_hidden + dot_nt(dy_rows, wd[shard])
-    return gate, up, d_hidden
-
-
-def outward(outs, d_gate, d_up, copies, held, send_ref):
-    wg, wu = held[:2]
+    dys = []
+    for offset, (x_rows, dy_rows) in zip(offsets, unfold(recv_ref)):
+        dys.append(dy_rows)
+        gate = gate + dot(x_rows, get(0, offset))
+        up = up + dot(x_rows, get(1, offset))
+        d_hidden = d_hidden + dot_nt(dy_rows, get(2, offset))
+    return gate, up, d_hidden, dys
+
+
+def outward(outs, d_gate, d_up, offsets, get, send_ref):
     rest = []
-    for shard in range(QUAD):
-        if copies is not None:
-            for copy in copies[shard]:
-                copy.wait()
-        dx = dot_nt(d_gate, wg[shard]) + dot_nt(d_up, wu[shard])
+    for shard, offset in enumerate(offsets):
+        dx = dot_nt(d_gate, get(0, offset)) + dot_nt(d_up, get(1, offset))
         rest += fold(send_ref, shard, outs[shard], dx)
     fold_rest(send_ref, rest)
 
@@ -146,32 +159,22 @@
     return jnp.where(((row >> 3) == (rest >> 1)) & ((row & 7) == (rest & 1)), 1.0, 0.0).astype(BF)
 
 
-def near_kernel(where_ref, recv_ref, *refs):
+def near_kernel(wants, where_ref, recv_ref, *refs):
     weights, held, sems = refs[:3], refs[7:10], refs[10]
     gate_ref, up_ref, dh_ref, dy_ref = refs[3:7]
-    copies = fetch(where_ref, 0, weights, held, sems)
+    get = fetch(where_ref, wants, weights, held, sems)
     zero = jnp.zeros(gate_ref.shape, F32)
-    dy_rows = []
-    gate_ref[...], up_ref[...], dh_ref[...] = inward(
-        recv_ref, copies, held, dy_rows, (zero, zero, zero)
-    )
-    for shard, rows in enumerate(dy_rows):
+    gate_ref[...], up_ref[...], dh_ref[...], dys = inward(recv_ref, NEAR, get, (zero, zero, zero))
+    for shard, rows in enumerate(dys):
         dy_ref[shard] = rows
 
 
-def far_kernel(where_ref, recv_ref, gate_ref, up_ref, dh_ref, near_ref, *refs):
-    weights, outs, held, sems, block = refs[:3], refs[3:12], refs[12:16], refs[16], refs[17]
-    home_ref, dgate_ref, dup_ref, send_ref, partial_ref = outs[:5]
-    copies = fetch(where_ref, 1, weights, held[:3], sems)
-    wd_near = []
-    for shard in range(QUAD):
-        at = pl.ds(shard_at(where_ref, 0, shard), 256)
-        copy = pltpu.make_async_copy(weights[2].at[:, at], held[3].at[shard], sems.at[shard, 3])
-        copy.start()
-        wd_near.append(copy)
-    dy_rows = []
-    gate, up, d_hidden = inward(
-        recv_ref, copies, held, dy_rows, (gate_ref[...], up_ref[...], dh_ref[...])
+def far_kernel(wants, where_ref, recv_ref, gate_ref, up_ref, dh_ref, near_ref, *refs):
+    weights, outs, held, sems = refs[:3], refs[3:8], refs[8:11], refs[11]
+    home_ref, dgate_ref, dup_ref, send_ref, partial_ref = outs
+    get = fetch(where_ref, wants, weights, held, sems)
+    gate, up, d_hidden, dys = inward(
+        recv_ref, FAR, get, (gate_ref[...], up_ref[...], dh_ref[...])
     )
     s = jax.nn.sigmoid(gate)
     hidden32 = gate * s * up
@@ -180,34 +183,31 @@
     d_up = (d_hidden * gate * s).astype(BF)
     dgate_ref[...] = d_gate
     dup_ref[...] = d_up
-    far_outs = [dot(hidden, held[2][shard]) for shard in range(QUAD)]
-    outward(far_outs, d_gate, d_up, None, held, send_ref)
+    dys = dict(zip(NEAR + FAR, [near_ref[shard] for shard in range(QUAD)] + dys))
+    made = {offset: dot(hidden, get(2, offset)) for offset in FAR + NEAR}
+    outward([made[offset] for offset in FIRST], d_gate, d_up, FIRST, get, send_ref)
+    get(0, FAR[0]), get(1, FAR[0])
+    for shard, offset in enumerate(LAST):
+        home_ref[shard] = made[offset].astype(BF)
     dots = jnp.zeros((gate.shape[0], 1), F32)
-    for shard in range(QUAD):
-        wd_near[shard].wait()
-        out = dot(hidden, held[3][shard]).astype(BF)
-        home_ref[shard] = out
-        for rows, dy in ((out, near_ref[shard]), (far_outs[shard].astype(BF), dy_rows[shard])):
-            dots = dots + jnp.sum(rows.astype(F32) * dy.astype(F32), axis=1, keepdims=True)
+    for offset in FAR + NEAR:
+        terms = made[offset].astype(BF).astype(F32) * dys[offset].astype(F32)
+        dots = dots + jnp.sum(terms, axis=1, keepdims=True)
     high = dots.astype(BF).astype(F32)
     terms = jnp.where(iota((dots.shape[0], 256), 1) < 128, high, dots - high)
     tail = dot(tail_pick(True), terms[MAIN * 16 :].astype(BF))
     terms = [v.reshape(16, 8, 256) for v in (terms[: MAIN * 16], tail)]
     send_ref[:, QUAD * 20 :, :] = jnp.concatenate(terms, axis=1).astype(BF)
     turned = hidden32.T.astype(BF)
-    for shard in range(QUAD):
-        at = slice(shard * 256, (shard + 1) * 256)
-        partial_ref[:, at] = dot(turned, dy_rows[shard]).astype(BF)
-        block[:, at] = dot(turned, near_ref[shard]).astype(BF)
-    for n, ref in enumerate(outs[5:]):
-        ref[...] = block[pl.ds(pl.multiple_of((where_ref[2] ^ n) * 192, 192), 192), :]
-
-
-def back_kernel(where_ref, home_ref, dgate_ref, dup_ref, *refs):
+    for n, offset in enumerate(NEAR + FAR):
+        partial_ref[:, n * 256 : (n + 1) * 256] = dot(turned, dys[offset]).astype(BF)
+
+
+def back_kernel(wants, where_ref, home_ref, dgate_ref, dup_ref, *refs):
     weights, send_ref, held, sems = refs[:2], refs[2], refs[3:5], refs[5]
-    copies = fetch(where_ref, 0, weights, held, sems)
+    get = fetch(where_ref, wants, weights, held, sems)
     outs = [home_ref[shard].astype(F32) for shard in range(QUAD)]
-    outward(outs, dgate_ref[...], dup_ref[...], copies, held, send_ref)
+    outward(outs, dgate_ref[...], dup_ref[...], LAST, get, send_ref)
 
 
 def split_lines(lines):
@@ -221,11 +221,6 @@
 def join_lines(ref):
     terms = ref[256:, :].astype(F32)
     return terms[:8, :128] + terms[:8, 128:] + terms[8:, :128]
-
-
-def first_kernel(where_ref, ids_ref, gates_ref, recv_ref, next_ref, *outs):
-    outs[-1][...] = next_ref[...]
-    combine_kernel(True, where_ref, ids_ref, gates_ref, recv_ref, *outs[:-1])
 
 
 def combine_kernel(first, where_ref, ids_ref, gates_ref, recv_ref, *outs):
@@ -257,14 +252,9 @@
         to[256:, :] = lines
 
 
-def end_kernel(where_ref, sum_ref, *refs):
-    for flip, to in enumerate(refs[-2:]):
-        rows = pl.ds(pl.multiple_of((where_ref[1] ^ flip) * 96, 96), 96)
-        total = refs[0][rows, :].astype(F32)
-        for ref in refs[1:-2]:
-            total = total + ref[rows, :].astype(F32)
-        to[:, : QUAD * 256] = total.astype(BF)
-        to[:, QUAD * 256 :] = sum_ref[rows, :]
+def end_kernel(where_ref, sum_ref, held_ref, over_ref):
+    for flip, ref in enumerate((held_ref, over_ref)):
+        ref[...] = sum_ref[pl.ds(pl.multiple_of((where_ref[1] ^ flip) * 96, 96), 96), :]
 
 
 def total_of(refs):
@@ -290,17 +280,17 @@
 
 
 def add_kernel(where_ref, held_ref, got_ref, out_ref):
-    for n in range(2 * QUAD):
+    for n, offset in enumerate(NEAR + FAR):
         at = slice(n * 256, (n + 1) * 256)
         total = held_ref[:, at].astype(F32) + got_ref[:, at].astype(F32)
-        out_ref[:, pl.ds(shard_at(where_ref, n // QUAD, n % QUAD), 256)] = total.astype(BF)
+        out_ref[:, pl.ds(shard_at(where_ref, offset), 256)] = total.astype(BF)
 
 
 def whole(shape):
     return pl.BlockSpec(shape, lambda i: (0,) * len(shape))
 
 
-def call(kernel, outs, micros, scalars, *operands, weights=(), downs=0, more=(), after=()):
+def call(kernel, outs, micros, scalars, *operands, weights=(), wants=(), after=()):
     specs = [pl.BlockSpec(memory_space=pltpu.SMEM)] + [whole(v.shape) for v in operands]
     specs += [pl.BlockSpec(memory_space=pl.ANY) for _ in (*weights, *after)]
     first = 1 + len(operands) + len(weights)
@@ -312,9 +302,11 @@
     scratch = []
     if weights:
         wide = weights[0].shape[1]
-        scratch = [pltpu.VMEM((QUAD, 256, wide), BF) for _ in weights[:2]]
-        scratch += [pltpu.VMEM((QUAD, wide, 256), BF) for _ in range(downs)]
-        scratch += [pltpu.SemaphoreType.DMA((QUAD, len(scratch)))]
+        for n, offsets in enumerate(wants):
+            cut = (wide, 256) if n == 2 else (256, wide)
+            scratch.append(pltpu.VMEM((len(offsets), *cut), BF))
+        scratch.append(pltpu.SemaphoreType.DMA((3, 2 * QUAD)))
+        kernel = functools.partial(kernel, wants)
     shapes = [jax.ShapeDtypeStruct(s, d) for s, d in outs]
     results = pl.pallas_call(
         body,
@@ -322,7 +314,7 @@
         out_shape=shapes,
         in_specs=specs,
         out_specs=[whole(v.shape) for v in shapes],
-        scratch_shapes=[*scratch, *more],
+        scratch_shapes=scratch,
         compiler_params=pltpu.CompilerParams(vmem_limit_bytes=VMEM),
         cost_estimate=pl.CostEstimate(
             flops=micros * 10**9, bytes_accessed=micros * 3 * 10**6, transcendentals=0
@@ -342,7 +334,7 @@
 
 def shards(tokens, grad_out, expert_ids, gate_weights, gate_proj, up_proj, down_proj):
     dp, lane = lax.axis_index("dp"), lax.axis_index("tp")
-    scalars = jnp.stack([lane, dp & 1, dp >> 1]).astype(jnp.int32)
+    scalars = jnp.stack([lane, dp & 1]).astype(jnp.int32)
     wg, wu, wd = gate_proj[0], up_proj[0], down_proj[0]
     width, hidden_width = wg.shape
     ids_t, gates_t = expert_ids.T, gate_weights.T
@@ -351,13 +343,13 @@
     travel = (16, QUAD * 20, 256)
 
     own = jnp.concatenate([tokens, grad_out], axis=0)
-    across = swap(own, "tp", 4)
-    near = [own] + [swap(own, "tp", d) for d in (1, 2, 3)]
-    far = [across] + [swap(across, "tp", d) for d in (1, 2, 3)]
-
-    send_near = call(dispatch_kernel, [(travel, BF)], 4, *table, *near, after=(across,))
+    near = {d: swap(own, "tp", d) for d in (4, 2, 1)}
+    send_near, pair = call(
+        near_dispatch, [(travel, BF), ((512, 256), BF)], 4, *table, own, near[1], near[2], near[4]
+    )
     got_near = over_ctx(send_near)
-    send_far = call(dispatch_kernel, [(travel, BF)], 4, *table, *far, after=(send_near,))
+    far = [swap(pair, "tp", 3), swap(near[4], "tp", 1), swap(near[4], "tp", 2)]
+    send_far = call(far_dispatch, [(travel, BF)], 4, *table, *far, after=(send_near,))
     got_far = over_ctx(send_far)
 
     sums = ((slots, hidden_width), F32)
@@ -365,33 +357,34 @@
     act = ((slots, hidden_width), BF)
     gate, up, d_hidden, dy_near = call(
         near_kernel, [sums, sums, sums, dy_shape], 5, scalars, got_near,
-        weights=(wg, wu, wd), downs=1, after=(send_far,),
+        weights=(wg, wu, wd), wants=(NEAR,) * 3, after=(send_far,),
     )
     longer = (16, QUAD * 20 + 16, 256)
-    home, d_gate, d_up, back_far, partial, *blocks = call(
+    home, d_gate, d_up, back_far, partial = call(
         far_kernel,
-        [dy_shape, act, act, (longer, BF), ((hidden_width, width // 2), BF)]
-        + [((hidden_width // 4, width // 2), BF)] * 4,
-        8, scalars, got_far, gate, up, d_hidden, dy_near, weights=(wg, wu, wd), downs=2,
-        more=(pltpu.VMEM((hidden_width, width // 2), BF),),
+        [dy_shape, act, act, (longer, BF), ((hidden_width, width), BF)],
+        8, scalars, got_far, gate, up, d_hidden, dy_near,
+        weights=(wg, wu, wd), wants=(FAR + (4,), FAR + (4,), FAR + NEAR),
     )
     home_far = over_ctx(back_far)
 
     quarter = lax.psum_scatter(
         partial, "dp", scatter_dimension=0, axis_index_groups=[[0, 2, 4, 6], [1, 3, 5, 7]], tiled=True
     )
-    came = [swap(blocks[d], "dp", d << 1) for d in (1, 2, 3)]
     back_near = call(
-        back_kernel, [(travel, BF)], 4, scalars, home, d_gate, d_up, weights=(wg, wu),
-    )
+        back_kernel, [(travel, BF)], 4, scalars, home, d_gate, d_up,
+        weights=(wg, wu), wants=(LAST, LAST),
+    )
+    home_near = over_ctx(back_near)
+
     part, longer = ((256, 256), BF), ((272, 256), BF)
-    *sums_far, leaving = call(
-        first_kernel, [longer] * 4 + [(travel, BF)], 4, *table, home_far, back_near, after=came
-    )
-    home_near = over_ctx(leaving)
+    sums_far = call(
+        functools.partial(combine_kernel, True), [longer] * 4, 4, *table, home_far,
+        after=(back_near,),
+    )
     came_far = [swap(sums_far[d], "tp", d) for d in (1, 2, 3)]
     end = ((96, width), BF)
-    held, over = call(end_kernel, [end, end], 1, scalars, quarter, blocks[0], *came, after=(sums_far[0],))
+    held, over = call(end_kernel, [end, end], 1, scalars, quarter, after=(sums_far[0],))
     ends = swap(over, "dp", 1)
     total_far = call(total_kernel, [longer], 1, scalars, sums_far[0], *came_far, after=(over,))
     from_far = swap(total_far, "tp", 4)

time: 259 us -> 238 us (0.919)
  starting transfers between devices: 118 us -> 88.3 us
  waiting for transfers between devices: 75 us -> 90.4 us
  local copies, waits for them, and re-layouts: 9.75 us -> 2.34 us
    all_to_all x4, waiting for transfers between devices: 14.8 us -> 30.1 us  [over_ctx(): return lax.all_to_all(value, 'ctx', split_axis=0, concat_axis=0, tiled=True)]
    ppermute x18 -> x14, starting transfers between devices: 80.2 us -> 65.3 us  [swap(): return lax.ppermute(value, axis, [(i, i ^ bit) for i in range(size)])]
    all_to_all x4, starting transfers between devices: 37.3 us -> 23 us  [over_ctx(): return lax.all_to_all(value, 'ctx', split_axis=0, concat_axis=0, tiled=True)]
    unnamed x53 -> x9, local copies, waits for them, and re-layouts: 8.9 us -> 1.5 us
    reduce_scatter x1, waiting for transfers between devices: 0.02 us -> 5.79 us  [shards(): lax.psum_scatter(partial, 'dp', scatter_dimension=0, axis_index_groups=[[...]
    ppermute x18 -> x14, waiting for transfers between devices: 60.2 us -> 54.5 us  [swap(): return lax.ppermute(value, axis, [(i, i ^ bit) for i in range(size)])]
  transfers between devices with their start and end apart: 23 -> 19, of which waited for: 8 -> 8; matrix products, arithmetic and copies ran while one was open for 0% -> 0% of each run, Pallas kernels for 10% -> 11%
where the time goes in v2:
time: 238 us; the launch traced here: 236 us
  waiting for transfers between devices  90.4 us (38%)
  starting transfers between devices  88.3 us (37%)
  Pallas kernels  40.4 us (17%)
  between operations  14.2 us (6%)
    ppermute x14, starting transfers between devices, swap(): return lax.ppermute(value, axis, [(i, i ^ bit) for i in range(size)])  65.3 us
    ppermute x14, waiting for transfers between devices, swap(): return lax.ppermute(value, axis, [(i, i ^ bit) for i in range(size)])  54.5 us
    pallas_call x11, Pallas kernels, call(): pl.pallas_call(body, grid=(1,), out_shape=shapes, in_specs=specs, out_spe...  40.4 us
    all_to_all x4, waiting for transfers between devices, over_ctx(): return lax.all_to_all(value, 'ctx', split_axis=0, concat_axis=0, tiled=True)  30.1 us
    all_to_all x4, starting transfers between devices, over_ctx(): return lax.all_to_all(value, 'ctx', split_axis=0, concat_axis=0, tiled=True)  23 us
    reduce_scatter x1, waiting for transfers between devices, shards(): lax.psum_scatter(partial, 'dp', scatter_dimension=0, axis_index_groups=[[...  5.79 us
  transfers between devices with their start and end apart: 19, of which 8 were waited for; matrix products, arithmetic and copies ran while one was open for 0% of the time, Pallas kernels for 11%

profile of v2, /device:TPU:1, one launch (start us, length us, event | category | flops | bytes accessed | tf_op | source)
XLA Modules:
  0.0 236.4 jit_solution(5523217991243146031)
XLA Ops:
  7.2 0.8 constant_dynamic-update-slice_fusion.1
  8.0 0.8 constant_dynamic-update-slice_fusion.refs_3_
  8.9 11.5 %collective-permute-start.2 = (bf16[256,256]{1,0:T(8,128)(2,1)S(1)}, bf16[256,256]{1,0:T(8,128)(2,1)S(1)}, u32[]{:S(2)}, u32[]{:S(2)}) collective-permute-start(bf16[256,256]{1,0:T(8,128)(2,1)S(1)} %constant_dynamic-update-slice_fusion.refs_3_), channel_id=1, source_target_pairs={{0,4},{1,5},{2,6},{3,7},{4,0},{5,1},{6,2},{7,3},{8,12},{9,13},{10,... | collective-permute-start | bytes 393224 | tf_op jit(solution)/shard_map/ppermute | solution.py:328
  20.3 5.8 %collective-permute-start.1 = (bf16[256,256]{1,0:T(8,128)(2,1)S(1)}, bf16[256,256]{1,0:T(8,128)(2,1)S(1)}, u32[]{:S(2)}, u32[]{:S(2)}) collective-permute-start(bf16[256,256]{1,0:T(8,128)(2,1)S(1)} %constant_dynamic-update-slice_fusion.refs_3_), channel_id=1, source_target_pairs={{0,2},{1,3},{2,0},{3,1},{4,6},{5,7},{6,4},{7,5},{8,10},{9,11},{10,... | collective-permute-start | bytes 393224 | tf_op jit(solution)/shard_map/ppermute | solution.py:328
  26.1 4.0 %collective-permute-start = (bf16[256,256]{1,0:T(8,128)(2,1)S(1)}, bf16[256,256]{1,0:T(8,128)(2,1)S(1)}, u32[]{:S(2)}, u32[]{:S(2)}) collective-permute-start(bf16[256,256]{1,0:T(8,128)(2,1)S(1)} %constant_dynamic-update-slice_fusion.refs_3_), channel_id=1, source_target_pairs={{0,1},{1,0},{2,3},{3,2},{4,5},{5,4},{6,7},{7,6},{8,9},{9,8},{10,11... | collective-permute-start | bytes 393224 | tf_op jit(solution)/shard_map/ppermute | solution.py:328
  30.2 0.6 pad_add_fusion.refs_0_
  30.8 0.0 collective-permute-done.2.refs_6_
  30.8 5.3 %collective-permute-done.refs_4_ = bf16[256,256]{1,0:T(8,128)(2,1)S(1)} collective-permute-done((bf16[256,256]{1,0:T(8,128)(2,1)S(1)}, bf16[256,256]{1,0:T(8,128)(2,1)S(1)}, u32[]{:S(2)}, u32[]{:S(2)}) %collective-permute-start) | collective-permute-done | bytes 131104 | tf_op jit(solution)/shard_map/ppermute | solution.py:328
  36.1 0.6 copy-done.3
  36.7 2.7 %shard_map.102 = (bf16[16,80,256]{2,1,0:T(8,128)(2,1)}, bf16[512,256]{1,0:T(8,128)(2,1)}) custom-call(s32[2]{0:T(128)} %pad_add_fusion.refs_0_, s32[8,128]{1,0:T(8,128)} %bitcast.17, f32[8,128]{1,0:T(8,128)} %bitcast.21, bf16[256,256]{1,0:T(8,128)(2,1)} %copy-done, bf16[256,256]{1,0:T(8,128)(2,1)} %copy-done.3, bf16[256,256]{1,0:T(8,128)(2,1)} %copy-done.2, ...), custom_call_target="tpu_custom_call" | custom-call | flops 4000000000 | bytes 12000000 | tf_op jit(solution)/shard_map/pallas_call | solution.py:311
  39.4 7.0 %all-to-all-start.1 = ((bf16[16,80,256]{2,1,0:T(8,128)(2,1)}), bf16[16,80,256]{2,1,0:T(8,128)(2,1)}, u32[]{:S(2)}, u32[]{:S(2)}) async-start(bf16[16,80,256]{2,1,0:T(8,128)(2,1)} %get-tuple-element.29.refs_6_), calls=%async_computation.1 | async-start | bytes 1310720 | tf_op jit(solution)/shard_map/all_to_all | solution.py:332
  46.5 5.2 %collective-permute-start.3 = (bf16[512,256]{1,0:T(8,128)(2,1)}, bf16[512,256]{1,0:T(8,128)(2,1)}, u32[]{:S(2)}, u32[]{:S(2)}) collective-permute-start(bf16[512,256]{1,0:T(8,128)(2,1)} %get-tuple-element.28), channel_id=1, source_target_pairs={{0,3},{1,2},{2,1},{3,0},{4,7},{5,6},{6,5},{7,4},{8,11},{9,10},{10,... | collective-permute-start | bytes 786440 | tf_op jit(solution)/shard_map/ppermute | solution.py:328
  51.7 1.9 collective-permute-start.5
  53.6 2.2 collective-permute-start.4
  55.8 12.9 %collective-permute-done.5.refs_5_ = bf16[256,256]{1,0:T(8,128)(2,1)} collective-permute-done((bf16[256,256]{1,0:T(8,128)(2,1)}, bf16[256,256]{1,0:T(8,128)(2,1)}, u32[]{:S(2)}, u32[]{:S(2)}) %collective-permute-start.5) | collective-permute-done | bytes 131104 | tf_op jit(solution)/shard_map/ppermute | solution.py:328
  68.7 0.0 collective-permute-done.4.refs_4_
  68.7 0.0 collective-permute-done.3.refs_3_
  68.7 2.6 %shard_map.103.refs_5_ = bf16[16,80,256]{2,1,0:T(8,128)(2,1)} custom-call(s32[2]{0:T(128)} %pad_add_fusion.refs_0_, s32[8,128]{1,0:T(8,128)} %bitcast.18, f32[8,128]{1,0:T(8,128)} %bitcast.22, bf16[512,256]{1,0:T(8,128)(2,1)} %collective-permute-done.3.refs_3_, bf16[256,256]{1,0:T(8,128)(2,1)} %collective-permute-done.4.refs_4_, ...), custom_call_target="tpu_custom_call" | custom-call | flops 4000000000 | bytes 12000000 | tf_op jit(solution)/shard_map/pallas_call | solution.py:311
  71.3 7.6 %all-to-all-start = ((bf16[16,80,256]{2,1,0:T(8,128)(2,1)}), bf16[16,80,256]{2,1,0:T(8,128)(2,1)}, u32[]{:S(2)}, u32[]{:S(2)}) async-start(bf16[16,80,256]{2,1,0:T(8,128)(2,1)} %shard_map.103.refs_5_), calls=%async_computation | async-start | bytes 1310720 | tf_op jit(solution)/shard_map/all_to_all | solution.py:332
  78.9 0.0 reduce-scatter.2.cloned.1.call-start
  79.0 5.6 %shard_map.104 = (f32[160,768]{1,0:T(8,128)}, f32[160,768]{1,0:T(8,128)}, f32[160,768]{1,0:T(8,128)}, bf16[4,160,256]{2,1,0:T(8,128)(2,1)}) custom-call(s32[2]{0:T(128)} %pad_add_fusion.refs_0_, bf16[16,80,256]{2,1,0:T(8,128)(2,1)} %all-to-all-done.1.refs_1_, bf16[2048,768]{1,0:T(8,128)(2,1)} %bitcast.11, bf16[2048,768]{1,0:T(8,128)(2,1)} %bitcast.14, ...), custom_call_target="tpu_custom_call" | custom-call | flops 5000000000 | bytes 15000000 | tf_op jit(solution)/shard_map/pallas_call | solution.py:311
  84.6 14.5 %all-to-all-done.refs_1_ = bf16[16,80,256]{2,1,0:T(8,128)(2,1)} async-done(((bf16[16,80,256]{2,1,0:T(8,128)(2,1)}), bf16[16,80,256]{2,1,0:T(8,128)(2,1)}, u32[]{:S(2)}, u32[]{:S(2)}) %all-to-all-start) | async-done | bytes 655392 | tf_op jit(solution)/shard_map/all_to_all | solution.py:332
  99.0 10.6 %shard_map.105 = (bf16[4,160,256]{2,1,0:T(8,128)(2,1)}, bf16[160,768]{1,0:T(8,128)(2,1)}, bf16[160,768]{1,0:T(8,128)(2,1)}, bf16[16,96,256]{2,1,0:T(8,128)(2,1)}, bf16[768,2048]{1,0:T(8,128)(2,1)}) custom-call(s32[2]{0:T(128)} %pad_add_fusion.refs_0_, bf16[16,80,256]{2,1,0:T(8,128)(2,1)} %all-to-all-done.refs_1_, f32[160,768]{1,0:T(8,128)} %get-tuple-element.30.refs_2_, ...), custom_call_target="tpu_custom_call" | custom-call | flops 8000000000 | bytes 24000000 | tf_op jit(solution)/shard_map/pallas_call | solution.py:311
  109.7 0.0 reduce-scatter.2.cloned.1.call-update
  109.7 4.2 %all-to-all-start.2 = ((bf16[16,96,256]{2,1,0:T(8,128)(2,1)}), bf16[16,96,256]{2,1,0:T(8,128)(2,1)}, u32[]{:S(2)}, u32[]{:S(2)}) async-start(bf16[16,96,256]{2,1,0:T(8,128)(2,1)} %get-tuple-element.34), calls=%async_computation.2 | async-start | bytes 1572864 | tf_op jit(solution)/shard_map/all_to_all | solution.py:332
  113.9 5.9 %shard_map.106.refs_4_ = bf16[16,80,256]{2,1,0:T(8,128)(2,1)} custom-call(s32[2]{0:T(128)} %pad_add_fusion.refs_0_, bf16[4,160,256]{2,1,0:T(8,128)(2,1)} %get-tuple-element.35.refs_1_, bf16[160,768]{1,0:T(8,128)(2,1)} %get-tuple-element.36.refs_2_, bf16[160,768]{1,0:T(8,128)(2,1)} %get-tuple-element.37.refs_3_, bf16[2048,768]{1,0:T(8,128)(2,1)} %bitcast.13, ...), custom_call_target="tpu_custom_call" | custom-call | flops 4000000000 | bytes 12000000 | tf_op jit(solution)/shard_map/pallas_call | solution.py:311
  119.8 15.7 %all-to-all-done.2.refs_3_ = bf16[16,96,256]{2,1,0:T(8,128)(2,1)} async-done(((bf16[16,96,256]{2,1,0:T(8,128)(2,1)}), bf16[16,96,256]{2,1,0:T(8,128)(2,1)}, u32[]{:S(2)}, u32[]{:S(2)}) %all-to-all-start.2) | async-done | bytes 786464 | tf_op jit(solution)/shard_map/all_to_all | solution.py:332
  135.5 4.2 %all-to-all-start.3 = ((bf16[16,80,256]{2,1,0:T(8,128)(2,1)}), bf16[16,80,256]{2,1,0:T(8,128)(2,1)}, u32[]{:S(2)}, u32[]{:S(2)}) async-start(bf16[16,80,256]{2,1,0:T(8,128)(2,1)} %shard_map.106.refs_4_), calls=%async_computation.4 | async-start | bytes 1310720 | tf_op jit(solution)/shard_map/all_to_all | solution.py:332
  139.7 2.7 %shard_map.107 = (bf16[272,256]{1,0:T(8,128)(2,1)}, bf16[272,256]{1,0:T(8,128)(2,1)}, bf16[272,256]{1,0:T(8,128)(2,1)}, bf16[272,256]{1,0:T(8,128)(2,1)}) custom-call(s32[2]{0:T(128)} %pad_add_fusion.refs_0_, s32[8,128]{1,0:T(8,128)} %bitcast.19, f32[8,128]{1,0:T(8,128)} %bitcast.23, bf16[16,96,256]{2,1,0:T(8,128)(2,1)} %all-to-all-done.2.refs_3_, ...), custom_call_target="tpu_custom_call" | custom-call | flops 4000000000 | bytes 12000000 | tf_op jit(solution)/shard_map/pallas_call | solution.py:311
  142.4 1.9 collective-permute-start.6
  144.3 4.5 %collective-permute-start.7 = (bf16[272,256]{1,0:T(8,128)(2,1)}, bf16[272,256]{1,0:T(8,128)(2,1)}, u32[]{:S(2)}, u32[]{:S(2)}) collective-permute-start(bf16[272,256]{1,0:T(8,128)(2,1)} %get-tuple-element.40), channel_id=1, source_target_pairs={{0,2},{1,3},{2,0},{3,1},{4,6},{5,7},{6,4},{7,5},{8,10},{9,11},{10,... | collective-permute-start | bytes 417800 | tf_op jit(solution)/shard_map/ppermute | solution.py:328
  148.9 2.8 %collective-permute-start.8 = (bf16[272,256]{1,0:T(8,128)(2,1)}, bf16[272,256]{1,0:T(8,128)(2,1)}, u32[]{:S(2)}, u32[]{:S(2)}) collective-permute-start(bf16[272,256]{1,0:T(8,128)(2,1)} %get-tuple-element.41), channel_id=1, source_target_pairs={{0,3},{1,2},{2,1},{3,0},{4,7},{5,6},{6,5},{7,4},{8,11},{9,10},{10,... | collective-permute-start | bytes 417800 | tf_op jit(solution)/shard_map/ppermute | solution.py:328
  151.7 5.8 %reduce-scatter.2.cloned.1.call-done.refs_1_ = bf16[192,2048]{1,0:T(8,128)(2,1)} async-done(((bf16[768,2048]{1,0:T(8,128)(2,1)}), bf16[192,2048]{1,0:T(8,128)(2,1)}) %reduce-scatter.2.cloned.1.call-update) | async-done | bytes 786448 | tf_op jit(solution)/shard_map/reduce_scatter | solution.py:371
  157.5 2.1 shard_map.108
  159.6 13.3 %collective-permute-start.13 = (bf16[96,2048]{1,0:T(8,128)(2,1)}, bf16[96,2048]{1,0:T(8,128)(2,1)}, u32[]{:S(2)}, u32[]{:S(2)}) collective-permute-start(bf16[96,2048]{1,0:T(8,128)(2,1)} %get-tuple-element.43.refs_5_), channel_id=1, source_target_pairs={{0,128},{128,0},{256,384},{384,256},{512,640},{640,512},{768,896},... | collective-permute-start | bytes 1179656 | tf_op jit(solution)/shard_map/ppermute | solution.py:328
  172.9 0.0 collective-permute-done.8.refs_4_
  172.9 1.8 shard_map.109.refs_4_.refs_1_
  174.7 2.9 %collective-permute-start.9 = (bf16[272,256]{1,0:T(8,128)(2,1)}, bf16[272,256]{1,0:T(8,128)(2,1)}, u32[]{:S(2)}, u32[]{:S(2)}) collective-permute-start(bf16[272,256]{1,0:T(8,128)(2,1)} %shard_map.109.refs_4_.refs_1_), channel_id=1, source_target_pairs={{0,4},{1,5},{2,6},{3,7},{4,0},{5,1},{6,2},{7,3},{8,12},{9,13},{10,... | collective-permute-start | bytes 417800 | tf_op jit(solution)/shard_map/ppermute | solution.py:328
  177.6 0.0 all-to-all-done.3.refs_3_
  177.7 2.5 %shard_map.110 = (bf16[256,256]{1,0:T(8,128)(2,1)}, bf16[256,256]{1,0:T(8,128)(2,1)}, bf16[256,256]{1,0:T(8,128)(2,1)}, bf16[256,256]{1,0:T(8,128)(2,1)}) custom-call(s32[2]{0:T(128)} %pad_add_fusion.refs_0_, s32[8,128]{1,0:T(8,128)} %bitcast.20, f32[8,128]{1,0:T(8,128)} %bitcast.24, bf16[16,80,256]{2,1,0:T(8,128)(2,1)} %all-to-all-done.3.refs_3_, ...), custom_call_target="tpu_custom_call" | custom-call | flops 4000000000 | bytes 12000000 | tf_op jit(solution)/shard_map/pallas_call | solution.py:311
  180.1 2.4 collective-permute-start.10
  182.5 2.6 %collective-permute-start.11 = (bf16[256,256]{1,0:T(8,128)(2,1)}, bf16[256,256]{1,0:T(8,128)(2,1)}, u32[]{:S(2)}, u32[]{:S(2)}) collective-permute-start(bf16[256,256]{1,0:T(8,128)(2,1)} %get-tuple-element.46), channel_id=1, source_target_pairs={{0,2},{1,3},{2,0},{3,1},{4,6},{5,7},{6,4},{7,5},{8,10},{9,11},{10,... | collective-permute-start | bytes 393224 | tf_op jit(solution)/shard_map/ppermute | solution.py:328
  185.1 4.3 %collective-permute-start.12 = (bf16[256,256]{1,0:T(8,128)(2,1)}, bf16[256,256]{1,0:T(8,128)(2,1)}, u32[]{:S(2)}, u32[]{:S(2)}) collective-permute-start(bf16[256,256]{1,0:T(8,128)(2,1)} %get-tuple-element.47), channel_id=1, source_target_pairs={{0,3},{1,2},{2,1},{3,0},{4,7},{5,6},{6,5},{7,4},{8,11},{9,10},{10,... | collective-permute-start | bytes 393224 | tf_op jit(solution)/shard_map/ppermute | solution.py:328
  189.4 23.3 %collective-permute-done.10.refs_4_ = bf16[256,256]{1,0:T(8,128)(2,1)} collective-permute-done((bf16[256,256]{1,0:T(8,128)(2,1)}, bf16[256,256]{1,0:T(8,128)(2,1)}, u32[]{:S(2)}, u32[]{:S(2)}) %collective-permute-start.10) | collective-permute-done | bytes 131104 | tf_op jit(solution)/shard_map/ppermute | solution.py:328
  212.7 0.5 collective-permute-done.11.refs_5_
  213.2 12.4 %collective-permute-done.12.refs_6_ = bf16[256,256]{1,0:T(8,128)(2,1)} collective-permute-done((bf16[256,256]{1,0:T(8,128)(2,1)}, bf16[256,256]{1,0:T(8,128)(2,1)}, u32[]{:S(2)}, u32[]{:S(2)}) %collective-permute-start.12) | collective-permute-done | bytes 131104 | tf_op jit(solution)/shard_map/ppermute | solution.py:328
  225.7 1.9 shard_map.111
  227.6 2.0 shard_map.112
  (13 shorter events, 0.0 us)
Async XLA Ops:
  8.9 17.3 %copy-start = (bf16[256,256]{1,0:T(8,128)(2,1)}, bf16[256,256]{1,0:T(8,128)(2,1)S(1)}, u32[]{:S(2)}) copy-start(bf16[256,256]{1,0:T(8,128)(2,1)S(1)} %constant_dynamic-update-slice_fusion.refs_3_) | copy-start | bytes 393220
  8.9 21.9 %collective-permute-start.2 = (bf16[256,256]{1,0:T(8,128)(2,1)S(1)}, bf16[256,256]{1,0:T(8,128)(2,1)S(1)}, u32[]{:S(2)}, u32[]{:S(2)}) collective-permute-start(bf16[256,256]{1,0:T(8,128)(2,1)S(1)} %constant_dynamic-update-slice_fusion.refs_3_), channel_id=1, source_target_pairs={{0,4},{1,5},{2,6},{3,7},{4,0},{5,1},{6,2},{7,3},{8,12},{9,13},{10,... | collective-permute-start | bytes 393224 | tf_op jit(solution)/shard_map/ppermute | solution.py:328
  20.3 10.5 %collective-permute-start.1 = (bf16[256,256]{1,0:T(8,128)(2,1)S(1)}, bf16[256,256]{1,0:T(8,128)(2,1)S(1)}, u32[]{:S(2)}, u32[]{:S(2)}) collective-permute-start(bf16[256,256]{1,0:T(8,128)(2,1)S(1)} %constant_dynamic-update-slice_fusion.refs_3_), channel_id=1, source_target_pairs={{0,2},{1,3},{2,0},{3,1},{4,6},{5,7},{6,4},{7,5},{8,10},{9,11},{10,... | collective-permute-start | bytes 393224 | tf_op jit(solution)/shard_map/ppermute | solution.py:328
  26.1 9.9 %collective-permute-start = (bf16[256,256]{1,0:T(8,128)(2,1)S(1)}, bf16[256,256]{1,0:T(8,128)(2,1)S(1)}, u32[]{:S(2)}, u32[]{:S(2)}) collective-permute-start(bf16[256,256]{1,0:T(8,128)(2,1)S(1)} %constant_dynamic-update-slice_fusion.refs_3_), channel_id=1, source_target_pairs={{0,1},{1,0},{2,3},{3,2},{4,5},{5,4},{6,7},{7,6},{8,9},{9,8},{10,11... | collective-permute-start | bytes 393224 | tf_op jit(solution)/shard_map/ppermute | solution.py:328
  30.8 5.3 %copy-start.1 = (bf16[256,256]{1,0:T(8,128)(2,1)}, bf16[256,256]{1,0:T(8,128)(2,1)S(1)}, u32[]{:S(2)}) copy-start(bf16[256,256]{1,0:T(8,128)(2,1)S(1)} %collective-permute-done.2.refs_6_) | copy-start | bytes 393220
  30.8 5.3 %copy-start.2 = (bf16[256,256]{1,0:T(8,128)(2,1)}, bf16[256,256]{1,0:T(8,128)(2,1)S(1)}, u32[]{:S(2)}) copy-start(bf16[256,256]{1,0:T(8,128)(2,1)S(1)} %collective-permute-done.1.refs_5_) | copy-start | bytes 393220
  36.1 0.6 copy-start.3
  39.4 31.9 %all-to-all-start.1 = ((bf16[16,80,256]{2,1,0:T(8,128)(2,1)}), bf16[16,80,256]{2,1,0:T(8,128)(2,1)}, u32[]{:S(2)}, u32[]{:S(2)}) async-start(bf16[16,80,256]{2,1,0:T(8,128)(2,1)} %get-tuple-element.29.refs_6_), calls=%async_computation.1 | async-start | bytes 1310720 | tf_op jit(solution)/shard_map/all_to_all | solution.py:332
  46.5 22.3 %collective-permute-start.3 = (bf16[512,256]{1,0:T(8,128)(2,1)}, bf16[512,256]{1,0:T(8,128)(2,1)}, u32[]{:S(2)}, u32[]{:S(2)}) collective-permute-start(bf16[512,256]{1,0:T(8,128)(2,1)} %get-tuple-element.28), channel_id=1, source_target_pairs={{0,3},{1,2},{2,1},{3,0},{4,7},{5,6},{6,5},{7,4},{8,11},{9,10},{10,... | collective-permute-start | bytes 786440 | tf_op jit(solution)/shard_map/ppermute | solution.py:328
  51.7 17.0 %collective-permute-start.5 = (bf16[256,256]{1,0:T(8,128)(2,1)}, bf16[256,256]{1,0:T(8,128)(2,1)}, u32[]{:S(2)}, u32[]{:S(2)}) collective-permute-start(bf16[256,256]{1,0:T(8,128)(2,1)} %copy-done.1), channel_id=1, source_target_pairs={{0,2},{1,3},{2,0},{3,1},{4,6},{5,7},{6,4},{7,5},{8,10},{9,11},{10,... | collective-permute-start | bytes 393224 | tf_op jit(solution)/shard_map/ppermute | solution.py:328
  53.6 15.1 %collective-permute-start.4 = (bf16[256,256]{1,0:T(8,128)(2,1)}, bf16[256,256]{1,0:T(8,128)(2,1)}, u32[]{:S(2)}, u32[]{:S(2)}) collective-permute-start(bf16[256,256]{1,0:T(8,128)(2,1)} %copy-done.1), channel_id=1, source_target_pairs={{0,1},{1,0},{2,3},{3,2},{4,5},{5,4},{6,7},{7,6},{8,9},{9,8},{10,11... | collective-permute-start | bytes 393224 | tf_op jit(solution)/shard_map/ppermute | solution.py:328
  71.3 27.7 %all-to-all-start = ((bf16[16,80,256]{2,1,0:T(8,128)(2,1)}), bf16[16,80,256]{2,1,0:T(8,128)(2,1)}, u32[]{:S(2)}, u32[]{:S(2)}) async-start(bf16[16,80,256]{2,1,0:T(8,128)(2,1)} %shard_map.103.refs_5_), calls=%async_computation | async-start | bytes 1310720 | tf_op jit(solution)/shard_map/all_to_all | solution.py:332
  78.9 78.6 %reduce-scatter.2.cloned.1.call-start = ((), (), s32[]{:S(2)}) async-start(), calls=%async_computation.5 | async-start | bytes 3932160 | tf_op jit(solution)/shard_map/reduce_scatter | solution.py:371
  109.7 25.8 %all-to-all-start.2 = ((bf16[16,96,256]{2,1,0:T(8,128)(2,1)}), bf16[16,96,256]{2,1,0:T(8,128)(2,1)}, u32[]{:S(2)}, u32[]{:S(2)}) async-start(bf16[16,96,256]{2,1,0:T(8,128)(2,1)} %get-tuple-element.34), calls=%async_computation.2 | async-start | bytes 1572864 | tf_op jit(solution)/shard_map/all_to_all | solution.py:332
  135.5 42.1 %all-to-all-start.3 = ((bf16[16,80,256]{2,1,0:T(8,128)(2,1)}), bf16[16,80,256]{2,1,0:T(8,128)(2,1)}, u32[]{:S(2)}, u32[]{:S(2)}) async-start(bf16[16,80,256]{2,1,0:T(8,128)(2,1)} %shard_map.106.refs_4_), calls=%async_computation.4 | async-start | bytes 1310720 | tf_op jit(solution)/shard_map/all_to_all | solution.py:332
  142.4 30.4 %collective-permute-start.6 = (bf16[272,256]{1,0:T(8,128)(2,1)}, bf16[272,256]{1,0:T(8,128)(2,1)}, u32[]{:S(2)}, u32[]{:S(2)}) collective-permute-start(bf16[272,256]{1,0:T(8,128)(2,1)} %get-tuple-element.39), channel_id=1, source_target_pairs={{0,1},{1,0},{2,3},{3,2},{4,5},{5,4},{6,7},{7,6},{8,9},{9,8},{10,11... | collective-permute-start | bytes 417800 | tf_op jit(solution)/shard_map/ppermute | solution.py:328
  144.3 28.5 %collective-permute-start.7 = (bf16[272,256]{1,0:T(8,128)(2,1)}, bf16[272,256]{1,0:T(8,128)(2,1)}, u32[]{:S(2)}, u32[]{:S(2)}) collective-permute-start(bf16[272,256]{1,0:T(8,128)(2,1)} %get-tuple-element.40), channel_id=1, source_target_pairs={{0,2},{1,3},{2,0},{3,1},{4,6},{5,7},{6,4},{7,5},{8,10},{9,11},{10,... | collective-permute-start | bytes 417800 | tf_op jit(solution)/shard_map/ppermute | solution.py:328
  148.9 24.0 %collective-permute-start.8 = (bf16[272,256]{1,0:T(8,128)(2,1)}, bf16[272,256]{1,0:T(8,128)(2,1)}, u32[]{:S(2)}, u32[]{:S(2)}) collective-permute-start(bf16[272,256]{1,0:T(8,128)(2,1)} %get-tuple-element.41), channel_id=1, source_target_pairs={{0,3},{1,2},{2,1},{3,0},{4,7},{5,6},{6,5},{7,4},{8,11},{9,10},{10,... | collective-permute-start | bytes 417800 | tf_op jit(solution)/shard_map/ppermute | solution.py:328
  159.6 68.0 %collective-permute-start.13 = (bf16[96,2048]{1,0:T(8,128)(2,1)}, bf16[96,2048]{1,0:T(8,128)(2,1)}, u32[]{:S(2)}, u32[]{:S(2)}) collective-permute-start(bf16[96,2048]{1,0:T(8,128)(2,1)} %get-tuple-element.43.refs_5_), channel_id=1, source_target_pairs={{0,128},{128,0},{256,384},{384,256},{512,640},{640,512},{768,896},... | collective-permute-start | bytes 1179656 | tf_op jit(solution)/shard_map/ppermute | solution.py:328
  174.7 51.0 %collective-permute-start.9 = (bf16[272,256]{1,0:T(8,128)(2,1)}, bf16[272,256]{1,0:T(8,128)(2,1)}, u32[]{:S(2)}, u32[]{:S(2)}) collective-permute-start(bf16[272,256]{1,0:T(8,128)(2,1)} %shard_map.109.refs_4_.refs_1_), channel_id=1, source_target_pairs={{0,4},{1,5},{2,6},{3,7},{4,0},{5,1},{6,2},{7,3},{8,12},{9,13},{10,... | collective-permute-start | bytes 417800 | tf_op jit(solution)/shard_map/ppermute | solution.py:328
  180.1 32.6 %collective-permute-start.10 = (bf16[256,256]{1,0:T(8,128)(2,1)}, bf16[256,256]{1,0:T(8,128)(2,1)}, u32[]{:S(2)}, u32[]{:S(2)}) collective-permute-start(bf16[256,256]{1,0:T(8,128)(2,1)} %get-tuple-element.45), channel_id=1, source_target_pairs={{0,1},{1,0},{2,3},{3,2},{4,5},{5,4},{6,7},{7,6},{8,9},{9,8},{10,11... | collective-permute-start | bytes 393224 | tf_op jit(solution)/shard_map/ppermute | solution.py:328
  182.5 30.8 %collective-permute-start.11 = (bf16[256,256]{1,0:T(8,128)(2,1)}, bf16[256,256]{1,0:T(8,128)(2,1)}, u32[]{:S(2)}, u32[]{:S(2)}) collective-permute-start(bf16[256,256]{1,0:T(8,128)(2,1)} %get-tuple-element.46), channel_id=1, source_target_pairs={{0,2},{1,3},{2,0},{3,1},{4,6},{5,7},{6,4},{7,5},{8,10},{9,11},{10,... | collective-permute-start | bytes 393224 | tf_op jit(solution)/shard_map/ppermute | solution.py:328
  185.1 40.6 %collective-permute-start.12 = (bf16[256,256]{1,0:T(8,128)(2,1)}, bf16[256,256]{1,0:T(8,128)(2,1)}, u32[]{:S(2)}, u32[]{:S(2)}) collective-permute-start(bf16[256,256]{1,0:T(8,128)(2,1)} %get-tuple-element.47), channel_id=1, source_target_pairs={{0,3},{1,2},{2,1},{3,0},{4,7},{5,6},{6,5},{7,4},{8,11},{9,10},{10,... | collective-permute-start | bytes 393224 | tf_op jit(solution)/shard_map/ppermute | solution.py:328
Sparse Core Ops, SparseCore 0:
  109.8 47.6 reduce-scatter.1

commit v3 on v2

--- a/solution.py
+++ b/solution.py
@@ -170,7 +170,7 @@
 
 
 def far_kernel(wants, where_ref, recv_ref, gate_ref, up_ref, dh_ref, near_ref, *refs):
-    weights, outs, held, sems = refs[:3], refs[3:8], refs[8:11], refs[11]
+    weights, outs, held, sems, block, ends = refs[:3], refs[3:8], refs[8:11], *refs[11:14]
     home_ref, dgate_ref, dup_ref, send_ref, partial_ref = outs
     get = fetch(where_ref, wants, weights, held, sems)
     gate, up, d_hidden, dys = inward(
@@ -184,6 +184,14 @@
     dgate_ref[...] = d_gate
     dup_ref[...] = d_up
     dys = dict(zip(NEAR + FAR, [near_ref[shard] for shard in range(QUAD)] + dys))
+    turned = hidden32.T.astype(BF)
+    leaving = []
+    for n, offset in enumerate(NEAR + FAR):
+        at = slice(n * 256, (n + 1) * 256)
+        block[:, at] = dot(turned, dys[offset]).astype(BF)
+        copy = pltpu.make_async_copy(block.at[:, at], partial_ref.at[:, at], ends.at[n])
+        copy.start()
+        leaving.append(copy)
     made = {offset: dot(hidden, get(2, offset)) for offset in FAR + NEAR}
     outward([made[offset] for offset in FIRST], d_gate, d_up, FIRST, get, send_ref)
     get(0, FAR[0]), get(1, FAR[0])
@@ -198,9 +206,8 @@
     tail = dot(tail_pick(True), terms[MAIN * 16 :].astype(BF))
     terms = [v.reshape(16, 8, 256) for v in (terms[: MAIN * 16], tail)]
     send_ref[:, QUAD * 20 :, :] = jnp.concatenate(terms, axis=1).astype(BF)
-    turned = hidden32.T.astype(BF)
-    for n, offset in enumerate(NEAR + FAR):
-        partial_ref[:, n * 256 : (n + 1) * 256] = dot(turned, dys[offset]).astype(BF)
+    for copy in leaving:
+        copy.wait()
 
 
 def back_kernel(wants, where_ref, home_ref, dgate_ref, dup_ref, *refs):
@@ -252,9 +259,8 @@
         to[256:, :] = lines
 
 
-def end_kernel(where_ref, sum_ref, held_ref, over_ref):
-    for flip, ref in enumerate((held_ref, over_ref)):
-        ref[...] = sum_ref[pl.ds(pl.multiple_of((where_ref[1] ^ flip) * 96, 96), 96), :]
+def end_kernel(where_ref, sum_ref, over_ref):
+    over_ref[...] = sum_ref[pl.ds(pl.multiple_of((where_ref[1] ^ 1) * 96, 96), 96), :]
 
 
 def total_of(refs):
@@ -272,25 +278,24 @@
     refs[-1][256:, :] = split_lines(lines)
 
 
-def last_kernel(where_ref, mine_ref, other_ref, *refs):
-    total = total_of((other_ref, *refs[:-3]))
-    refs[-3][...] = total[:128]
-    refs[-2][...] = total[128:]
-    refs[-1][...] = join_lines(mine_ref) + join_lines(other_ref)
-
-
-def add_kernel(where_ref, held_ref, got_ref, out_ref):
+def last_kernel(where_ref, mine_ref, other_ref, sum_ref, got_ref, *refs):
+    combined_ref, grad_ref, lines_ref, down_ref = refs[-4:]
+    total = total_of((other_ref, *refs[:-4]))
+    combined_ref[...] = total[:128]
+    grad_ref[...] = total[128:]
+    lines_ref[...] = join_lines(mine_ref) + join_lines(other_ref)
+    rows = pl.ds(pl.multiple_of(where_ref[1] * 96, 96), 96)
     for n, offset in enumerate(NEAR + FAR):
         at = slice(n * 256, (n + 1) * 256)
-        total = held_ref[:, at].astype(F32) + got_ref[:, at].astype(F32)
-        out_ref[:, pl.ds(shard_at(where_ref, offset), 256)] = total.astype(BF)
+        total = sum_ref[rows, at].astype(F32) + got_ref[:, at].astype(F32)
+        down_ref[:, pl.ds(shard_at(where_ref, offset), 256)] = total.astype(BF)
 
 
 def whole(shape):
     return pl.BlockSpec(shape, lambda i: (0,) * len(shape))
 
 
-def call(kernel, outs, micros, scalars, *operands, weights=(), wants=(), after=()):
+def call(kernel, outs, micros, scalars, *operands, weights=(), wants=(), more=(), loose=0, after=()):
     specs = [pl.BlockSpec(memory_space=pltpu.SMEM)] + [whole(v.shape) for v in operands]
     specs += [pl.BlockSpec(memory_space=pl.ANY) for _ in (*weights, *after)]
     first = 1 + len(operands) + len(weights)
@@ -313,8 +318,9 @@
         grid=(1,),
         out_shape=shapes,
         in_specs=specs,
-        out_specs=[whole(v.shape) for v in shapes],
-        scratch_shapes=scratch,
+        out_specs=[whole(v.shape) for v in shapes[: len(shapes) - loose]]
+        + [pl.BlockSpec(memory_space=pl.ANY)] * loose,
+        scratch_shapes=[*scratch, *more],
         compiler_params=pltpu.CompilerParams(vmem_limit_bytes=VMEM),
         cost_estimate=pl.CostEstimate(
             flops=micros * 10**9, bytes_accessed=micros * 3 * 10**6, transcendentals=0
@@ -365,6 +371,8 @@
         [dy_shape, act, act, (longer, BF), ((hidden_width, width), BF)],
         8, scalars, got_far, gate, up, d_hidden, dy_near,
         weights=(wg, wu, wd), wants=(FAR + (4,), FAR + (4,), FAR + NEAR),
+        more=(pltpu.VMEM((hidden_width, width), BF), pltpu.SemaphoreType.DMA((2 * QUAD,))),
+        loose=1,
     )
     home_far = over_ctx(back_far)
 
@@ -384,7 +392,7 @@
     )
     came_far = [swap(sums_far[d], "tp", d) for d in (1, 2, 3)]
     end = ((96, width), BF)
-    held, over = call(end_kernel, [end, end], 1, scalars, quarter, after=(sums_far[0],))
+    over = call(end_kernel, [end], 1, scalars, quarter, after=(sums_far[0],))
     ends = swap(over, "dp", 1)
     total_far = call(total_kernel, [longer], 1, scalars, sums_far[0], *came_far, after=(over,))
     from_far = swap(total_far, "tp", 4)
@@ -394,11 +402,10 @@
     )
     came_near = [swap(sums_near[d], "tp", d) for d in (1, 2, 3)]
     flat = ((128, 256), BF)
-    combined, grad_tokens, lines = call(
-        last_kernel, [flat, flat, (ids_t.shape, F32)], 1,
-        scalars, total_far, from_far, sums_near[0], *came_near,
-    )
-    grad_down = call(add_kernel, [end], 2, scalars, held, ends)
+    combined, grad_tokens, lines, grad_down = call(
+        last_kernel, [flat, flat, (ids_t.shape, F32), end], 2,
+        scalars, total_far, from_far, quarter, ends, sums_near[0], *came_near,
+    )
     return combined, grad_tokens, lines.T, grad_down[None]
 
 

time: 238 us -> 236 us (level)
    pallas_call x11 -> x10, Pallas kernels: 40.4 us -> 38.6 us  [call(): pl.pallas_call(body, grid=(1,), out_shape=shapes, in_specs=specs, out_spe...]
  transfers between devices with their start and end apart: 19 -> 19, of which waited for: 8 -> 8; matrix products, arithmetic and copies ran while one was open for 0% -> 0% of each run, Pallas kernels for 11% -> 10%
where the time goes in v3:
time: 236 us; the launch traced here: 235 us
  waiting for transfers between devices  90.4 us (38%)
  starting transfers between devices  88.3 us (37%)
  Pallas kernels  38.6 us (16%)
  between operations  14.2 us (6%)
    ppermute x14, starting transfers between devices, swap(): return lax.ppermute(value, axis, [(i, i ^ bit) for i in range(size)])  65.3 us
    ppermute x14, waiting for transfers between devices, swap(): return lax.ppermute(value, axis, [(i, i ^ bit) for i in range(size)])  54.4 us
    pallas_call x10, Pallas kernels, call(): pl.pallas_call(body, grid=(1,), out_shape=shapes, in_specs=specs, out_spe...  38.6 us
    all_to_all x4, waiting for transfers between devices, over_ctx(): return lax.all_to_all(value, 'ctx', split_axis=0, concat_axis=0, tiled=True)  30.1 us
    all_to_all x4, starting transfers between devices, over_ctx(): return lax.all_to_all(value, 'ctx', split_axis=0, concat_axis=0, tiled=True)  23 us
    reduce_scatter x1, waiting for transfers between devices, shards(): lax.psum_scatter(partial, 'dp', scatter_dimension=0, axis_index_groups=[[...  5.79 us
  transfers between devices with their start and end apart: 19, of which 8 were waited for; matrix products, arithmetic and copies ran while one was open for 0% of the time, Pallas kernels for 10%

profile of v3, /device:TPU:1, one launch (start us, length us, event | category | flops | bytes accessed | tf_op | source)
XLA Modules:
  0.0 234.5 jit_solution(13729314251831779692)
XLA Ops:
  7.2 0.8 constant_dynamic-update-slice_fusion.1
  8.0 0.8 constant_dynamic-update-slice_fusion.refs_3_
  8.9 11.5 %collective-permute-start.2 = (bf16[256,256]{1,0:T(8,128)(2,1)S(1)}, bf16[256,256]{1,0:T(8,128)(2,1)S(1)}, u32[]{:S(2)}, u32[]{:S(2)}) collective-permute-start(bf16[256,256]{1,0:T(8,128)(2,1)S(1)} %constant_dynamic-update-slice_fusion.refs_3_), channel_id=1, source_target_pairs={{0,4},{1,5},{2,6},{3,7},{4,0},{5,1},{6,2},{7,3},{8,12},{9,13},{10,... | collective-permute-start | bytes 393224 | tf_op jit(solution)/shard_map/ppermute | solution.py:334
  20.3 5.8 %collective-permute-start.1 = (bf16[256,256]{1,0:T(8,128)(2,1)S(1)}, bf16[256,256]{1,0:T(8,128)(2,1)S(1)}, u32[]{:S(2)}, u32[]{:S(2)}) collective-permute-start(bf16[256,256]{1,0:T(8,128)(2,1)S(1)} %constant_dynamic-update-slice_fusion.refs_3_), channel_id=1, source_target_pairs={{0,2},{1,3},{2,0},{3,1},{4,6},{5,7},{6,4},{7,5},{8,10},{9,11},{10,... | collective-permute-start | bytes 393224 | tf_op jit(solution)/shard_map/ppermute | solution.py:334
  26.1 4.0 %collective-permute-start = (bf16[256,256]{1,0:T(8,128)(2,1)S(1)}, bf16[256,256]{1,0:T(8,128)(2,1)S(1)}, u32[]{:S(2)}, u32[]{:S(2)}) collective-permute-start(bf16[256,256]{1,0:T(8,128)(2,1)S(1)} %constant_dynamic-update-slice_fusion.refs_3_), channel_id=1, source_target_pairs={{0,1},{1,0},{2,3},{3,2},{4,5},{5,4},{6,7},{7,6},{8,9},{9,8},{10,11... | collective-permute-start | bytes 393224 | tf_op jit(solution)/shard_map/ppermute | solution.py:334
  30.2 0.6 pad_add_fusion.refs_0_
  30.8 0.0 collective-permute-done.2.refs_6_
  30.8 0.0 collective-permute-done.1.refs_5_
  30.8 5.3 %collective-permute-done.refs_4_ = bf16[256,256]{1,0:T(8,128)(2,1)S(1)} collective-permute-done((bf16[256,256]{1,0:T(8,128)(2,1)S(1)}, bf16[256,256]{1,0:T(8,128)(2,1)S(1)}, u32[]{:S(2)}, u32[]{:S(2)}) %collective-permute-start) | collective-permute-done | bytes 131104 | tf_op jit(solution)/shard_map/ppermute | solution.py:334
  36.1 0.6 copy-done.3
  36.7 2.7 %shard_map.102 = (bf16[16,80,256]{2,1,0:T(8,128)(2,1)}, bf16[512,256]{1,0:T(8,128)(2,1)}) custom-call(s32[2]{0:T(128)} %pad_add_fusion.refs_0_, s32[8,128]{1,0:T(8,128)} %bitcast.17, f32[8,128]{1,0:T(8,128)} %bitcast.21, bf16[256,256]{1,0:T(8,128)(2,1)} %copy-done, bf16[256,256]{1,0:T(8,128)(2,1)} %copy-done.3, bf16[256,256]{1,0:T(8,128)(2,1)} %copy-done.2, ...), custom_call_target="tpu_custom_call" | custom-call | flops 4000000000 | bytes 12000000 | tf_op jit(solution)/shard_map/pallas_call | solution.py:316
  39.4 7.0 %all-to-all-start.1 = ((bf16[16,80,256]{2,1,0:T(8,128)(2,1)}), bf16[16,80,256]{2,1,0:T(8,128)(2,1)}, u32[]{:S(2)}, u32[]{:S(2)}) async-start(bf16[16,80,256]{2,1,0:T(8,128)(2,1)} %get-tuple-element.28.refs_6_), calls=%async_computation.1 | async-start | bytes 1310720 | tf_op jit(solution)/shard_map/all_to_all | solution.py:338
  46.5 5.2 %collective-permute-start.3 = (bf16[512,256]{1,0:T(8,128)(2,1)}, bf16[512,256]{1,0:T(8,128)(2,1)}, u32[]{:S(2)}, u32[]{:S(2)}) collective-permute-start(bf16[512,256]{1,0:T(8,128)(2,1)} %get-tuple-element.27), channel_id=1, source_target_pairs={{0,3},{1,2},{2,1},{3,0},{4,7},{5,6},{6,5},{7,4},{8,11},{9,10},{10,... | collective-permute-start | bytes 786440 | tf_op jit(solution)/shard_map/ppermute | solution.py:334
  51.7 1.9 collective-permute-start.5
  53.6 2.2 collective-permute-start.4
  55.8 12.9 %collective-permute-done.5.refs_5_ = bf16[256,256]{1,0:T(8,128)(2,1)} collective-permute-done((bf16[256,256]{1,0:T(8,128)(2,1)}, bf16[256,256]{1,0:T(8,128)(2,1)}, u32[]{:S(2)}, u32[]{:S(2)}) %collective-permute-start.5) | collective-permute-done | bytes 131104 | tf_op jit(solution)/shard_map/ppermute | solution.py:334
  68.7 0.0 collective-permute-done.4.refs_4_
  68.7 0.0 collective-permute-done.3.refs_3_
  68.7 2.6 %shard_map.103.refs_5_ = bf16[16,80,256]{2,1,0:T(8,128)(2,1)} custom-call(s32[2]{0:T(128)} %pad_add_fusion.refs_0_, s32[8,128]{1,0:T(8,128)} %bitcast.18, f32[8,128]{1,0:T(8,128)} %bitcast.22, bf16[512,256]{1,0:T(8,128)(2,1)} %collective-permute-done.3.refs_3_, bf16[256,256]{1,0:T(8,128)(2,1)} %collective-permute-done.4.refs_4_, ...), custom_call_target="tpu_custom_call" | custom-call | flops 4000000000 | bytes 12000000 | tf_op jit(solution)/shard_map/pallas_call | solution.py:316
  71.3 7.6 %all-to-all-start = ((bf16[16,80,256]{2,1,0:T(8,128)(2,1)}), bf16[16,80,256]{2,1,0:T(8,128)(2,1)}, u32[]{:S(2)}, u32[]{:S(2)}) async-start(bf16[16,80,256]{2,1,0:T(8,128)(2,1)} %shard_map.103.refs_5_), calls=%async_computation | async-start | bytes 1310720 | tf_op jit(solution)/shard_map/all_to_all | solution.py:338
  78.9 0.0 reduce-scatter.2.cloned.1.call-start
  79.0 5.6 %shard_map.104 = (f32[160,768]{1,0:T(8,128)}, f32[160,768]{1,0:T(8,128)}, f32[160,768]{1,0:T(8,128)}, bf16[4,160,256]{2,1,0:T(8,128)(2,1)}) custom-call(s32[2]{0:T(128)} %pad_add_fusion.refs_0_, bf16[16,80,256]{2,1,0:T(8,128)(2,1)} %all-to-all-done.1.refs_1_, bf16[2048,768]{1,0:T(8,128)(2,1)} %bitcast.11, bf16[2048,768]{1,0:T(8,128)(2,1)} %bitcast.14, ...), custom_call_target="tpu_custom_call" | custom-call | flops 5000000000 | bytes 15000000 | tf_op jit(solution)/shard_map/pallas_call | solution.py:316
  84.6 14.5 %all-to-all-done.refs_1_ = bf16[16,80,256]{2,1,0:T(8,128)(2,1)} async-done(((bf16[16,80,256]{2,1,0:T(8,128)(2,1)}), bf16[16,80,256]{2,1,0:T(8,128)(2,1)}, u32[]{:S(2)}, u32[]{:S(2)}) %all-to-all-start) | async-done | bytes 655392 | tf_op jit(solution)/shard_map/all_to_all | solution.py:338
  99.1 10.3 %shard_map.105 = (bf16[4,160,256]{2,1,0:T(8,128)(2,1)}, bf16[160,768]{1,0:T(8,128)(2,1)}, bf16[160,768]{1,0:T(8,128)(2,1)}, bf16[16,96,256]{2,1,0:T(8,128)(2,1)}, bf16[768,2048]{1,0:T(8,128)(2,1)}) custom-call(s32[2]{0:T(128)} %pad_add_fusion.refs_0_, bf16[16,80,256]{2,1,0:T(8,128)(2,1)} %all-to-all-done.refs_1_, f32[160,768]{1,0:T(8,128)} %get-tuple-element.29.refs_2_, ...), custom_call_target="tpu_custom_call" | custom-call | flops 8000000000 | bytes 24000000 | tf_op jit(solution)/shard_map/pallas_call | solution.py:316
  109.4 0.0 reduce-scatter.2.cloned.1.call-update
  109.4 4.2 %all-to-all-start.2 = ((bf16[16,96,256]{2,1,0:T(8,128)(2,1)}), bf16[16,96,256]{2,1,0:T(8,128)(2,1)}, u32[]{:S(2)}, u32[]{:S(2)}) async-start(bf16[16,96,256]{2,1,0:T(8,128)(2,1)} %get-tuple-element.33), calls=%async_computation.2 | async-start | bytes 1572864 | tf_op jit(solution)/shard_map/all_to_all | solution.py:338
  113.6 5.9 %shard_map.106.refs_4_ = bf16[16,80,256]{2,1,0:T(8,128)(2,1)} custom-call(s32[2]{0:T(128)} %pad_add_fusion.refs_0_, bf16[4,160,256]{2,1,0:T(8,128)(2,1)} %get-tuple-element.34.refs_1_, bf16[160,768]{1,0:T(8,128)(2,1)} %get-tuple-element.35.refs_2_, bf16[160,768]{1,0:T(8,128)(2,1)} %get-tuple-element.36.refs_3_, bf16[2048,768]{1,0:T(8,128)(2,1)} %bitcast.13, ...), custom_call_target="tpu_custom_call" | custom-call | flops 4000000000 | bytes 12000000 | tf_op jit(solution)/shard_map/pallas_call | solution.py:316
  119.5 15.7 %all-to-all-done.2.refs_3_ = bf16[16,96,256]{2,1,0:T(8,128)(2,1)} async-done(((bf16[16,96,256]{2,1,0:T(8,128)(2,1)}), bf16[16,96,256]{2,1,0:T(8,128)(2,1)}, u32[]{:S(2)}, u32[]{:S(2)}) %all-to-all-start.2) | async-done | bytes 786464 | tf_op jit(solution)/shard_map/all_to_all | solution.py:338
  135.2 4.2 %all-to-all-start.3 = ((bf16[16,80,256]{2,1,0:T(8,128)(2,1)}), bf16[16,80,256]{2,1,0:T(8,128)(2,1)}, u32[]{:S(2)}, u32[]{:S(2)}) async-start(bf16[16,80,256]{2,1,0:T(8,128)(2,1)} %shard_map.106.refs_4_), calls=%async_computation.4 | async-start | bytes 1310720 | tf_op jit(solution)/shard_map/all_to_all | solution.py:338
  139.4 2.7 %shard_map.107 = (bf16[272,256]{1,0:T(8,128)(2,1)}, bf16[272,256]{1,0:T(8,128)(2,1)}, bf16[272,256]{1,0:T(8,128)(2,1)}, bf16[272,256]{1,0:T(8,128)(2,1)}) custom-call(s32[2]{0:T(128)} %pad_add_fusion.refs_0_, s32[8,128]{1,0:T(8,128)} %bitcast.19, f32[8,128]{1,0:T(8,128)} %bitcast.23, bf16[16,96,256]{2,1,0:T(8,128)(2,1)} %all-to-all-done.2.refs_3_, ...), custom_call_target="tpu_custom_call" | custom-call | flops 4000000000 | bytes 12000000 | tf_op jit(solution)/shard_map/pallas_call | solution.py:316
  142.1 1.9 collective-permute-start.6
  144.0 4.5 %collective-permute-start.7 = (bf16[272,256]{1,0:T(8,128)(2,1)}, bf16[272,256]{1,0:T(8,128)(2,1)}, u32[]{:S(2)}, u32[]{:S(2)}) collective-permute-start(bf16[272,256]{1,0:T(8,128)(2,1)} %get-tuple-element.39), channel_id=1, source_target_pairs={{0,2},{1,3},{2,0},{3,1},{4,6},{5,7},{6,4},{7,5},{8,10},{9,11},{10,... | collective-permute-start | bytes 417800 | tf_op jit(solution)/shard_map/ppermute | solution.py:334
  148.6 2.8 %collective-permute-start.8 = (bf16[272,256]{1,0:T(8,128)(2,1)}, bf16[272,256]{1,0:T(8,128)(2,1)}, u32[]{:S(2)}, u32[]{:S(2)}) collective-permute-start(bf16[272,256]{1,0:T(8,128)(2,1)} %get-tuple-element.40), channel_id=1, source_target_pairs={{0,3},{1,2},{2,1},{3,0},{4,7},{5,6},{6,5},{7,4},{8,11},{9,10},{10,... | collective-permute-start | bytes 417800 | tf_op jit(solution)/shard_map/ppermute | solution.py:334
  151.4 5.8 %reduce-scatter.2.cloned.1.call-done.refs_1_.refs_3_ = bf16[192,2048]{1,0:T(8,128)(2,1)} async-done(((bf16[768,2048]{1,0:T(8,128)(2,1)}), bf16[192,2048]{1,0:T(8,128)(2,1)}) %reduce-scatter.2.cloned.1.call-update) | async-done | bytes 786448 | tf_op jit(solution)/shard_map/reduce_scatter | solution.py:379
  157.2 1.9 shard_map.108.refs_5_
  159.1 13.2 %collective-permute-start.10 = (bf16[96,2048]{1,0:T(8,128)(2,1)}, bf16[96,2048]{1,0:T(8,128)(2,1)}, u32[]{:S(2)}, u32[]{:S(2)}) collective-permute-start(bf16[96,2048]{1,0:T(8,128)(2,1)} %shard_map.108.refs_5_), channel_id=1, source_target_pairs={{0,128},{128,0},{256,384},{384,256},{512,640},{640,512},{768,896},... | collective-permute-start | bytes 1179656 | tf_op jit(solution)/shard_map/ppermute | solution.py:334
  172.4 0.0 collective-permute-done.6.refs_2_
  172.4 0.0 collective-permute-done.7.refs_3_
  172.4 1.9 shard_map.109.refs_4_.refs_1_
  174.3 2.9 %collective-permute-start.9 = (bf16[272,256]{1,0:T(8,128)(2,1)}, bf16[272,256]{1,0:T(8,128)(2,1)}, u32[]{:S(2)}, u32[]{:S(2)}) collective-permute-start(bf16[272,256]{1,0:T(8,128)(2,1)} %shard_map.109.refs_4_.refs_1_), channel_id=1, source_target_pairs={{0,4},{1,5},{2,6},{3,7},{4,0},{5,1},{6,2},{7,3},{8,12},{9,13},{10,... | collective-permute-start | bytes 417800 | tf_op jit(solution)/shard_map/ppermute | solution.py:334
  177.2 2.4 %shard_map.110 = (bf16[256,256]{1,0:T(8,128)(2,1)}, bf16[256,256]{1,0:T(8,128)(2,1)}, bf16[256,256]{1,0:T(8,128)(2,1)}, bf16[256,256]{1,0:T(8,128)(2,1)}) custom-call(s32[2]{0:T(128)} %pad_add_fusion.refs_0_, s32[8,128]{1,0:T(8,128)} %bitcast.20, f32[8,128]{1,0:T(8,128)} %bitcast.24, bf16[16,80,256]{2,1,0:T(8,128)(2,1)} %all-to-all-done.3.refs_3_, ...), custom_call_target="tpu_custom_call" | custom-call | flops 4000000000 | bytes 12000000 | tf_op jit(solution)/shard_map/pallas_call | solution.py:316
  179.7 2.4 %collective-permute-start.11 = (bf16[256,256]{1,0:T(8,128)(2,1)}, bf16[256,256]{1,0:T(8,128)(2,1)}, u32[]{:S(2)}, u32[]{:S(2)}) collective-permute-start(bf16[256,256]{1,0:T(8,128)(2,1)} %get-tuple-element.43), channel_id=1, source_target_pairs={{0,1},{1,0},{2,3},{3,2},{4,5},{5,4},{6,7},{7,6},{8,9},{9,8},{10,11... | collective-permute-start | bytes 393224 | tf_op jit(solution)/shard_map/ppermute | solution.py:334
  182.0 2.6 %collective-permute-start.12 = (bf16[256,256]{1,0:T(8,128)(2,1)}, bf16[256,256]{1,0:T(8,128)(2,1)}, u32[]{:S(2)}, u32[]{:S(2)}) collective-permute-start(bf16[256,256]{1,0:T(8,128)(2,1)} %get-tuple-element.44), channel_id=1, source_target_pairs={{0,2},{1,3},{2,0},{3,1},{4,6},{5,7},{6,4},{7,5},{8,10},{9,11},{10,... | collective-permute-start | bytes 393224 | tf_op jit(solution)/shard_map/ppermute | solution.py:334
  184.6 4.3 %collective-permute-start.13 = (bf16[256,256]{1,0:T(8,128)(2,1)}, bf16[256,256]{1,0:T(8,128)(2,1)}, u32[]{:S(2)}, u32[]{:S(2)}) collective-permute-start(bf16[256,256]{1,0:T(8,128)(2,1)} %get-tuple-element.45), channel_id=1, source_target_pairs={{0,3},{1,2},{2,1},{3,0},{4,7},{5,6},{6,5},{7,4},{8,11},{9,10},{10,... | collective-permute-start | bytes 393224 | tf_op jit(solution)/shard_map/ppermute | solution.py:334
  189.0 23.2 %collective-permute-done.11.refs_6_ = bf16[256,256]{1,0:T(8,128)(2,1)} collective-permute-done((bf16[256,256]{1,0:T(8,128)(2,1)}, bf16[256,256]{1,0:T(8,128)(2,1)}, u32[]{:S(2)}, u32[]{:S(2)}) %collective-permute-start.11) | collective-permute-done | bytes 131104 | tf_op jit(solution)/shard_map/ppermute | solution.py:334
  212.1 0.7 collective-permute-done.12.refs_7_
  212.9 12.3 %collective-permute-done.13.refs_8_ = bf16[256,256]{1,0:T(8,128)(2,1)} collective-permute-done((bf16[256,256]{1,0:T(8,128)(2,1)}, bf16[256,256]{1,0:T(8,128)(2,1)}, u32[]{:S(2)}, u32[]{:S(2)}) %collective-permute-start.13) | collective-permute-done | bytes 131104 | tf_op jit(solution)/shard_map/ppermute | solution.py:334
  225.2 2.4 %shard_map.111 = (bf16[128,256]{1,0:T(8,128)(2,1)}, bf16[128,256]{1,0:T(8,128)(2,1)}, f32[8,128]{1,0:T(8,128)}, bf16[96,2048]{1,0:T(8,128)(2,1)}) custom-call(s32[2]{0:T(128)} %pad_add_fusion.refs_0_, bf16[272,256]{1,0:T(8,128)(2,1)} %shard_map.109.refs_4_.refs_1_, bf16[272,256]{1,0:T(8,128)(2,1)} %collective-permute-done.9.refs_2_, ...), custom_call_target="tpu_custom_call" | custom-call | flops 2000000000 | bytes 6000000 | tf_op jit(solution)/shard_map/pallas_call | solution.py:316
  (12 shorter events, 0.0 us)
Async XLA Ops:
  8.9 17.3 %copy-start = (bf16[256,256]{1,0:T(8,128)(2,1)}, bf16[256,256]{1,0:T(8,128)(2,1)S(1)}, u32[]{:S(2)}) copy-start(bf16[256,256]{1,0:T(8,128)(2,1)S(1)} %constant_dynamic-update-slice_fusion.refs_3_) | copy-start | bytes 393220
  8.9 22.0 %collective-permute-start.2 = (bf16[256,256]{1,0:T(8,128)(2,1)S(1)}, bf16[256,256]{1,0:T(8,128)(2,1)S(1)}, u32[]{:S(2)}, u32[]{:S(2)}) collective-permute-start(bf16[256,256]{1,0:T(8,128)(2,1)S(1)} %constant_dynamic-update-slice_fusion.refs_3_), channel_id=1, source_target_pairs={{0,4},{1,5},{2,6},{3,7},{4,0},{5,1},{6,2},{7,3},{8,12},{9,13},{10,... | collective-permute-start | bytes 393224 | tf_op jit(solution)/shard_map/ppermute | solution.py:334
  20.3 10.5 %collective-permute-start.1 = (bf16[256,256]{1,0:T(8,128)(2,1)S(1)}, bf16[256,256]{1,0:T(8,128)(2,1)S(1)}, u32[]{:S(2)}, u32[]{:S(2)}) collective-permute-start(bf16[256,256]{1,0:T(8,128)(2,1)S(1)} %constant_dynamic-update-slice_fusion.refs_3_), channel_id=1, source_target_pairs={{0,2},{1,3},{2,0},{3,1},{4,6},{5,7},{6,4},{7,5},{8,10},{9,11},{10,... | collective-permute-start | bytes 393224 | tf_op jit(solution)/shard_map/ppermute | solution.py:334
  26.1 9.9 %collective-permute-start = (bf16[256,256]{1,0:T(8,128)(2,1)S(1)}, bf16[256,256]{1,0:T(8,128)(2,1)S(1)}, u32[]{:S(2)}, u32[]{:S(2)}) collective-permute-start(bf16[256,256]{1,0:T(8,128)(2,1)S(1)} %constant_dynamic-update-slice_fusion.refs_3_), channel_id=1, source_target_pairs={{0,1},{1,0},{2,3},{3,2},{4,5},{5,4},{6,7},{7,6},{8,9},{9,8},{10,11... | collective-permute-start | bytes 393224 | tf_op jit(solution)/shard_map/ppermute | solution.py:334
  30.8 5.3 %copy-start.1 = (bf16[256,256]{1,0:T(8,128)(2,1)}, bf16[256,256]{1,0:T(8,128)(2,1)S(1)}, u32[]{:S(2)}) copy-start(bf16[256,256]{1,0:T(8,128)(2,1)S(1)} %collective-permute-done.2.refs_6_) | copy-start | bytes 393220
  30.8 5.3 %copy-start.2 = (bf16[256,256]{1,0:T(8,128)(2,1)}, bf16[256,256]{1,0:T(8,128)(2,1)S(1)}, u32[]{:S(2)}) copy-start(bf16[256,256]{1,0:T(8,128)(2,1)S(1)} %collective-permute-done.1.refs_5_) | copy-start | bytes 393220
  36.1 0.7 copy-start.3
  39.4 31.9 %all-to-all-start.1 = ((bf16[16,80,256]{2,1,0:T(8,128)(2,1)}), bf16[16,80,256]{2,1,0:T(8,128)(2,1)}, u32[]{:S(2)}, u32[]{:S(2)}) async-start(bf16[16,80,256]{2,1,0:T(8,128)(2,1)} %get-tuple-element.28.refs_6_), calls=%async_computation.1 | async-start | bytes 1310720 | tf_op jit(solution)/shard_map/all_to_all | solution.py:338
  46.5 22.3 %collective-permute-start.3 = (bf16[512,256]{1,0:T(8,128)(2,1)}, bf16[512,256]{1,0:T(8,128)(2,1)}, u32[]{:S(2)}, u32[]{:S(2)}) collective-permute-start(bf16[512,256]{1,0:T(8,128)(2,1)} %get-tuple-element.27), channel_id=1, source_target_pairs={{0,3},{1,2},{2,1},{3,0},{4,7},{5,6},{6,5},{7,4},{8,11},{9,10},{10,... | collective-permute-start | bytes 786440 | tf_op jit(solution)/shard_map/ppermute | solution.py:334
  51.7 17.0 %collective-permute-start.5 = (bf16[256,256]{1,0:T(8,128)(2,1)}, bf16[256,256]{1,0:T(8,128)(2,1)}, u32[]{:S(2)}, u32[]{:S(2)}) collective-permute-start(bf16[256,256]{1,0:T(8,128)(2,1)} %copy-done.1), channel_id=1, source_target_pairs={{0,2},{1,3},{2,0},{3,1},{4,6},{5,7},{6,4},{7,5},{8,10},{9,11},{10,... | collective-permute-start | bytes 393224 | tf_op jit(solution)/shard_map/ppermute | solution.py:334
  53.6 15.1 %collective-permute-start.4 = (bf16[256,256]{1,0:T(8,128)(2,1)}, bf16[256,256]{1,0:T(8,128)(2,1)}, u32[]{:S(2)}, u32[]{:S(2)}) collective-permute-start(bf16[256,256]{1,0:T(8,128)(2,1)} %copy-done.1), channel_id=1, source_target_pairs={{0,1},{1,0},{2,3},{3,2},{4,5},{5,4},{6,7},{7,6},{8,9},{9,8},{10,11... | collective-permute-start | bytes 393224 | tf_op jit(solution)/shard_map/ppermute | solution.py:334
  71.3 27.7 %all-to-all-start = ((bf16[16,80,256]{2,1,0:T(8,128)(2,1)}), bf16[16,80,256]{2,1,0:T(8,128)(2,1)}, u32[]{:S(2)}, u32[]{:S(2)}) async-start(bf16[16,80,256]{2,1,0:T(8,128)(2,1)} %shard_map.103.refs_5_), calls=%async_computation | async-start | bytes 1310720 | tf_op jit(solution)/shard_map/all_to_all | solution.py:338
  78.9 78.3 %reduce-scatter.2.cloned.1.call-start = ((), (), s32[]{:S(2)}) async-start(), calls=%async_computation.5 | async-start | bytes 3932160 | tf_op jit(solution)/shard_map/reduce_scatter | solution.py:379
  109.4 25.8 %all-to-all-start.2 = ((bf16[16,96,256]{2,1,0:T(8,128)(2,1)}), bf16[16,96,256]{2,1,0:T(8,128)(2,1)}, u32[]{:S(2)}, u32[]{:S(2)}) async-start(bf16[16,96,256]{2,1,0:T(8,128)(2,1)} %get-tuple-element.33), calls=%async_computation.2 | async-start | bytes 1572864 | tf_op jit(solution)/shard_map/all_to_all | solution.py:338
  135.2 42.0 %all-to-all-start.3 = ((bf16[16,80,256]{2,1,0:T(8,128)(2,1)}), bf16[16,80,256]{2,1,0:T(8,128)(2,1)}, u32[]{:S(2)}, u32[]{:S(2)}) async-start(bf16[16,80,256]{2,1,0:T(8,128)(2,1)} %shard_map.106.refs_4_), calls=%async_computation.4 | async-start | bytes 1310720 | tf_op jit(solution)/shard_map/all_to_all | solution.py:338
  142.1 30.3 %collective-permute-start.6 = (bf16[272,256]{1,0:T(8,128)(2,1)}, bf16[272,256]{1,0:T(8,128)(2,1)}, u32[]{:S(2)}, u32[]{:S(2)}) collective-permute-start(bf16[272,256]{1,0:T(8,128)(2,1)} %get-tuple-element.38), channel_id=1, source_target_pairs={{0,1},{1,0},{2,3},{3,2},{4,5},{5,4},{6,7},{7,6},{8,9},{9,8},{10,11... | collective-permute-start | bytes 417800 | tf_op jit(solution)/shard_map/ppermute | solution.py:334
  144.0 28.4 %collective-permute-start.7 = (bf16[272,256]{1,0:T(8,128)(2,1)}, bf16[272,256]{1,0:T(8,128)(2,1)}, u32[]{:S(2)}, u32[]{:S(2)}) collective-permute-start(bf16[272,256]{1,0:T(8,128)(2,1)} %get-tuple-element.39), channel_id=1, source_target_pairs={{0,2},{1,3},{2,0},{3,1},{4,6},{5,7},{6,4},{7,5},{8,10},{9,11},{10,... | collective-permute-start | bytes 417800 | tf_op jit(solution)/shard_map/ppermute | solution.py:334
  148.6 23.8 %collective-permute-start.8 = (bf16[272,256]{1,0:T(8,128)(2,1)}, bf16[272,256]{1,0:T(8,128)(2,1)}, u32[]{:S(2)}, u32[]{:S(2)}) collective-permute-start(bf16[272,256]{1,0:T(8,128)(2,1)} %get-tuple-element.40), channel_id=1, source_target_pairs={{0,3},{1,2},{2,1},{3,0},{4,7},{5,6},{6,5},{7,4},{8,11},{9,10},{10,... | collective-permute-start | bytes 417800 | tf_op jit(solution)/shard_map/ppermute | solution.py:334
  159.1 66.1 %collective-permute-start.10 = (bf16[96,2048]{1,0:T(8,128)(2,1)}, bf16[96,2048]{1,0:T(8,128)(2,1)}, u32[]{:S(2)}, u32[]{:S(2)}) collective-permute-start(bf16[96,2048]{1,0:T(8,128)(2,1)} %shard_map.108.refs_5_), channel_id=1, source_target_pairs={{0,128},{128,0},{256,384},{384,256},{512,640},{640,512},{768,896},... | collective-permute-start | bytes 1179656 | tf_op jit(solution)/shard_map/ppermute | solution.py:334
  174.3 50.9 %collective-permute-start.9 = (bf16[272,256]{1,0:T(8,128)(2,1)}, bf16[272,256]{1,0:T(8,128)(2,1)}, u32[]{:S(2)}, u32[]{:S(2)}) collective-permute-start(bf16[272,256]{1,0:T(8,128)(2,1)} %shard_map.109.refs_4_.refs_1_), channel_id=1, source_target_pairs={{0,4},{1,5},{2,6},{3,7},{4,0},{5,1},{6,2},{7,3},{8,12},{9,13},{10,... | collective-permute-start | bytes 417800 | tf_op jit(solution)/shard_map/ppermute | solution.py:334
  179.7 32.5 %collective-permute-start.11 = (bf16[256,256]{1,0:T(8,128)(2,1)}, bf16[256,256]{1,0:T(8,128)(2,1)}, u32[]{:S(2)}, u32[]{:S(2)}) collective-permute-start(bf16[256,256]{1,0:T(8,128)(2,1)} %get-tuple-element.43), channel_id=1, source_target_pairs={{0,1},{1,0},{2,3},{3,2},{4,5},{5,4},{6,7},{7,6},{8,9},{9,8},{10,11... | collective-permute-start | bytes 393224 | tf_op jit(solution)/shard_map/ppermute | solution.py:334
  182.0 30.8 %collective-permute-start.12 = (bf16[256,256]{1,0:T(8,128)(2,1)}, bf16[256,256]{1,0:T(8,128)(2,1)}, u32[]{:S(2)}, u32[]{:S(2)}) collective-permute-start(bf16[256,256]{1,0:T(8,128)(2,1)} %get-tuple-element.44), channel_id=1, source_target_pairs={{0,2},{1,3},{2,0},{3,1},{4,6},{5,7},{6,4},{7,5},{8,10},{9,11},{10,... | collective-permute-start | bytes 393224 | tf_op jit(solution)/shard_map/ppermute | solution.py:334
  184.6 40.6 %collective-permute-start.13 = (bf16[256,256]{1,0:T(8,128)(2,1)}, bf16[256,256]{1,0:T(8,128)(2,1)}, u32[]{:S(2)}, u32[]{:S(2)}) collective-permute-start(bf16[256,256]{1,0:T(8,128)(2,1)} %get-tuple-element.45), channel_id=1, source_target_pairs={{0,3},{1,2},{2,1},{3,0},{4,7},{5,6},{6,5},{7,4},{8,11},{9,10},{10,... | collective-permute-start | bytes 393224 | tf_op jit(solution)/shard_map/ppermute | solution.py:334
Sparse Core Ops, SparseCore 0:
  109.5 47.6 reduce-scatter.1

commit v4 on v3

--- a/solution.py
+++ b/solution.py
@@ -144,11 +144,12 @@
     return gate, up, d_hidden, dys
 
 
-def outward(outs, d_gate, d_up, offsets, get, send_ref):
+def outward(hidden, d_gate, d_up, offsets, get, send_ref):
     rest = []
     for shard, offset in enumerate(offsets):
+        out = dot(hidden, get(2, offset))
         dx = dot_nt(d_gate, get(0, offset)) + dot_nt(d_up, get(1, offset))
-        rest += fold(send_ref, shard, outs[shard], dx)
+        rest += fold(send_ref, shard, out, dx)
     fold_rest(send_ref, rest)
 
 
@@ -171,7 +172,7 @@
 
 def far_kernel(wants, where_ref, recv_ref, gate_ref, up_ref, dh_ref, near_ref, *refs):
     weights, outs, held, sems, block, ends = refs[:3], refs[3:8], refs[8:11], *refs[11:14]
-    home_ref, dgate_ref, dup_ref, send_ref, partial_ref = outs
+    hidden_ref, dgate_ref, dup_ref, send_ref, partial_ref = outs
     get = fetch(where_ref, wants, weights, held, sems)
     gate, up, d_hidden, dys = inward(
         recv_ref, FAR, get, (gate_ref[...], up_ref[...], dh_ref[...])
@@ -181,6 +182,7 @@
     hidden = hidden32.astype(BF)
     d_gate = (d_hidden * up * s * (1.0 + gate * (1.0 - s))).astype(BF)
     d_up = (d_hidden * gate * s).astype(BF)
+    hidden_ref[...] = hidden
     dgate_ref[...] = d_gate
     dup_ref[...] = d_up
     dys = dict(zip(NEAR + FAR, [near_ref[shard] for shard in range(QUAD)] + dys))
@@ -192,15 +194,8 @@
         copy = pltpu.make_async_copy(block.at[:, at], partial_ref.at[:, at], ends.at[n])
         copy.start()
         leaving.append(copy)
-    made = {offset: dot(hidden, get(2, offset)) for offset in FAR + NEAR}
-    outward([made[offset] for offset in FIRST], d_gate, d_up, FIRST, get, send_ref)
-    get(0, FAR[0]), get(1, FAR[0])
-    for shard, offset in enumerate(LAST):
-        home_ref[shard] = made[offset].astype(BF)
-    dots = jnp.zeros((gate.shape[0], 1), F32)
-    for offset in FAR + NEAR:
-        terms = made[offset].astype(BF).astype(F32) * dys[offset].astype(F32)
-        dots = dots + jnp.sum(terms, axis=1, keepdims=True)
+    outward(hidden, d_gate, d_up, FIRST, get, send_ref)
+    dots = jnp.sum(hidden.astype(F32) * d_hidden, axis=1, keepdims=True)
     high = dots.astype(BF).astype(F32)
     terms = jnp.where(iota((dots.shape[0], 256), 1) < 128, high, dots - high)
     tail = dot(tail_pick(True), terms[MAIN * 16 :].astype(BF))
@@ -210,11 +205,10 @@
         copy.wait()
 
 
-def back_kernel(wants, where_ref, home_ref, dgate_ref, dup_ref, *refs):
-    weights, send_ref, held, sems = refs[:2], refs[2], refs[3:5], refs[5]
+def back_kernel(wants, where_ref, hidden_ref, dgate_ref, dup_ref, *refs):
+    weights, send_ref, held, sems = refs[:3], refs[3], refs[4:7], refs[7]
     get = fetch(where_ref, wants, weights, held, sems)
-    outs = [home_ref[shard].astype(F32) for shard in range(QUAD)]
-    outward(outs, dgate_ref[...], dup_ref[...], LAST, get, send_ref)
+    outward(hidden_ref[...], dgate_ref[...], dup_ref[...], LAST, get, send_ref)
 
 
 def split_lines(lines):
@@ -366,11 +360,11 @@
         weights=(wg, wu, wd), wants=(NEAR,) * 3, after=(send_far,),
     )
     longer = (16, QUAD * 20 + 16, 256)
-    home, d_gate, d_up, back_far, partial = call(
+    hidden, d_gate, d_up, back_far, partial = call(
         far_kernel,
-        [dy_shape, act, act, (longer, BF), ((hidden_width, width), BF)],
+        [act, act, act, (longer, BF), ((hidden_width, width), BF)],
         8, scalars, got_far, gate, up, d_hidden, dy_near,
-        weights=(wg, wu, wd), wants=(FAR + (4,), FAR + (4,), FAR + NEAR),
+        weights=(wg, wu, wd), wants=(FAR + (4,),) * 3,
         more=(pltpu.VMEM((hidden_width, width), BF), pltpu.SemaphoreType.DMA((2 * QUAD,))),
         loose=1,
     )
@@ -380,8 +374,8 @@
         partial, "dp", scatter_dimension=0, axis_index_groups=[[0, 2, 4, 6], [1, 3, 5, 7]], tiled=True
     )
     back_near = call(
-        back_kernel, [(travel, BF)], 4, scalars, home, d_gate, d_up,
-        weights=(wg, wu), wants=(LAST, LAST),
+        back_kernel, [(travel, BF)], 4, scalars, hidden, d_gate, d_up,
+        weights=(wg, wu, wd), wants=(LAST,) * 3,
     )
     home_near = over_ctx(back_near)
 

time: 236 us -> 235 us (level)
  no operation moved by 1% of the time
where the time goes in v4:
time: 235 us; the launch traced here: 233 us
  waiting for transfers between devices  89.2 us (38%)
  starting transfers between devices  88.3 us (38%)
  Pallas kernels  38.7 us (16%)
  between operations  14.2 us (6%)
  local copies, waits for them, and re-layouts  2.35 us (1%)
    ppermute x14, starting transfers between devices, swap(): return lax.ppermute(value, axis, [(i, i ^ bit) for i in range(size)])  65.3 us
    ppermute x14, waiting for transfers between devices, swap(): return lax.ppermute(value, axis, [(i, i ^ bit) for i in range(size)])  54.4 us
    pallas_call x10, Pallas kernels, call(): pl.pallas_call(body, grid=(1,), out_shape=shapes, in_specs=specs, out_spe...  38.7 us
    all_to_all x4, waiting for transfers between devices, over_ctx(): return lax.all_to_all(value, 'ctx', split_axis=0, concat_axis=0, tiled=True)  29 us
    all_to_all x4, starting transfers between devices, over_ctx(): return lax.all_to_all(value, 'ctx', split_axis=0, concat_axis=0, tiled=True)  23 us
    reduce_scatter x1, waiting for transfers between devices, shards(): lax.psum_scatter(partial, 'dp', scatter_dimension=0, axis_index_groups=[[...  5.79 us
  transfers between devices with their start and end apart: 19, of which 8 were waited for; matrix products, arithmetic and copies ran while one was open for 0% of the time, Pallas kernels for 10%

profile of v4, /device:TPU:1, one launch (start us, length us, event | category | flops | bytes accessed | tf_op | source)
XLA Modules:
  0.0 233.4 jit_solution(7244495520774018203)
XLA Ops:
  7.2 0.8 constant_dynamic-update-slice_fusion.1
  8.0 0.8 constant_dynamic-update-slice_fusion.refs_3_
  8.9 11.5 %collective-permute-start.2 = (bf16[256,256]{1,0:T(8,128)(2,1)S(1)}, bf16[256,256]{1,0:T(8,128)(2,1)S(1)}, u32[]{:S(2)}, u32[]{:S(2)}) collective-permute-start(bf16[256,256]{1,0:T(8,128)(2,1)S(1)} %constant_dynamic-update-slice_fusion.refs_3_), channel_id=1, source_target_pairs={{0,4},{1,5},{2,6},{3,7},{4,0},{5,1},{6,2},{7,3},{8,12},{9,13},{10,... | collective-permute-start | bytes 393224 | tf_op jit(solution)/shard_map/ppermute | solution.py:328
  20.3 5.8 %collective-permute-start.1 = (bf16[256,256]{1,0:T(8,128)(2,1)S(1)}, bf16[256,256]{1,0:T(8,128)(2,1)S(1)}, u32[]{:S(2)}, u32[]{:S(2)}) collective-permute-start(bf16[256,256]{1,0:T(8,128)(2,1)S(1)} %constant_dynamic-update-slice_fusion.refs_3_), channel_id=1, source_target_pairs={{0,2},{1,3},{2,0},{3,1},{4,6},{5,7},{6,4},{7,5},{8,10},{9,11},{10,... | collective-permute-start | bytes 393224 | tf_op jit(solution)/shard_map/ppermute | solution.py:328
  26.1 4.0 %collective-permute-start = (bf16[256,256]{1,0:T(8,128)(2,1)S(1)}, bf16[256,256]{1,0:T(8,128)(2,1)S(1)}, u32[]{:S(2)}, u32[]{:S(2)}) collective-permute-start(bf16[256,256]{1,0:T(8,128)(2,1)S(1)} %constant_dynamic-update-slice_fusion.refs_3_), channel_id=1, source_target_pairs={{0,1},{1,0},{2,3},{3,2},{4,5},{5,4},{6,7},{7,6},{8,9},{9,8},{10,11... | collective-permute-start | bytes 393224 | tf_op jit(solution)/shard_map/ppermute | solution.py:328
  30.2 0.7 pad_add_fusion.refs_0_
  30.8 5.3 %collective-permute-done.refs_4_ = bf16[256,256]{1,0:T(8,128)(2,1)S(1)} collective-permute-done((bf16[256,256]{1,0:T(8,128)(2,1)S(1)}, bf16[256,256]{1,0:T(8,128)(2,1)S(1)}, u32[]{:S(2)}, u32[]{:S(2)}) %collective-permute-start) | collective-permute-done | bytes 131104 | tf_op jit(solution)/shard_map/ppermute | solution.py:328
  36.1 0.6 copy-done.3
  36.7 2.7 %shard_map.102 = (bf16[16,80,256]{2,1,0:T(8,128)(2,1)}, bf16[512,256]{1,0:T(8,128)(2,1)}) custom-call(s32[2]{0:T(128)} %pad_add_fusion.refs_0_, s32[8,128]{1,0:T(8,128)} %bitcast.18, f32[8,128]{1,0:T(8,128)} %bitcast.22, bf16[256,256]{1,0:T(8,128)(2,1)} %copy-done, bf16[256,256]{1,0:T(8,128)(2,1)} %copy-done.3, bf16[256,256]{1,0:T(8,128)(2,1)} %copy-done.2, ...), custom_call_target="tpu_custom_call" | custom-call | flops 4000000000 | bytes 12000000 | tf_op jit(solution)/shard_map/pallas_call | solution.py:310
  39.4 7.0 %all-to-all-start.1 = ((bf16[16,80,256]{2,1,0:T(8,128)(2,1)}), bf16[16,80,256]{2,1,0:T(8,128)(2,1)}, u32[]{:S(2)}, u32[]{:S(2)}) async-start(bf16[16,80,256]{2,1,0:T(8,128)(2,1)} %get-tuple-element.28.refs_6_), calls=%async_computation.1 | async-start | bytes 1310720 | tf_op jit(solution)/shard_map/all_to_all | solution.py:332
  46.5 5.2 %collective-permute-start.3 = (bf16[512,256]{1,0:T(8,128)(2,1)}, bf16[512,256]{1,0:T(8,128)(2,1)}, u32[]{:S(2)}, u32[]{:S(2)}) collective-permute-start(bf16[512,256]{1,0:T(8,128)(2,1)} %get-tuple-element.27), channel_id=1, source_target_pairs={{0,3},{1,2},{2,1},{3,0},{4,7},{5,6},{6,5},{7,4},{8,11},{9,10},{10,... | collective-permute-start | bytes 786440 | tf_op jit(solution)/shard_map/ppermute | solution.py:328
  51.7 1.9 collective-permute-start.5
  53.6 2.2 collective-permute-start.4
  55.8 12.9 %collective-permute-done.5.refs_5_ = bf16[256,256]{1,0:T(8,128)(2,1)} collective-permute-done((bf16[256,256]{1,0:T(8,128)(2,1)}, bf16[256,256]{1,0:T(8,128)(2,1)}, u32[]{:S(2)}, u32[]{:S(2)}) %collective-permute-start.5) | collective-permute-done | bytes 131104 | tf_op jit(solution)/shard_map/ppermute | solution.py:328
  68.7 0.0 collective-permute-done.4.refs_4_
  68.7 0.0 collective-permute-done.3.refs_3_
  68.7 2.6 %shard_map.103.refs_5_ = bf16[16,80,256]{2,1,0:T(8,128)(2,1)} custom-call(s32[2]{0:T(128)} %pad_add_fusion.refs_0_, s32[8,128]{1,0:T(8,128)} %bitcast.19, f32[8,128]{1,0:T(8,128)} %bitcast.23, bf16[512,256]{1,0:T(8,128)(2,1)} %collective-permute-done.3.refs_3_, bf16[256,256]{1,0:T(8,128)(2,1)} %collective-permute-done.4.refs_4_, ...), custom_call_target="tpu_custom_call" | custom-call | flops 4000000000 | bytes 12000000 | tf_op jit(solution)/shard_map/pallas_call | solution.py:310
  71.3 7.6 %all-to-all-start = ((bf16[16,80,256]{2,1,0:T(8,128)(2,1)}), bf16[16,80,256]{2,1,0:T(8,128)(2,1)}, u32[]{:S(2)}, u32[]{:S(2)}) async-start(bf16[16,80,256]{2,1,0:T(8,128)(2,1)} %shard_map.103.refs_5_), calls=%async_computation | async-start | bytes 1310720 | tf_op jit(solution)/shard_map/all_to_all | solution.py:332
  78.9 0.0 reduce-scatter.2.cloned.1.call-start
  79.0 5.6 %shard_map.104 = (f32[160,768]{1,0:T(8,128)}, f32[160,768]{1,0:T(8,128)}, f32[160,768]{1,0:T(8,128)}, bf16[4,160,256]{2,1,0:T(8,128)(2,1)}) custom-call(s32[2]{0:T(128)} %pad_add_fusion.refs_0_, bf16[16,80,256]{2,1,0:T(8,128)(2,1)} %all-to-all-done.1.refs_1_, bf16[2048,768]{1,0:T(8,128)(2,1)} %bitcast.9, bf16[2048,768]{1,0:T(8,128)(2,1)} %bitcast.12, ...), custom_call_target="tpu_custom_call" | custom-call | flops 5000000000 | bytes 15000000 | tf_op jit(solution)/shard_map/pallas_call | solution.py:310
  84.6 14.5 %all-to-all-done.refs_1_ = bf16[16,80,256]{2,1,0:T(8,128)(2,1)} async-done(((bf16[16,80,256]{2,1,0:T(8,128)(2,1)}), bf16[16,80,256]{2,1,0:T(8,128)(2,1)}, u32[]{:S(2)}, u32[]{:S(2)}) %all-to-all-start) | async-done | bytes 655392 | tf_op jit(solution)/shard_map/all_to_all | solution.py:332
  99.1 9.2 %shard_map.105 = (bf16[160,768]{1,0:T(8,128)(2,1)}, bf16[160,768]{1,0:T(8,128)(2,1)}, bf16[160,768]{1,0:T(8,128)(2,1)}, bf16[16,96,256]{2,1,0:T(8,128)(2,1)}, bf16[768,2048]{1,0:T(8,128)(2,1)}) custom-call(s32[2]{0:T(128)} %pad_add_fusion.refs_0_, bf16[16,80,256]{2,1,0:T(8,128)(2,1)} %all-to-all-done.refs_1_, f32[160,768]{1,0:T(8,128)} %get-tuple-element.29.refs_2_, ...), custom_call_target="tpu_custom_call" | custom-call | flops 8000000000 | bytes 24000000 | tf_op jit(solution)/shard_map/pallas_call | solution.py:310
  108.3 0.0 reduce-scatter.2.cloned.1.call-update
  108.3 4.2 %all-to-all-start.2 = ((bf16[16,96,256]{2,1,0:T(8,128)(2,1)}), bf16[16,96,256]{2,1,0:T(8,128)(2,1)}, u32[]{:S(2)}, u32[]{:S(2)}) async-start(bf16[16,96,256]{2,1,0:T(8,128)(2,1)} %get-tuple-element.33), calls=%async_computation.2 | async-start | bytes 1572864 | tf_op jit(solution)/shard_map/all_to_all | solution.py:332
  112.5 7.1 %shard_map.106.refs_4_ = bf16[16,80,256]{2,1,0:T(8,128)(2,1)} custom-call(s32[2]{0:T(128)} %pad_add_fusion.refs_0_, bf16[160,768]{1,0:T(8,128)(2,1)} %get-tuple-element.34.refs_1_, bf16[160,768]{1,0:T(8,128)(2,1)} %get-tuple-element.35.refs_2_, bf16[160,768]{1,0:T(8,128)(2,1)} %get-tuple-element.36.refs_3_, bf16[2048,768]{1,0:T(8,128)(2,1)} %bitcast.11, ...), custom_call_target="tpu_custom_call" | custom-call | flops 4000000000 | bytes 12000000 | tf_op jit(solution)/shard_map/pallas_call | solution.py:310
  119.6 14.5 %all-to-all-done.2.refs_3_ = bf16[16,96,256]{2,1,0:T(8,128)(2,1)} async-done(((bf16[16,96,256]{2,1,0:T(8,128)(2,1)}), bf16[16,96,256]{2,1,0:T(8,128)(2,1)}, u32[]{:S(2)}, u32[]{:S(2)}) %all-to-all-start.2) | async-done | bytes 786464 | tf_op jit(solution)/shard_map/all_to_all | solution.py:332
  134.1 4.2 %all-to-all-start.3 = ((bf16[16,80,256]{2,1,0:T(8,128)(2,1)}), bf16[16,80,256]{2,1,0:T(8,128)(2,1)}, u32[]{:S(2)}, u32[]{:S(2)}) async-start(bf16[16,80,256]{2,1,0:T(8,128)(2,1)} %shard_map.106.refs_4_), calls=%async_computation.4 | async-start | bytes 1310720 | tf_op jit(solution)/shard_map/all_to_all | solution.py:332
  138.3 2.7 %shard_map.107 = (bf16[272,256]{1,0:T(8,128)(2,1)}, bf16[272,256]{1,0:T(8,128)(2,1)}, bf16[272,256]{1,0:T(8,128)(2,1)}, bf16[272,256]{1,0:T(8,128)(2,1)}) custom-call(s32[2]{0:T(128)} %pad_add_fusion.refs_0_, s32[8,128]{1,0:T(8,128)} %bitcast.20, f32[8,128]{1,0:T(8,128)} %bitcast.24, bf16[16,96,256]{2,1,0:T(8,128)(2,1)} %all-to-all-done.2.refs_3_, ...), custom_call_target="tpu_custom_call" | custom-call | flops 4000000000 | bytes 12000000 | tf_op jit(solution)/shard_map/pallas_call | solution.py:310
  141.0 1.9 collective-permute-start.6
  143.0 4.5 %collective-permute-start.7 = (bf16[272,256]{1,0:T(8,128)(2,1)}, bf16[272,256]{1,0:T(8,128)(2,1)}, u32[]{:S(2)}, u32[]{:S(2)}) collective-permute-start(bf16[272,256]{1,0:T(8,128)(2,1)} %get-tuple-element.39), channel_id=1, source_target_pairs={{0,2},{1,3},{2,0},{3,1},{4,6},{5,7},{6,4},{7,5},{8,10},{9,11},{10,... | collective-permute-start | bytes 417800 | tf_op jit(solution)/shard_map/ppermute | solution.py:328
  147.5 2.8 %collective-permute-start.8 = (bf16[272,256]{1,0:T(8,128)(2,1)}, bf16[272,256]{1,0:T(8,128)(2,1)}, u32[]{:S(2)}, u32[]{:S(2)}) collective-permute-start(bf16[272,256]{1,0:T(8,128)(2,1)} %get-tuple-element.40), channel_id=1, source_target_pairs={{0,3},{1,2},{2,1},{3,0},{4,7},{5,6},{6,5},{7,4},{8,11},{9,10},{10,... | collective-permute-start | bytes 417800 | tf_op jit(solution)/shard_map/ppermute | solution.py:328
  150.3 5.8 %reduce-scatter.2.cloned.1.call-done.refs_1_.refs_3_ = bf16[192,2048]{1,0:T(8,128)(2,1)} async-done(((bf16[768,2048]{1,0:T(8,128)(2,1)}), bf16[192,2048]{1,0:T(8,128)(2,1)}) %reduce-scatter.2.cloned.1.call-update) | async-done | bytes 786448 | tf_op jit(solution)/shard_map/reduce_scatter | solution.py:373
  156.1 1.9 shard_map.108.refs_5_
  158.0 13.2 %collective-permute-start.10 = (bf16[96,2048]{1,0:T(8,128)(2,1)}, bf16[96,2048]{1,0:T(8,128)(2,1)}, u32[]{:S(2)}, u32[]{:S(2)}) collective-permute-start(bf16[96,2048]{1,0:T(8,128)(2,1)} %shard_map.108.refs_5_), channel_id=1, source_target_pairs={{0,128},{128,0},{256,384},{384,256},{512,640},{640,512},{768,896},... | collective-permute-start | bytes 1179656 | tf_op jit(solution)/shard_map/ppermute | solution.py:328
  171.3 0.0 collective-permute-done.6.refs_2_
  171.3 0.0 collective-permute-done.7.refs_3_
  171.3 1.9 shard_map.109.refs_4_.refs_1_
  173.2 2.9 %collective-permute-start.9 = (bf16[272,256]{1,0:T(8,128)(2,1)}, bf16[272,256]{1,0:T(8,128)(2,1)}, u32[]{:S(2)}, u32[]{:S(2)}) collective-permute-start(bf16[272,256]{1,0:T(8,128)(2,1)} %shard_map.109.refs_4_.refs_1_), channel_id=1, source_target_pairs={{0,4},{1,5},{2,6},{3,7},{4,0},{5,1},{6,2},{7,3},{8,12},{9,13},{10,... | collective-permute-start | bytes 417800 | tf_op jit(solution)/shard_map/ppermute | solution.py:328
  176.1 0.0 all-to-all-done.3.refs_3_
  176.1 2.4 %shard_map.110 = (bf16[256,256]{1,0:T(8,128)(2,1)}, bf16[256,256]{1,0:T(8,128)(2,1)}, bf16[256,256]{1,0:T(8,128)(2,1)}, bf16[256,256]{1,0:T(8,128)(2,1)}) custom-call(s32[2]{0:T(128)} %pad_add_fusion.refs_0_, s32[8,128]{1,0:T(8,128)} %bitcast.21, f32[8,128]{1,0:T(8,128)} %bitcast.25, bf16[16,80,256]{2,1,0:T(8,128)(2,1)} %all-to-all-done.3.refs_3_, ...), custom_call_target="tpu_custom_call" | custom-call | flops 4000000000 | bytes 12000000 | tf_op jit(solution)/shard_map/pallas_call | solution.py:310
  178.6 2.4 %collective-permute-start.11 = (bf16[256,256]{1,0:T(8,128)(2,1)}, bf16[256,256]{1,0:T(8,128)(2,1)}, u32[]{:S(2)}, u32[]{:S(2)}) collective-permute-start(bf16[256,256]{1,0:T(8,128)(2,1)} %get-tuple-element.43), channel_id=1, source_target_pairs={{0,1},{1,0},{2,3},{3,2},{4,5},{5,4},{6,7},{7,6},{8,9},{9,8},{10,11... | collective-permute-start | bytes 393224 | tf_op jit(solution)/shard_map/ppermute | solution.py:328
  180.9 2.6 %collective-permute-start.12 = (bf16[256,256]{1,0:T(8,128)(2,1)}, bf16[256,256]{1,0:T(8,128)(2,1)}, u32[]{:S(2)}, u32[]{:S(2)}) collective-permute-start(bf16[256,256]{1,0:T(8,128)(2,1)} %get-tuple-element.44), channel_id=1, source_target_pairs={{0,2},{1,3},{2,0},{3,1},{4,6},{5,7},{6,4},{7,5},{8,10},{9,11},{10,... | collective-permute-start | bytes 393224 | tf_op jit(solution)/shard_map/ppermute | solution.py:328
  183.6 4.3 %collective-permute-start.13 = (bf16[256,256]{1,0:T(8,128)(2,1)}, bf16[256,256]{1,0:T(8,128)(2,1)}, u32[]{:S(2)}, u32[]{:S(2)}) collective-permute-start(bf16[256,256]{1,0:T(8,128)(2,1)} %get-tuple-element.45), channel_id=1, source_target_pairs={{0,3},{1,2},{2,1},{3,0},{4,7},{5,6},{6,5},{7,4},{8,11},{9,10},{10,... | collective-permute-start | bytes 393224 | tf_op jit(solution)/shard_map/ppermute | solution.py:328
  187.9 23.2 %collective-permute-done.11.refs_6_ = bf16[256,256]{1,0:T(8,128)(2,1)} collective-permute-done((bf16[256,256]{1,0:T(8,128)(2,1)}, bf16[256,256]{1,0:T(8,128)(2,1)}, u32[]{:S(2)}, u32[]{:S(2)}) %collective-permute-start.11) | collective-permute-done | bytes 131104 | tf_op jit(solution)/shard_map/ppermute | solution.py:328
  211.0 0.7 collective-permute-done.12.refs_7_
  211.8 12.3 %collective-permute-done.13.refs_8_ = bf16[256,256]{1,0:T(8,128)(2,1)} collective-permute-done((bf16[256,256]{1,0:T(8,128)(2,1)}, bf16[256,256]{1,0:T(8,128)(2,1)}, u32[]{:S(2)}, u32[]{:S(2)}) %collective-permute-start.13) | collective-permute-done | bytes 131104 | tf_op jit(solution)/shard_map/ppermute | solution.py:328
  224.1 0.0 collective-permute-done.10.refs_4_
  224.1 2.4 %shard_map.111 = (bf16[128,256]{1,0:T(8,128)(2,1)}, bf16[128,256]{1,0:T(8,128)(2,1)}, f32[8,128]{1,0:T(8,128)}, bf16[96,2048]{1,0:T(8,128)(2,1)}) custom-call(s32[2]{0:T(128)} %pad_add_fusion.refs_0_, bf16[272,256]{1,0:T(8,128)(2,1)} %shard_map.109.refs_4_.refs_1_, bf16[272,256]{1,0:T(8,128)(2,1)} %collective-permute-done.9.refs_2_, ...), custom_call_target="tpu_custom_call" | custom-call | flops 2000000000 | bytes 6000000 | tf_op jit(solution)/shard_map/pallas_call | solution.py:310
  (12 shorter events, 0.0 us)
Async XLA Ops:
  8.9 17.3 %copy-start = (bf16[256,256]{1,0:T(8,128)(2,1)}, bf16[256,256]{1,0:T(8,128)(2,1)S(1)}, u32[]{:S(2)}) copy-start(bf16[256,256]{1,0:T(8,128)(2,1)S(1)} %constant_dynamic-update-slice_fusion.refs_3_) | copy-start | bytes 393220
  8.9 22.0 %collective-permute-start.2 = (bf16[256,256]{1,0:T(8,128)(2,1)S(1)}, bf16[256,256]{1,0:T(8,128)(2,1)S(1)}, u32[]{:S(2)}, u32[]{:S(2)}) collective-permute-start(bf16[256,256]{1,0:T(8,128)(2,1)S(1)} %constant_dynamic-update-slice_fusion.refs_3_), channel_id=1, source_target_pairs={{0,4},{1,5},{2,6},{3,7},{4,0},{5,1},{6,2},{7,3},{8,12},{9,13},{10,... | collective-permute-start | bytes 393224 | tf_op jit(solution)/shard_map/ppermute | solution.py:328
  20.3 10.5 %collective-permute-start.1 = (bf16[256,256]{1,0:T(8,128)(2,1)S(1)}, bf16[256,256]{1,0:T(8,128)(2,1)S(1)}, u32[]{:S(2)}, u32[]{:S(2)}) collective-permute-start(bf16[256,256]{1,0:T(8,128)(2,1)S(1)} %constant_dynamic-update-slice_fusion.refs_3_), channel_id=1, source_target_pairs={{0,2},{1,3},{2,0},{3,1},{4,6},{5,7},{6,4},{7,5},{8,10},{9,11},{10,... | collective-permute-start | bytes 393224 | tf_op jit(solution)/shard_map/ppermute | solution.py:328
  26.1 9.9 %collective-permute-start = (bf16[256,256]{1,0:T(8,128)(2,1)S(1)}, bf16[256,256]{1,0:T(8,128)(2,1)S(1)}, u32[]{:S(2)}, u32[]{:S(2)}) collective-permute-start(bf16[256,256]{1,0:T(8,128)(2,1)S(1)} %constant_dynamic-update-slice_fusion.refs_3_), channel_id=1, source_target_pairs={{0,1},{1,0},{2,3},{3,2},{4,5},{5,4},{6,7},{7,6},{8,9},{9,8},{10,11... | collective-permute-start | bytes 393224 | tf_op jit(solution)/shard_map/ppermute | solution.py:328
  30.8 5.3 %copy-start.1 = (bf16[256,256]{1,0:T(8,128)(2,1)}, bf16[256,256]{1,0:T(8,128)(2,1)S(1)}, u32[]{:S(2)}) copy-start(bf16[256,256]{1,0:T(8,128)(2,1)S(1)} %collective-permute-done.2.refs_6_) | copy-start | bytes 393220
  30.8 5.3 %copy-start.2 = (bf16[256,256]{1,0:T(8,128)(2,1)}, bf16[256,256]{1,0:T(8,128)(2,1)S(1)}, u32[]{:S(2)}) copy-start(bf16[256,256]{1,0:T(8,128)(2,1)S(1)} %collective-permute-done.1.refs_5_) | copy-start | bytes 393220
  36.1 0.7 copy-start.3
  39.4 31.9 %all-to-all-start.1 = ((bf16[16,80,256]{2,1,0:T(8,128)(2,1)}), bf16[16,80,256]{2,1,0:T(8,128)(2,1)}, u32[]{:S(2)}, u32[]{:S(2)}) async-start(bf16[16,80,256]{2,1,0:T(8,128)(2,1)} %get-tuple-element.28.refs_6_), calls=%async_computation.1 | async-start | bytes 1310720 | tf_op jit(solution)/shard_map/all_to_all | solution.py:332
  46.5 22.3 %collective-permute-start.3 = (bf16[512,256]{1,0:T(8,128)(2,1)}, bf16[512,256]{1,0:T(8,128)(2,1)}, u32[]{:S(2)}, u32[]{:S(2)}) collective-permute-start(bf16[512,256]{1,0:T(8,128)(2,1)} %get-tuple-element.27), channel_id=1, source_target_pairs={{0,3},{1,2},{2,1},{3,0},{4,7},{5,6},{6,5},{7,4},{8,11},{9,10},{10,... | collective-permute-start | bytes 786440 | tf_op jit(solution)/shard_map/ppermute | solution.py:328
  51.7 17.0 %collective-permute-start.5 = (bf16[256,256]{1,0:T(8,128)(2,1)}, bf16[256,256]{1,0:T(8,128)(2,1)}, u32[]{:S(2)}, u32[]{:S(2)}) collective-permute-start(bf16[256,256]{1,0:T(8,128)(2,1)} %copy-done.1), channel_id=1, source_target_pairs={{0,2},{1,3},{2,0},{3,1},{4,6},{5,7},{6,4},{7,5},{8,10},{9,11},{10,... | collective-permute-start | bytes 393224 | tf_op jit(solution)/shard_map/ppermute | solution.py:328
  53.6 15.1 %collective-permute-start.4 = (bf16[256,256]{1,0:T(8,128)(2,1)}, bf16[256,256]{1,0:T(8,128)(2,1)}, u32[]{:S(2)}, u32[]{:S(2)}) collective-permute-start(bf16[256,256]{1,0:T(8,128)(2,1)} %copy-done.1), channel_id=1, source_target_pairs={{0,1},{1,0},{2,3},{3,2},{4,5},{5,4},{6,7},{7,6},{8,9},{9,8},{10,11... | collective-permute-start | bytes 393224 | tf_op jit(solution)/shard_map/ppermute | solution.py:328
  71.3 27.7 %all-to-all-start = ((bf16[16,80,256]{2,1,0:T(8,128)(2,1)}), bf16[16,80,256]{2,1,0:T(8,128)(2,1)}, u32[]{:S(2)}, u32[]{:S(2)}) async-start(bf16[16,80,256]{2,1,0:T(8,128)(2,1)} %shard_map.103.refs_5_), calls=%async_computation | async-start | bytes 1310720 | tf_op jit(solution)/shard_map/all_to_all | solution.py:332
  78.9 77.2 %reduce-scatter.2.cloned.1.call-start = ((), (), s32[]{:S(2)}) async-start(), calls=%async_computation.5 | async-start | bytes 3932160 | tf_op jit(solution)/shard_map/reduce_scatter | solution.py:373
  108.3 25.8 %all-to-all-start.2 = ((bf16[16,96,256]{2,1,0:T(8,128)(2,1)}), bf16[16,96,256]{2,1,0:T(8,128)(2,1)}, u32[]{:S(2)}, u32[]{:S(2)}) async-start(bf16[16,96,256]{2,1,0:T(8,128)(2,1)} %get-tuple-element.33), calls=%async_computation.2 | async-start | bytes 1572864 | tf_op jit(solution)/shard_map/all_to_all | solution.py:332
  134.1 42.0 %all-to-all-start.3 = ((bf16[16,80,256]{2,1,0:T(8,128)(2,1)}), bf16[16,80,256]{2,1,0:T(8,128)(2,1)}, u32[]{:S(2)}, u32[]{:S(2)}) async-start(bf16[16,80,256]{2,1,0:T(8,128)(2,1)} %shard_map.106.refs_4_), calls=%async_computation.4 | async-start | bytes 1310720 | tf_op jit(solution)/shard_map/all_to_all | solution.py:332
  141.0 30.3 %collective-permute-start.6 = (bf16[272,256]{1,0:T(8,128)(2,1)}, bf16[272,256]{1,0:T(8,128)(2,1)}, u32[]{:S(2)}, u32[]{:S(2)}) collective-permute-start(bf16[272,256]{1,0:T(8,128)(2,1)} %get-tuple-element.38), channel_id=1, source_target_pairs={{0,1},{1,0},{2,3},{3,2},{4,5},{5,4},{6,7},{7,6},{8,9},{9,8},{10,11... | collective-permute-start | bytes 417800 | tf_op jit(solution)/shard_map/ppermute | solution.py:328
  143.0 28.4 %collective-permute-start.7 = (bf16[272,256]{1,0:T(8,128)(2,1)}, bf16[272,256]{1,0:T(8,128)(2,1)}, u32[]{:S(2)}, u32[]{:S(2)}) collective-permute-start(bf16[272,256]{1,0:T(8,128)(2,1)} %get-tuple-element.39), channel_id=1, source_target_pairs={{0,2},{1,3},{2,0},{3,1},{4,6},{5,7},{6,4},{7,5},{8,10},{9,11},{10,... | collective-permute-start | bytes 417800 | tf_op jit(solution)/shard_map/ppermute | solution.py:328
  147.5 23.8 %collective-permute-start.8 = (bf16[272,256]{1,0:T(8,128)(2,1)}, bf16[272,256]{1,0:T(8,128)(2,1)}, u32[]{:S(2)}, u32[]{:S(2)}) collective-permute-start(bf16[272,256]{1,0:T(8,128)(2,1)} %get-tuple-element.40), channel_id=1, source_target_pairs={{0,3},{1,2},{2,1},{3,0},{4,7},{5,6},{6,5},{7,4},{8,11},{9,10},{10,... | collective-permute-start | bytes 417800 | tf_op jit(solution)/shard_map/ppermute | solution.py:328
  158.0 66.1 %collective-permute-start.10 = (bf16[96,2048]{1,0:T(8,128)(2,1)}, bf16[96,2048]{1,0:T(8,128)(2,1)}, u32[]{:S(2)}, u32[]{:S(2)}) collective-permute-start(bf16[96,2048]{1,0:T(8,128)(2,1)} %shard_map.108.refs_5_), channel_id=1, source_target_pairs={{0,128},{128,0},{256,384},{384,256},{512,640},{640,512},{768,896},... | collective-permute-start | bytes 1179656 | tf_op jit(solution)/shard_map/ppermute | solution.py:328
  173.2 50.9 %collective-permute-start.9 = (bf16[272,256]{1,0:T(8,128)(2,1)}, bf16[272,256]{1,0:T(8,128)(2,1)}, u32[]{:S(2)}, u32[]{:S(2)}) collective-permute-start(bf16[272,256]{1,0:T(8,128)(2,1)} %shard_map.109.refs_4_.refs_1_), channel_id=1, source_target_pairs={{0,4},{1,5},{2,6},{3,7},{4,0},{5,1},{6,2},{7,3},{8,12},{9,13},{10,... | collective-permute-start | bytes 417800 | tf_op jit(solution)/shard_map/ppermute | solution.py:328
  178.6 32.5 %collective-permute-start.11 = (bf16[256,256]{1,0:T(8,128)(2,1)}, bf16[256,256]{1,0:T(8,128)(2,1)}, u32[]{:S(2)}, u32[]{:S(2)}) collective-permute-start(bf16[256,256]{1,0:T(8,128)(2,1)} %get-tuple-element.43), channel_id=1, source_target_pairs={{0,1},{1,0},{2,3},{3,2},{4,5},{5,4},{6,7},{7,6},{8,9},{9,8},{10,11... | collective-permute-start | bytes 393224 | tf_op jit(solution)/shard_map/ppermute | solution.py:328
  180.9 30.8 %collective-permute-start.12 = (bf16[256,256]{1,0:T(8,128)(2,1)}, bf16[256,256]{1,0:T(8,128)(2,1)}, u32[]{:S(2)}, u32[]{:S(2)}) collective-permute-start(bf16[256,256]{1,0:T(8,128)(2,1)} %get-tuple-element.44), channel_id=1, source_target_pairs={{0,2},{1,3},{2,0},{3,1},{4,6},{5,7},{6,4},{7,5},{8,10},{9,11},{10,... | collective-permute-start | bytes 393224 | tf_op jit(solution)/shard_map/ppermute | solution.py:328
  183.6 40.6 %collective-permute-start.13 = (bf16[256,256]{1,0:T(8,128)(2,1)}, bf16[256,256]{1,0:T(8,128)(2,1)}, u32[]{:S(2)}, u32[]{:S(2)}) collective-permute-start(bf16[256,256]{1,0:T(8,128)(2,1)} %get-tuple-element.45), channel_id=1, source_target_pairs={{0,3},{1,2},{2,1},{3,0},{4,7},{5,6},{6,5},{7,4},{8,11},{9,10},{10,... | collective-permute-start | bytes 393224 | tf_op jit(solution)/shard_map/ppermute | solution.py:328
Sparse Core Ops, SparseCore 0:
  108.5 47.6 reduce-scatter.1
